TPU v7x, 32 devices: a whole 2x2x4 slice. The times are simulated.
32 devices in a mesh: dp: 2 (over y), expert: 16 (over z, x, core).
Axes of the slice: x: 2, y: 2, z: 4, core: 2. Of those that a mesh axis runs over, the one named last changes fastest.
Arguments:
- tokens: bfloat16 [1024, 2048], P(('dp', 'expert')), may hold values from -6 to 6
- cotangent: bfloat16 [1024, 2048], P(('dp', 'expert')), may hold values from -0.29882812 to 0.29882812
- routes: int32 [1024, 8], P(('dp', 'expert')), may hold values from 0 to 15, all different within a row; in each aligned block of 32 rows (0 to 31, 32 to 63, ...) at most 32 rows name the same one
- combine: float32 [1024, 8], P(('dp', 'expert')), may hold values from 0.05 to 0.5
- w_in: bfloat16 [16, 2, 512, 2048], P('expert', None, 'dp'), may hold values from -0.125 to 0.125
- w_out: bfloat16 [16, 512, 2048], P('expert', 'dp'), may hold values from -0.25 to 0.25
- v_in: bfloat16 [16, 2, 512, 2048], P('expert', None, 'dp'), may hold values from -0.125 to 0.125
Outputs:
- hvp: float32 [16, 2, 512, 2048], P('expert', None, 'dp')
Inputs may be any that keep to these rules, and one draw needn't show every extreme that they name: `routes`: each token names 8 different experts. Among the tokens of one device no expert is named more than 32 times, and on some device an expert is named exactly 32 times.
All inputs are finite; a program needn't handle non-finite values.
Results may differ from a plain program's by a relative error of at most 0.015.
Values may be sent and summed in bfloat16 or wider, within the bound.
No kernel may reach another device: no remote copies, remote signals or barrier semaphores. Data moves between devices by JAX's collectives and lax.ppermute only.
A program may use at most 128 MiB of HBM per device.

v0:
```python
import functools

import jax
import jax.numpy as jnp
from jax import lax
from jax.experimental import pallas as pl
from jax.experimental.pallas import tpu as pltpu
from jax.sharding import PartitionSpec as P

NT = (((1,), (1,)), ((), ()))
NN = (((1,), (0,)), ((), ()))


def expert_terms(slot_rows, slot_grads, w_pair, v_pair, w_down):
    hidden_width = w_pair.shape[1]
    model_dim = w_pair.shape[2]
    stacked = jnp.concatenate([w_pair, v_pair], axis=0).reshape(4 * hidden_width, model_dim)
    projected = lax.dot_general(slot_rows, stacked, NT, preferred_element_type=jnp.float32)
    pre_gate = projected[:, :hidden_width]
    pre_up = projected[:, hidden_width : 2 * hidden_width]
    tan_gate = projected[:, 2 * hidden_width : 3 * hidden_width]
    tan_up = projected[:, 3 * hidden_width :]
    back_grad = lax.dot_general(slot_grads, w_down, NT, preferred_element_type=jnp.float32)
    gate_dir, up_dir = directions(pre_gate, pre_up, tan_gate, tan_up, back_grad)
    gate_term = lax.dot_general(
        gate_dir, slot_rows, (((0,), (0,)), ((), ())), preferred_element_type=jnp.float32
    )
    up_term = lax.dot_general(
        up_dir, slot_rows, (((0,), (0,)), ((), ())), preferred_element_type=jnp.float32
    )
    return jnp.stack([gate_term, up_term], axis=0)


def directions(pre_gate, pre_up, tan_gate, tan_up, back_grad):
    gate_sig = jax.nn.sigmoid(pre_gate)
    first_deriv = gate_sig * (1.0 + pre_gate * (1.0 - gate_sig))
    second_deriv = gate_sig * (1.0 - gate_sig) * (2.0 + pre_gate * (1.0 - 2.0 * gate_sig))
    gate_dir = back_grad * (tan_up * first_deriv + pre_up * second_deriv * tan_gate)
    up_dir = back_grad * first_deriv * tan_gate
    return gate_dir.astype(jnp.bfloat16), up_dir.astype(jnp.bfloat16)


def dispatched(tokens, cotangent, routes, combine, w_in, w_out, v_in):
    n_expert = lax.axis_size("expert")
    exp_dev = w_in.shape[0]
    experts = n_expert * exp_dev
    tok_dev, top_k = routes.shape
    model_dim = tokens.shape[1]
    capacity = 2 * tok_dev * top_k // experts
    pair_count = tok_dev * top_k
    slot_count = n_expert * capacity
    flat_routes = routes.reshape(pair_count)
    onehot = (flat_routes[:, None] == jnp.arange(experts, dtype=jnp.int32)[None, :]).astype(
        jnp.int32
    )
    earlier = jnp.cumsum(onehot, axis=0) - onehot
    slot_rank = jnp.sum(earlier * onehot, axis=1)
    position = flat_routes * capacity + slot_rank
    slot_table = jnp.full((experts * capacity,), pair_count, jnp.int32)
    slot_table = slot_table.at[position].set(jnp.arange(pair_count, dtype=jnp.int32))
    token_index = slot_table // top_k
    padded_tokens = jnp.concatenate([tokens, jnp.zeros((1, model_dim), jnp.bfloat16)], axis=0)
    scaled = (combine[:, :, None] * cotangent[:, None, :].astype(jnp.float32)).astype(jnp.bfloat16)
    padded_scaled = jnp.concatenate(
        [scaled.reshape(pair_count, model_dim), jnp.zeros((1, model_dim), jnp.bfloat16)], axis=0
    )
    send_rows = padded_tokens[token_index].reshape(n_expert, exp_dev * capacity, model_dim)
    send_grads = padded_scaled[slot_table].reshape(n_expert, exp_dev * capacity, model_dim)
    recv_rows = lax.all_to_all(send_rows, "expert", split_axis=0, concat_axis=0, tiled=True)
    recv_grads = lax.all_to_all(send_grads, "expert", split_axis=0, concat_axis=0, tiled=True)

    def regroup(received):
        shaped = received.reshape(n_expert, exp_dev, capacity, model_dim)
        return jnp.transpose(shaped, (1, 0, 2, 3)).reshape(exp_dev, slot_count, model_dim)

    local_rows = regroup(recv_rows)
    local_grads = regroup(recv_grads)
    batched_terms = jax.vmap(expert_terms)
    pair_piece, probe_piece, down_piece = lax.all_gather(
        (w_in, v_in, w_out[:, None]), "dp", axis=2, tiled=True
    )
    partials = batched_terms(local_rows, local_grads, pair_piece, probe_piece, down_piece[:, 0])
    return lax.psum_scatter(
        partials.astype(jnp.bfloat16), "dp", scatter_dimension=2, tiled=True
    ).astype(jnp.float32)


CORE, X, Y = 1, 2, 16
Z_NEAR, Z_FAR = 4, 8
LANES = 128


def pack_kernel(tok_ref, cot_ref, route_ref, comb_ref, out_ref, *, experts):
    tok_dev, model_dim = tok_ref.shape
    out_ref[0:tok_dev, 0:model_dim] = tok_ref[...]
    out_ref[tok_dev:, 0:model_dim] = cot_ref[...]
    line = lax.broadcasted_iota(jnp.int32, (LANES, tok_dev), 0)
    weight = jnp.zeros((LANES, tok_dev), jnp.float32)
    for k in range(route_ref.shape[0]):
        named = route_ref[k : k + 1, :] == line % experts
        weight = jnp.where(named, comb_ref[k : k + 1, :], weight)
    high = weight.astype(jnp.bfloat16).astype(jnp.float32)
    middle = (weight - high).astype(jnp.bfloat16).astype(jnp.float32)
    low = weight - high - middle
    part = line // experts
    zero = jnp.zeros_like(weight)
    value = jnp.where(part == 0, high, jnp.where(part == 1, middle, jnp.where(part == 2, low, zero)))
    row = lax.broadcasted_iota(jnp.int32, (tok_dev, tok_dev), 0)
    column = lax.broadcasted_iota(jnp.int32, (tok_dev, tok_dev), 1)
    same = (row == column).astype(jnp.float32).astype(jnp.bfloat16)
    turned = lax.dot_general(
        same, value.astype(jnp.bfloat16), NT, preferred_element_type=jnp.float32
    )
    out_ref[0:tok_dev, model_dim:] = turned.astype(jnp.bfloat16)
    out_ref[tok_dev:, model_dim:] = jnp.zeros((tok_dev, LANES), jnp.bfloat16)


def stack_kernel(flag_ref, *refs, count, layouts):
    for out_ref, parts in zip(refs[count:], layouts):
        row = 0
        for part in parts:
            at = pl.ds(row, part[0][2] if isinstance(part[0], tuple) else part[2])
            if isinstance(part[0], tuple):
                for taken, (n, first, rows) in zip((1, 0), part):

                    @pl.when(flag_ref[0] == taken)
                    def _(n=n, first=first, rows=rows, at=at, out_ref=out_ref):
                        out_ref[at, :] = refs[n][first : first + rows]

            else:
                n, first, rows = part
                out_ref[at, :] = refs[n][first : first + rows]
            row += at.size


def unpack(pieces, x_ref, c_ref, wt_ref, tok_dev):
    model_dim = x_ref.shape[1]
    row = 0
    for piece in pieces:
        for first in range(0, piece.shape[0], 2 * tok_dev):
            at = pl.ds(row, tok_dev)
            x_ref[at, :] = piece[first : first + tok_dev, 0:model_dim]
            wt_ref[at, :] = piece[first : first + tok_dev, model_dim:]
            c_ref[at, :] = piece[first + tok_dev : first + 2 * tok_dev, 0:model_dim]
            row += tok_dev


def unit_dirs(weight, w_ref, v_ref, wo_ref, x_ref, c_ref, dir_ref):
    half = wo_ref.shape[0]
    both = jnp.concatenate([w_ref[...], v_ref[...]], axis=0)
    seen = lax.dot_general(both, x_ref[...], NT, preferred_element_type=jnp.float32)
    back = lax.dot_general(wo_ref[...], c_ref[...], NT, preferred_element_type=jnp.float32)
    parts = [seen[n * half : (n + 1) * half] for n in range(4)]
    gate_dir, up_dir = directions(*parts, back * weight)
    dir_ref[0:half, :] = gate_dir
    dir_ref[half:, :] = up_dir


def rows_to_dirs(stacks, pick_ref, shards, x_ref, c_ref, wt_ref, dir_ref, tok_dev):
    unpack(stacks, x_ref, c_ref, wt_ref, tok_dev)
    weight = lax.dot_general(pick_ref[...], wt_ref[...], NT, preferred_element_type=jnp.float32)
    unit_dirs(weight[0:1], *shards, x_ref, c_ref, dir_ref)


def first_kernel(mine, theirs, pick_ref, w, v, wo, x_ref, dir_ref, c_ref, wt_ref, *, tok_dev):
    rows_to_dirs((mine, theirs), pick_ref, (w, v, wo), x_ref, c_ref, wt_ref, dir_ref, tok_dev)


COLUMNS = 512


def second_kernel(
    mine, theirs, pick_ref, w, v, wo, early_x, early_dir, sum_ref, x_ref, dir_ref, c_ref, wt_ref,
    *, tok_dev
):
    rows_to_dirs((mine, theirs), pick_ref, (w, v, wo), x_ref, c_ref, wt_ref, dir_ref, tok_dev)
    dirs = jnp.concatenate([early_dir[...], dir_ref[...]], axis=1)
    for n in range(sum_ref.shape[1] // COLUMNS):
        at = pl.ds(n * COLUMNS, COLUMNS)
        rows = jnp.concatenate([early_x[:, at], x_ref[:, at]], axis=0)
        sum_ref[:, at] = lax.dot_general(dirs, rows, NN, preferred_element_type=jnp.float32)


def last_kernel(
    mine, theirs, pick_ref, w, v, wo, add_ref, out_ref, x_ref, dir_ref, c_ref, wt_ref, sum_ref, sems,
    *, tok_dev
):
    rows_to_dirs((mine, theirs), pick_ref, (w, v, wo), x_ref, c_ref, wt_ref, dir_ref, tok_dev)
    copies = []
    for n in range(out_ref.shape[1] // COLUMNS):
        at = pl.ds(n * COLUMNS, COLUMNS)
        total = lax.dot_general(
            dir_ref[...], x_ref[:, at], NN, preferred_element_type=jnp.float32
        )
        sum_ref[:, at] = total + add_ref[:, at]
        copy = pltpu.make_async_copy(sum_ref.at[:, at], out_ref.at[:, at], sems.at[n])
        copy.start()
        copies.append(copy)
    for copy in copies:
        copy.wait()


def swap(value, mask, sender=None):
    axes = ("dp", "expert")
    count = lax.axis_size("dp") * lax.axis_size("expert")
    pairs = [(i, i ^ mask) for i in range(count) if sender is None or sender(i)]
    return lax.ppermute(value, axes, pairs)


def inner(place):
    return (place & Z_NEAR) // Z_NEAR != (place & Z_FAR) // Z_FAR


def after(value, *others):
    return lax.optimization_barrier((value, *others))[0]


def tied(values, *others):
    return list(lax.optimization_barrier((*values, *others)))[: len(values)]


def dense(tokens, cotangent, routes, combine, w_in, w_out, v_in):
    experts = lax.axis_size("expert")
    tok_dev, model_dim = tokens.shape
    half = w_in.shape[2]
    wide = model_dim + LANES
    inside = pl.BlockSpec(memory_space=pltpu.VMEM)
    own = pl.pallas_call(
        functools.partial(pack_kernel, experts=experts),
        in_specs=[inside] * 4,
        out_specs=inside,
        out_shape=jax.ShapeDtypeStruct((2 * tok_dev, wide), jnp.bfloat16),
        compiler_params=pltpu.CompilerParams(vmem_limit_bytes=2 * 2**20),
    )(tokens, cotangent, routes.T, combine.T)

    lane = jnp.arange(LANES, dtype=jnp.int32)[None, :]
    expert = lax.axis_index("expert")
    pick = ((lane % experts == expert) & (lane < 3 * experts)).astype(jnp.bfloat16)
    pick = jnp.broadcast_to(pick, (16, LANES))
    is_inner = inner(expert)
    shards = (
        w_in.reshape(2 * half, model_dim),
        v_in.reshape(2 * half, model_dim),
        w_out.reshape(half, model_dim),
    )

    def call(kernel, stack, theirs, more, outs, scratch, limit):
        rows = stack.shape[0]
        operands = (stack, theirs, pick, *shards, *more)
        held = [
            ((rows, model_dim), jnp.bfloat16),
            ((2 * half, rows), jnp.bfloat16),
            ((rows, model_dim), jnp.bfloat16),
            ((rows, LANES), jnp.bfloat16),
        ]
        if outs is None:
            outs, held = held[:2], held[2:]
            out_specs = [inside] * 2
        else:
            out_specs = [inside if outs[1] else pl.BlockSpec(memory_space=pl.ANY)]
            outs = [((2 * half, model_dim), jnp.float32)]
        return pl.pallas_call(
            functools.partial(kernel, tok_dev=tok_dev),
            in_specs=[inside] * len(operands),
            out_specs=out_specs,
            out_shape=[jax.ShapeDtypeStruct(*o) for o in outs],
            scratch_shapes=[pltpu.VMEM(*h) for h in held] + scratch,
            compiler_params=pltpu.CompilerParams(vmem_limit_bytes=limit * 2**20),
            cost_estimate=pl.CostEstimate(
                flops=2 * rows * model_dim * 7 * half,
                bytes_accessed=12 * 2**20,
                transcendentals=rows * half,
            ),
        )(*operands)

    flag = is_inner.astype(jnp.int32)[None]
    block = 2 * tok_dev

    def stack(inputs, *layouts):
        def size(part):
            return part[0][2] if isinstance(part[0], tuple) else part[2]

        return pl.pallas_call(
            functools.partial(stack_kernel, count=len(inputs), layouts=layouts),
            in_specs=[pl.BlockSpec(memory_space=pltpu.SMEM)] + [inside] * len(inputs),
            out_specs=[inside] * len(layouts),
            out_shape=[
                jax.ShapeDtypeStruct((sum(map(size, parts)), wide), jnp.bfloat16)
                for parts in layouts
            ],
            compiler_params=pltpu.CompilerParams(vmem_limit_bytes=2 * 2**20),
        )(flag, *inputs)

    def rows_of(n, first=0, count=1):
        return (n, first * block, count * block)

    order = (Z_NEAR ^ Z_FAR, X ^ Y, X, Y, Z_NEAR)
    first = tied([swap(own, m) for m in order])
    middle, across, beside_x, beside_y, near = first

    through, outward, pair = stack(
        [near, middle, across],
        [rows_of(0), rows_of(2)],
        [rows_of(1), rows_of(2)],
        [rows_of(0), rows_of(1)],
    )
    through = swap(through, Z_NEAR ^ Z_FAR, inner)
    outward = swap(outward, Z_NEAR)
    pair_x, pair_y = swap(pair, X), swap(pair, Y)
    (stack_a,) = stack([own, beside_x, beside_y, across], [rows_of(n) for n in range(4)])
    early = call(first_kernel, stack_a, swap(stack_a, CORE), (), None, [], 6)
    outward, through, pair_x, pair_y, *early = tied([outward, through, pair_x, pair_y, *early])

    far, beyond, relayed = stack(
        [through, outward, middle],
        [(rows_of(0), rows_of(1))],
        [(rows_of(0), rows_of(2))],
        [rows_of(0, 1)],
    )
    third = [swap(beyond, X ^ Y), swap(far, X), swap(far, Y), swap(relayed, Z_NEAR, inner)]
    (stack_b,) = stack(
        [pair, pair_x, pair_y, outward, far],
        [rows_of(0, 0, 2), rows_of(1, 0, 2), rows_of(2, 0, 2), rows_of(3, 1), rows_of(4)],
    )
    (total,) = call(second_kernel, stack_b, swap(stack_b, CORE), early, (0, True), [], 11)
    *third, total = tied([*third, total])

    (stack_c,) = stack(
        [*third, through],
        [rows_of(0), rows_of(1), rows_of(2), (rows_of(4, 1), rows_of(3))],
    )
    scratch = [
        pltpu.VMEM((2 * half, model_dim), jnp.float32),
        pltpu.SemaphoreType.DMA((model_dim // COLUMNS,)),
    ]
    (out,) = call(last_kernel, stack_c, swap(stack_c, CORE), (total,), (0, False), scratch, 11)
    return out.reshape(1, 2, half, model_dim)


def local(tokens, cotangent, routes, combine, w_in, w_out, v_in):
    experts = lax.axis_size("expert") * w_in.shape[0]
    tok_dev, top_k = routes.shape
    sizes = (lax.axis_size("dp"), lax.axis_size("expert"))
    if sizes == (2, 16) and w_in.shape[0] == 1 and 2 * tok_dev * top_k // experts >= tok_dev:
        return dense(tokens, cotangent, routes, combine, w_in, w_out, v_in)
    return dispatched(tokens, cotangent, routes, combine, w_in, w_out, v_in)


def solution(mesh):
    in_specs = (
        P(("dp", "expert"), None),
        P(("dp", "expert"), None),
        P(("dp", "expert"), None),
        P(("dp", "expert"), None),
        P("expert", None, "dp", None),
        P("expert", "dp", None),
        P("expert", None, "dp", None),
    )
    out_specs = P("expert", None, "dp", None)
    return jax.shard_map(local, mesh=mesh, in_specs=in_specs, out_specs=out_specs, check_vma=False)
```

profile of v0, /device:TPU:0, one launch (start us, length us, event | category | flops | bytes accessed | tf_op | source)
XLA Modules:
  0.0 68.0 jit_solution(203614520372115437)
XLA Ops:
  0.0 0.0 copy-start
  0.0 0.0 copy-start.3
  0.0 0.0 copy-start.4
  0.0 1.1 %copy-done.4 = bf16[32,2048]{1,0:T(8,128)(2,1)S(1)} copy-done((bf16[32,2048]{1,0:T(8,128)(2,1)S(1)}, bf16[32,2048]{1,0:T(8,128)(2,1)}, u32[]{:S(2)}) %copy-start.4) | copy-done | bytes 131096
  1.1 0.0 copy-start.5
  1.1 0.9 %copy-done.5 = bf16[32,2048]{1,0:T(8,128)(2,1)S(1)} copy-done((bf16[32,2048]{1,0:T(8,128)(2,1)S(1)}, bf16[32,2048]{1,0:T(8,128)(2,1)}, u32[]{:S(2)}) %copy-start.5) | copy-done | bytes 131096
  2.0 0.0 copy-start.6
  2.0 0.7 %copy-done.6 = s32[32,8]{0,1:T(8,128)S(1)} copy-done((s32[32,8]{0,1:T(8,128)S(1)}, s32[32,8]{0,1:T(8,128)}, u32[]{:S(2)}) %copy-start.6) | copy-done | bytes 1048
  2.7 0.0 copy-start.7
  2.7 0.7 %copy-done.7 = f32[32,8]{0,1:T(8,128)S(1)} copy-done((f32[32,8]{0,1:T(8,128)S(1)}, f32[32,8]{0,1:T(8,128)}, u32[]{:S(2)}) %copy-start.7) | copy-done | bytes 1048
  3.3 0.9 %shard_map.73.refs_0_ = bf16[64,2176]{1,0:T(8,128)(2,1)} custom-call(bf16[32,2048]{1,0:T(8,128)(2,1)S(1)} %copy-done.4, bf16[32,2048]{1,0:T(8,128)(2,1)S(1)} %copy-done.5, s32[8,32]{1,0:T(8,128)S(1)} %bitcast.16, f32[8,32]{1,0:T(8,128)S(1)} %bitcast.17), custom_call_target="tpu_custom_call" | custom-call | tf_op jit(solution)/shard_map/pallas_call | solution.py:228
  4.2 5.0 %collective-permute-start = (bf16[64,2176]{1,0:T(8,128)(2,1)}, bf16[64,2176]{1,0:T(8,128)(2,1)S(1)}, u32[]{:S(2)}, u32[]{:S(2)}) collective-permute-start(bf16[64,2176]{1,0:T(8,128)(2,1)} %shard_map.73.refs_0_), channel_id=1, source_target_pairs={{0,12},{1,13},{2,14},{3,15},{4,8},{5,9},{6,10},{7,11},{8,4},{9,5},... | collective-permute-start | bytes 835592 | tf_op jit(solution)/shard_map/ppermute | solution.py:207
  9.2 2.4 %collective-permute-start.1 = (bf16[64,2176]{1,0:T(8,128)(2,1)}, bf16[64,2176]{1,0:T(8,128)(2,1)}, u32[]{:S(2)}, u32[]{:S(2)}) collective-permute-start(bf16[64,2176]{1,0:T(8,128)(2,1)} %shard_map.73.refs_0_), channel_id=1, source_target_pairs={{0,18},{1,19},{2,16},{3,17},{4,22},{5,23},{6,20},{7,21},{8,26},{9,... | collective-permute-start | bytes 835592 | tf_op jit(solution)/shard_map/ppermute | solution.py:207
  11.7 0.5 collective-permute-start.2
  12.2 0.5 collective-permute-start.3
  12.7 0.0 collective-permute-start.4
  12.7 4.2 %collective-permute-done.refs_1_.refs_2_ = bf16[64,2176]{1,0:T(8,128)(2,1)S(1)} collective-permute-done((bf16[64,2176]{1,0:T(8,128)(2,1)}, bf16[64,2176]{1,0:T(8,128)(2,1)S(1)}, u32[]{:S(2)}, u32[]{:S(2)}) %collective-permute-start) | collective-permute-done | bytes 278560 | tf_op jit(solution)/shard_map/ppermute | solution.py:207
  17.0 3.1 %collective-permute-done.1.refs_2_.refs_3_ = bf16[64,2176]{1,0:T(8,128)(2,1)} collective-permute-done((bf16[64,2176]{1,0:T(8,128)(2,1)}, bf16[64,2176]{1,0:T(8,128)(2,1)}, u32[]{:S(2)}, u32[]{:S(2)}) %collective-permute-start.1) | collective-permute-done | bytes 278560 | tf_op jit(solution)/shard_map/ppermute | solution.py:207
  20.1 4.6 %collective-permute-done.2.refs_1_ = bf16[64,2176]{1,0:T(8,128)(2,1)} collective-permute-done((bf16[64,2176]{1,0:T(8,128)(2,1)}, bf16[64,2176]{1,0:T(8,128)(2,1)}, u32[]{:S(2)}, u32[]{:S(2)}) %collective-permute-start.2) | collective-permute-done | bytes 278560 | tf_op jit(solution)/shard_map/ppermute | solution.py:207
  24.6 0.0 collective-permute-done.3.refs_2_
  24.7 0.0 collective-permute-done.4.refs_0_
  24.7 1.3 %shard_map.75.mine = bf16[256,2176]{1,0:T(8,128)(2,1)S(1)} custom-call(s32[1]{0:T(128)} %bitcast.flag_ref, bf16[64,2176]{1,0:T(8,128)(2,1)} %shard_map.73.refs_0_, bf16[64,2176]{1,0:T(8,128)(2,1)} %collective-permute-done.2.refs_1_, bf16[64,2176]{1,0:T(8,128)(2,1)} %collective-permute-done.3.refs_2_, bf16[64,2176]{1,0:T(8,128)(2,1)} %collective-permute-done.1.refs_2_.refs_3_), custom_call_target="tpu_custom_call" | custom-call | tf_op jit(solution)/shard_map/pallas_call | solution.py:283
  25.9 0.1 collective-permute-start.9
  26.0 1.2 %shard_map.74 = (bf16[128,2176]{1,0:T(8,128)(2,1)S(1)}, bf16[128,2176]{1,0:T(8,128)(2,1)S(1)}, bf16[128,2176]{1,0:T(8,128)(2,1)S(1)}) custom-call(s32[1]{0:T(128)} %bitcast.flag_ref, bf16[64,2176]{1,0:T(8,128)(2,1)} %collective-permute-done.4.refs_0_, bf16[64,2176]{1,0:T(8,128)(2,1)S(1)} %collective-permute-done.refs_1_.refs_2_, ...), custom_call_target="tpu_custom_call" | custom-call | tf_op jit(solution)/shard_map/pallas_call | solution.py:283
  27.2 0.1 collective-permute-start.5
  27.3 0.7 %collective-permute-start.6 = (bf16[128,2176]{1,0:T(8,128)(2,1)S(1)}, bf16[128,2176]{1,0:T(8,128)(2,1)S(1)}, u32[]{:S(2)}, u32[]{:S(2)}) collective-permute-start(bf16[128,2176]{1,0:T(8,128)(2,1)S(1)} %get-tuple-element.33), channel_id=1, source_target_pairs={{4,8},{5,9},{6,10},{7,11},{8,4},{9,5},{10,6},{11,7},{20,24},{21,25... | collective-permute-start | bytes 1671176 | tf_op jit(solution)/shard_map/ppermute | solution.py:207
  28.0 1.6 %collective-permute-start.7 = (bf16[128,2176]{1,0:T(8,128)(2,1)S(1)}, bf16[128,2176]{1,0:T(8,128)(2,1)S(1)}, u32[]{:S(2)}, u32[]{:S(2)}) collective-permute-start(bf16[128,2176]{1,0:T(8,128)(2,1)S(1)} %get-tuple-element.34.refs_0_), channel_id=1, source_target_pairs={{0,2},{1,3},{2,0},{3,1},{4,6},{5,7},{6,4},{7,5},{8,10},{9,11},{10,... | collective-permute-start | bytes 1671176 | tf_op jit(solution)/shard_map/ppermute | solution.py:207
  29.5 1.4 %collective-permute-start.8 = (bf16[128,2176]{1,0:T(8,128)(2,1)S(1)}, bf16[128,2176]{1,0:T(8,128)(2,1)S(1)}, u32[]{:S(2)}, u32[]{:S(2)}) collective-permute-start(bf16[128,2176]{1,0:T(8,128)(2,1)S(1)} %get-tuple-element.34.refs_0_), channel_id=1, source_target_pairs={{0,16},{1,17},{2,18},{3,19},{4,20},{5,21},{6,22},{7,23},{8,24},{9,... | collective-permute-start | bytes 1671176 | tf_op jit(solution)/shard_map/ppermute | solution.py:207
  30.9 0.0 collective-permute-done.9.theirs
  31.0 0.0 copy-done
  31.0 0.0 copy-done.3
  31.0 0.0 copy-start.1
  31.0 1.6 %copy-done.1 = bf16[1,2,256,2048]{3,2,1,0:T(8,128)(2,1)S(1)} copy-done((bf16[1,2,256,2048]{3,2,1,0:T(8,128)(2,1)S(1)}, bf16[1,2,256,2048]{3,2,1,0:T(8,128)(2,1)}, u32[]{:S(2)}) %copy-start.1) | copy-done | bytes 2097176
  32.6 1.7 %shard_map.76 = (bf16[256,2048]{1,0:T(8,128)(2,1)S(1)}, bf16[512,256]{1,0:T(8,128)(2,1)S(1)}) custom-call(bf16[256,2176]{1,0:T(8,128)(2,1)S(1)} %shard_map.75.mine, bf16[256,2176]{1,0:T(8,128)(2,1)S(1)} %collective-permute-done.9.theirs, bf16[16,128]{1,0:T(8,128)(2,1)S(1)} %broadcast_in_dim.13.pick_ref, bf16[512,2048]{1,0:T(8,128)(2,1)S(1)} %bitcast.7, ...), custom_call_target="tpu_custom_call" | custom-call | flops 1879048192 | bytes 12582912 | tf_op jit(solution)/shard_map/pallas_call | solution.py:262
  34.3 8.0 %collective-permute-done.5.refs_1_.refs_3_ = bf16[128,2176]{1,0:T(8,128)(2,1)S(1)} collective-permute-done((bf16[128,2176]{1,0:T(8,128)(2,1)S(1)}, bf16[128,2176]{1,0:T(8,128)(2,1)S(1)}, u32[]{:S(2)}, u32[]{:S(2)}) %collective-permute-start.5) | collective-permute-done | bytes 557088 | tf_op jit(solution)/shard_map/ppermute | solution.py:207
  42.3 0.0 collective-permute-done.6.refs_0_.refs_4_
  42.3 0.8 %collective-permute-done.7.refs_1_ = bf16[128,2176]{1,0:T(8,128)(2,1)S(1)} collective-permute-done((bf16[128,2176]{1,0:T(8,128)(2,1)S(1)}, bf16[128,2176]{1,0:T(8,128)(2,1)S(1)}, u32[]{:S(2)}, u32[]{:S(2)}) %collective-permute-start.7) | collective-permute-done | bytes 557088 | tf_op jit(solution)/shard_map/ppermute | solution.py:207
  43.1 1.2 %collective-permute-done.8.refs_2_ = bf16[128,2176]{1,0:T(8,128)(2,1)S(1)} collective-permute-done((bf16[128,2176]{1,0:T(8,128)(2,1)S(1)}, bf16[128,2176]{1,0:T(8,128)(2,1)S(1)}, u32[]{:S(2)}, u32[]{:S(2)}) %collective-permute-start.8) | collective-permute-done | bytes 557088 | tf_op jit(solution)/shard_map/ppermute | solution.py:207
  44.3 0.1 shard_map.77
  44.3 0.0 copy-start.2
  44.4 0.2 shard_map.78.mine
  44.5 0.1 collective-permute-start.14
  44.6 0.6 collective-permute-start.11
  45.2 1.4 %collective-permute-start.12 = (bf16[64,2176]{1,0:T(8,128)(2,1)S(1)}, bf16[64,2176]{1,0:T(8,128)(2,1)S(1)}, u32[]{:S(2)}, u32[]{:S(2)}) collective-permute-start(bf16[64,2176]{1,0:T(8,128)(2,1)S(1)} %get-tuple-element.42.refs_4_), channel_id=1, source_target_pairs={{0,16},{1,17},{2,18},{3,19},{4,20},{5,21},{6,22},{7,23},{8,24},{9,... | collective-permute-start | bytes 835592 | tf_op jit(solution)/shard_map/ppermute | solution.py:207
  46.6 1.5 %collective-permute-start.10 = (bf16[64,2176]{1,0:T(8,128)(2,1)S(1)}, bf16[64,2176]{1,0:T(8,128)(2,1)S(1)}, u32[]{:S(2)}, u32[]{:S(2)}) collective-permute-start(bf16[64,2176]{1,0:T(8,128)(2,1)S(1)} %get-tuple-element.41), channel_id=1, source_target_pairs={{0,18},{1,19},{2,16},{3,17},{4,22},{5,23},{6,20},{7,21},{8,26},{9,... | collective-permute-start | bytes 835592 | tf_op jit(solution)/shard_map/ppermute | solution.py:207
  48.2 1.3 %collective-permute-start.13 = (bf16[64,2176]{1,0:T(8,128)(2,1)S(1)}, bf16[64,2176]{1,0:T(8,128)(2,1)S(1)}, u32[]{:S(2)}, u32[]{:S(2)}) collective-permute-start(bf16[64,2176]{1,0:T(8,128)(2,1)S(1)} %get-tuple-element.43), channel_id=1, source_target_pairs={{4,0},{5,1},{6,2},{7,3},{8,12},{9,13},{10,14},{11,15},{20,16},{21,... | collective-permute-start | bytes 835592 | tf_op jit(solution)/shard_map/ppermute | solution.py:207
  49.4 0.0 collective-permute-done.14.theirs
  49.5 0.0 copy-done.2
  49.5 4.8 %shard_map.79.add_ref = f32[512,2048]{1,0:T(8,128)S(1)} custom-call(bf16[512,2176]{1,0:T(8,128)(2,1)S(1)} %shard_map.78.mine, bf16[512,2176]{1,0:T(8,128)(2,1)S(1)} %collective-permute-done.14.theirs, bf16[16,128]{1,0:T(8,128)(2,1)S(1)} %broadcast_in_dim.13.pick_ref, bf16[512,2048]{1,0:T(8,128)(2,1)S(1)} %bitcast.8, bf16[512,2048]{1,0:T(8,128)(2,1)S(1)} %bitcast.11, ...), custom_call_target="tpu_custom_call" | custom-call | flops 3758096384 | bytes 12582912 | tf_op jit(solution)/shard_map/pallas_call | solution.py:262
  54.3 6.2 %collective-permute-done.10.refs_0_ = bf16[64,2176]{1,0:T(8,128)(2,1)S(1)} collective-permute-done((bf16[64,2176]{1,0:T(8,128)(2,1)S(1)}, bf16[64,2176]{1,0:T(8,128)(2,1)S(1)}, u32[]{:S(2)}, u32[]{:S(2)}) %collective-permute-start.10) | collective-permute-done | bytes 278560 | tf_op jit(solution)/shard_map/ppermute | solution.py:207
  60.5 0.0 collective-permute-done.11.refs_1_
  60.5 0.0 collective-permute-done.12.refs_2_
  60.5 0.0 collective-permute-done.13.refs_3_
  60.5 0.1 shard_map.80.mine
  60.6 0.1 collective-permute-start.15
  60.7 2.7 %collective-permute-done.15.theirs = bf16[256,2176]{1,0:T(8,128)(2,1)S(1)} collective-permute-done((bf16[256,2176]{1,0:T(8,128)(2,1)S(1)}, bf16[256,2176]{1,0:T(8,128)(2,1)S(1)}, u32[]{:S(2)}, u32[]{:S(2)}) %collective-permute-start.15) | collective-permute-done | bytes 1114144 | tf_op jit(solution)/shard_map/ppermute | solution.py:207
  63.4 4.5 %shard_map.81 = f32[512,2048]{1,0:T(8,128)} custom-call(bf16[256,2176]{1,0:T(8,128)(2,1)S(1)} %shard_map.80.mine, bf16[256,2176]{1,0:T(8,128)(2,1)S(1)} %collective-permute-done.15.theirs, bf16[16,128]{1,0:T(8,128)(2,1)S(1)} %broadcast_in_dim.13.pick_ref, bf16[512,2048]{1,0:T(8,128)(2,1)S(1)} %bitcast.9, bf16[512,2048]{1,0:T(8,128)(2,1)S(1)} %bitcast.12, ...), custom_call_target="tpu_custom_call" | custom-call | flops 1879048192 | bytes 12582912 | tf_op jit(solution)/shard_map/pallas_call | solution.py:262
  (2 shorter events, 0.0 us)
Async XLA Ops:
  0.0 31.0 %copy-start = (bf16[1,2,256,2048]{3,2,1,0:T(8,128)(2,1)S(1)}, bf16[1,2,256,2048]{3,2,1,0:T(8,128)(2,1)}, u32[]{:S(2)}) copy-start(bf16[1,2,256,2048]{3,2,1,0:T(8,128)(2,1)} %param.11) | copy-start | bytes 6291460
  0.0 31.0 %copy-start.3 = (bf16[1,256,2048]{2,1,0:T(8,128)(2,1)S(1)}, bf16[1,256,2048]{2,1,0:T(8,128)(2,1)}, u32[]{:S(2)}) copy-start(bf16[1,256,2048]{2,1,0:T(8,128)(2,1)} %param.12) | copy-start | bytes 3145732
  0.0 1.1 %copy-start.4 = (bf16[32,2048]{1,0:T(8,128)(2,1)S(1)}, bf16[32,2048]{1,0:T(8,128)(2,1)}, u32[]{:S(2)}) copy-start(bf16[32,2048]{1,0:T(8,128)(2,1)} %tok_ref.1) | copy-start | bytes 393220
  1.1 0.9 %copy-start.5 = (bf16[32,2048]{1,0:T(8,128)(2,1)S(1)}, bf16[32,2048]{1,0:T(8,128)(2,1)}, u32[]{:S(2)}) copy-start(bf16[32,2048]{1,0:T(8,128)(2,1)} %cot_ref.1) | copy-start | bytes 393220
  2.0 0.7 %copy-start.6 = (s32[32,8]{0,1:T(8,128)S(1)}, s32[32,8]{0,1:T(8,128)}, u32[]{:S(2)}) copy-start(s32[32,8]{0,1:T(8,128)} %param.9) | copy-start | bytes 3076
  2.7 0.7 %copy-start.7 = (f32[32,8]{0,1:T(8,128)S(1)}, f32[32,8]{0,1:T(8,128)}, u32[]{:S(2)}) copy-start(f32[32,8]{0,1:T(8,128)} %param.10) | copy-start | bytes 3076
  4.2 12.8 %collective-permute-start = (bf16[64,2176]{1,0:T(8,128)(2,1)}, bf16[64,2176]{1,0:T(8,128)(2,1)S(1)}, u32[]{:S(2)}, u32[]{:S(2)}) collective-permute-start(bf16[64,2176]{1,0:T(8,128)(2,1)} %shard_map.73.refs_0_), channel_id=1, source_target_pairs={{0,12},{1,13},{2,14},{3,15},{4,8},{5,9},{6,10},{7,11},{8,4},{9,5},... | collective-permute-start | bytes 835592 | tf_op jit(solution)/shard_map/ppermute | solution.py:207
  9.2 10.8 %collective-permute-start.1 = (bf16[64,2176]{1,0:T(8,128)(2,1)}, bf16[64,2176]{1,0:T(8,128)(2,1)}, u32[]{:S(2)}, u32[]{:S(2)}) collective-permute-start(bf16[64,2176]{1,0:T(8,128)(2,1)} %shard_map.73.refs_0_), channel_id=1, source_target_pairs={{0,18},{1,19},{2,16},{3,17},{4,22},{5,23},{6,20},{7,21},{8,26},{9,... | collective-permute-start | bytes 835592 | tf_op jit(solution)/shard_map/ppermute | solution.py:207
  11.7 13.0 %collective-permute-start.2 = (bf16[64,2176]{1,0:T(8,128)(2,1)}, bf16[64,2176]{1,0:T(8,128)(2,1)}, u32[]{:S(2)}, u32[]{:S(2)}) collective-permute-start(bf16[64,2176]{1,0:T(8,128)(2,1)} %shard_map.73.refs_0_), channel_id=1, source_target_pairs={{0,2},{1,3},{2,0},{3,1},{4,6},{5,7},{6,4},{7,5},{8,10},{9,11},{10,... | collective-permute-start | bytes 835592 | tf_op jit(solution)/shard_map/ppermute | solution.py:207
  12.2 12.4 %collective-permute-start.3 = (bf16[64,2176]{1,0:T(8,128)(2,1)}, bf16[64,2176]{1,0:T(8,128)(2,1)}, u32[]{:S(2)}, u32[]{:S(2)}) collective-permute-start(bf16[64,2176]{1,0:T(8,128)(2,1)} %shard_map.73.refs_0_), channel_id=1, source_target_pairs={{0,16},{1,17},{2,18},{3,19},{4,20},{5,21},{6,22},{7,23},{8,24},{9,... | collective-permute-start | bytes 835592 | tf_op jit(solution)/shard_map/ppermute | solution.py:207
  12.7 11.9 %collective-permute-start.4 = (bf16[64,2176]{1,0:T(8,128)(2,1)}, bf16[64,2176]{1,0:T(8,128)(2,1)}, u32[]{:S(2)}, u32[]{:S(2)}) collective-permute-start(bf16[64,2176]{1,0:T(8,128)(2,1)} %shard_map.73.refs_0_), channel_id=1, source_target_pairs={{0,4},{1,5},{2,6},{3,7},{4,0},{5,1},{6,2},{7,3},{8,12},{9,13},{10,... | collective-permute-start | bytes 835592 | tf_op jit(solution)/shard_map/ppermute | solution.py:207
  25.9 5.0 %collective-permute-start.9 = (bf16[256,2176]{1,0:T(8,128)(2,1)S(1)}, bf16[256,2176]{1,0:T(8,128)(2,1)S(1)}, u32[]{:S(2)}, u32[]{:S(2)}) collective-permute-start(bf16[256,2176]{1,0:T(8,128)(2,1)S(1)} %shard_map.75.mine), channel_id=1, source_target_pairs={{0,1},{1,0},{2,3},{3,2},{4,5},{5,4},{6,7},{7,6},{8,9},{9,8},{10,11... | collective-permute-start | bytes 3342344 | tf_op jit(solution)/shard_map/ppermute | solution.py:207
  27.2 15.1 %collective-permute-start.5 = (bf16[128,2176]{1,0:T(8,128)(2,1)S(1)}, bf16[128,2176]{1,0:T(8,128)(2,1)S(1)}, u32[]{:S(2)}, u32[]{:S(2)}) collective-permute-start(bf16[128,2176]{1,0:T(8,128)(2,1)S(1)} %get-tuple-element.32), channel_id=1, source_target_pairs={{0,4},{1,5},{2,6},{3,7},{4,0},{5,1},{6,2},{7,3},{8,12},{9,13},{10,... | collective-permute-start | bytes 1671176 | tf_op jit(solution)/shard_map/ppermute | solution.py:207
  27.3 15.0 %collective-permute-start.6 = (bf16[128,2176]{1,0:T(8,128)(2,1)S(1)}, bf16[128,2176]{1,0:T(8,128)(2,1)S(1)}, u32[]{:S(2)}, u32[]{:S(2)}) collective-permute-start(bf16[128,2176]{1,0:T(8,128)(2,1)S(1)} %get-tuple-element.33), channel_id=1, source_target_pairs={{4,8},{5,9},{6,10},{7,11},{8,4},{9,5},{10,6},{11,7},{20,24},{21,25... | collective-permute-start | bytes 1671176 | tf_op jit(solution)/shard_map/ppermute | solution.py:207
  28.0 15.1 %collective-permute-start.7 = (bf16[128,2176]{1,0:T(8,128)(2,1)S(1)}, bf16[128,2176]{1,0:T(8,128)(2,1)S(1)}, u32[]{:S(2)}, u32[]{:S(2)}) collective-permute-start(bf16[128,2176]{1,0:T(8,128)(2,1)S(1)} %get-tuple-element.34.refs_0_), channel_id=1, source_target_pairs={{0,2},{1,3},{2,0},{3,1},{4,6},{5,7},{6,4},{7,5},{8,10},{9,11},{10,... | collective-permute-start | bytes 1671176 | tf_op jit(solution)/shard_map/ppermute | solution.py:207
  29.5 14.7 %collective-permute-start.8 = (bf16[128,2176]{1,0:T(8,128)(2,1)S(1)}, bf16[128,2176]{1,0:T(8,128)(2,1)S(1)}, u32[]{:S(2)}, u32[]{:S(2)}) collective-permute-start(bf16[128,2176]{1,0:T(8,128)(2,1)S(1)} %get-tuple-element.34.refs_0_), channel_id=1, source_target_pairs={{0,16},{1,17},{2,18},{3,19},{4,20},{5,21},{6,22},{7,23},{8,24},{9,... | collective-permute-start | bytes 1671176 | tf_op jit(solution)/shard_map/ppermute | solution.py:207
  31.0 1.6 %copy-start.1 = (bf16[1,2,256,2048]{3,2,1,0:T(8,128)(2,1)S(1)}, bf16[1,2,256,2048]{3,2,1,0:T(8,128)(2,1)}, u32[]{:S(2)}) copy-start(bf16[1,2,256,2048]{3,2,1,0:T(8,128)(2,1)} %param.13) | copy-start | bytes 6291460
  44.3 5.1 %copy-start.2 = (bf16[1,2,256,2048]{3,2,1,0:T(8,128)(2,1)S(1)}, bf16[1,2,256,2048]{3,2,1,0:T(8,128)(2,1)}, u32[]{:S(2)}) copy-start(bf16[1,2,256,2048]{3,2,1,0:T(8,128)(2,1)} %param.13) | copy-start | bytes 6291460
  44.5 4.9 %collective-permute-start.14 = (bf16[512,2176]{1,0:T(8,128)(2,1)S(1)}, bf16[512,2176]{1,0:T(8,128)(2,1)S(1)}, u32[]{:S(2)}, u32[]{:S(2)}) collective-permute-start(bf16[512,2176]{1,0:T(8,128)(2,1)S(1)} %shard_map.78.mine), channel_id=1, source_target_pairs={{0,1},{1,0},{2,3},{3,2},{4,5},{5,4},{6,7},{7,6},{8,9},{9,8},{10,11... | collective-permute-start | bytes 6684680 | tf_op jit(solution)/shard_map/ppermute | solution.py:207
  44.6 15.9 %collective-permute-start.11 = (bf16[64,2176]{1,0:T(8,128)(2,1)S(1)}, bf16[64,2176]{1,0:T(8,128)(2,1)S(1)}, u32[]{:S(2)}, u32[]{:S(2)}) collective-permute-start(bf16[64,2176]{1,0:T(8,128)(2,1)S(1)} %get-tuple-element.42.refs_4_), channel_id=1, source_target_pairs={{0,2},{1,3},{2,0},{3,1},{4,6},{5,7},{6,4},{7,5},{8,10},{9,11},{10,... | collective-permute-start | bytes 835592 | tf_op jit(solution)/shard_map/ppermute | solution.py:207
  45.2 15.3 %collective-permute-start.12 = (bf16[64,2176]{1,0:T(8,128)(2,1)S(1)}, bf16[64,2176]{1,0:T(8,128)(2,1)S(1)}, u32[]{:S(2)}, u32[]{:S(2)}) collective-permute-start(bf16[64,2176]{1,0:T(8,128)(2,1)S(1)} %get-tuple-element.42.refs_4_), channel_id=1, source_target_pairs={{0,16},{1,17},{2,18},{3,19},{4,20},{5,21},{6,22},{7,23},{8,24},{9,... | collective-permute-start | bytes 835592 | tf_op jit(solution)/shard_map/ppermute | solution.py:207
  46.6 13.9 %collective-permute-start.10 = (bf16[64,2176]{1,0:T(8,128)(2,1)S(1)}, bf16[64,2176]{1,0:T(8,128)(2,1)S(1)}, u32[]{:S(2)}, u32[]{:S(2)}) collective-permute-start(bf16[64,2176]{1,0:T(8,128)(2,1)S(1)} %get-tuple-element.41), channel_id=1, source_target_pairs={{0,18},{1,19},{2,16},{3,17},{4,22},{5,23},{6,20},{7,21},{8,26},{9,... | collective-permute-start | bytes 835592 | tf_op jit(solution)/shard_map/ppermute | solution.py:207
  48.2 12.3 %collective-permute-start.13 = (bf16[64,2176]{1,0:T(8,128)(2,1)S(1)}, bf16[64,2176]{1,0:T(8,128)(2,1)S(1)}, u32[]{:S(2)}, u32[]{:S(2)}) collective-permute-start(bf16[64,2176]{1,0:T(8,128)(2,1)S(1)} %get-tuple-element.43), channel_id=1, source_target_pairs={{4,0},{5,1},{6,2},{7,3},{8,12},{9,13},{10,14},{11,15},{20,16},{21,... | collective-permute-start | bytes 835592 | tf_op jit(solution)/shard_map/ppermute | solution.py:207
  60.6 2.8 %collective-permute-start.15 = (bf16[256,2176]{1,0:T(8,128)(2,1)S(1)}, bf16[256,2176]{1,0:T(8,128)(2,1)S(1)}, u32[]{:S(2)}, u32[]{:S(2)}) collective-permute-start(bf16[256,2176]{1,0:T(8,128)(2,1)S(1)} %shard_map.80.mine), channel_id=1, source_target_pairs={{0,1},{1,0},{2,3},{3,2},{4,5},{5,4},{6,7},{7,6},{8,9},{9,8},{10,11... | collective-permute-start | bytes 3342344 | tf_op jit(solution)/shard_map/ppermute | solution.py:207
where the time goes:
time: 68.6 us; the launch traced here: 68 us
  waiting for transfers between devices  30.9 us (45%)
  starting transfers between devices  17.3 us (25%)
  Pallas kernels  14.6 us (21%)
  local copies, waits for them, and re-layouts  4.93 us (7%)
    ppermute x16, waiting for transfers between devices, swap(): return lax.ppermute(value, axes, pairs)  30.9 us
    ppermute x16, starting transfers between devices, swap(): return lax.ppermute(value, axes, pairs)  17.3 us
    pallas_call x3, Pallas kernels, call(): pl.pallas_call(functools.partial(kernel, tok_dev=tok_dev), in_specs=[insi...  11 us
    unnamed x16, local copies, waits for them, and re-layouts  4.93 us
    pallas_call x5, Pallas kernels, stack(): pl.pallas_call(functools.partial(stack_kernel, count=len(inputs), layouts...  2.75 us
  transfers between devices with their start and end apart: 16, of which 8 were waited for; matrix products, arithmetic and copies ran while one was open for 0% of the time, Pallas kernels for 11%

commit v1 on v0

--- a/solution.py
+++ b/solution.py
@@ -90,10 +90,18 @@
 LANES = 128
 
 
-def pack_kernel(tok_ref, cot_ref, route_ref, comb_ref, out_ref, *, experts):
-    tok_dev, model_dim = tok_ref.shape
-    out_ref[0:tok_dev, 0:model_dim] = tok_ref[...]
-    out_ref[tok_dev:, 0:model_dim] = cot_ref[...]
+def pack_kernel(
+    tok_hbm, cot_hbm, route_hbm, comb_hbm, out_ref, route_ref, comb_ref, sems, *, experts
+):
+    tok_dev, model_dim = tok_hbm.shape
+    tok_at = out_ref.at[pl.ds(0, tok_dev), pl.ds(0, model_dim)]
+    cot_at = out_ref.at[pl.ds(tok_dev, tok_dev), pl.ds(0, model_dim)]
+    moves = ((route_hbm, route_ref), (comb_hbm, comb_ref), (tok_hbm, tok_at), (cot_hbm, cot_at))
+    copies = [pltpu.make_async_copy(*m, sems.at[n]) for n, m in enumerate(moves)]
+    for copy in copies:
+        copy.start()
+    copies[0].wait()
+    copies[1].wait()
     line = lax.broadcasted_iota(jnp.int32, (LANES, tok_dev), 0)
     weight = jnp.zeros((LANES, tok_dev), jnp.float32)
     for k in range(route_ref.shape[0]):
@@ -113,6 +121,8 @@
     )
     out_ref[0:tok_dev, model_dim:] = turned.astype(jnp.bfloat16)
     out_ref[tok_dev:, model_dim:] = jnp.zeros((tok_dev, LANES), jnp.bfloat16)
+    copies[2].wait()
+    copies[3].wait()
 
 
 def stack_kernel(flag_ref, *refs, count, layouts):
@@ -227,10 +237,15 @@
     inside = pl.BlockSpec(memory_space=pltpu.VMEM)
     own = pl.pallas_call(
         functools.partial(pack_kernel, experts=experts),
-        in_specs=[inside] * 4,
+        in_specs=[pl.BlockSpec(memory_space=pl.ANY)] * 4,
         out_specs=inside,
         out_shape=jax.ShapeDtypeStruct((2 * tok_dev, wide), jnp.bfloat16),
-        compiler_params=pltpu.CompilerParams(vmem_limit_bytes=2 * 2**20),
+        scratch_shapes=[
+            pltpu.VMEM(routes.shape[::-1], jnp.int32),
+            pltpu.VMEM(combine.shape[::-1], jnp.float32),
+            pltpu.SemaphoreType.DMA((4,)),
+        ],
+        compiler_params=pltpu.CompilerParams(vmem_limit_bytes=63_190_000),
     )(tokens, cotangent, routes.T, combine.T)
 
     lane = jnp.arange(LANES, dtype=jnp.int32)[None, :]
@@ -295,8 +310,7 @@
         return (n, first * block, count * block)
 
     order = (Z_NEAR ^ Z_FAR, X ^ Y, X, Y, Z_NEAR)
-    first = tied([swap(own, m) for m in order])
-    middle, across, beside_x, beside_y, near = first
+    middle, across, beside_x, beside_y, near = (swap(own, m) for m in order)
 
     through, outward, pair = stack(
         [near, middle, across],
@@ -306,10 +320,9 @@
     )
     through = swap(through, Z_NEAR ^ Z_FAR, inner)
     outward = swap(outward, Z_NEAR)
-    pair_x, pair_y = swap(pair, X), swap(pair, Y)
-    (stack_a,) = stack([own, beside_x, beside_y, across], [rows_of(n) for n in range(4)])
+    pair_x, pair_y = swap(pair, X), swap(after(pair, beside_x, beside_y), Y)
+    (stack_a,) = stack([after(own, outward), beside_x, beside_y, across], [rows_of(n) for n in range(4)])
     early = call(first_kernel, stack_a, swap(stack_a, CORE), (), None, [], 6)
-    outward, through, pair_x, pair_y, *early = tied([outward, through, pair_x, pair_y, *early])
 
     far, beyond, relayed = stack(
         [through, outward, middle],

time: 68.6 us -> 62.9 us (0.917)
  local copies, waits for them, and re-layouts: 4.93 us -> 0.72 us
  starting transfers between devices: 17.3 us -> 19.2 us
  waiting for transfers between devices: 30.9 us -> 29.4 us
  Pallas kernels: 14.6 us -> 13.2 us
    unnamed x16 -> x8, local copies, waits for them, and re-layouts: 4.93 us -> 0.72 us
    pallas_call x5, Pallas kernels: 2.75 us -> 0.49 us  [stack(): pl.pallas_call(functools.partial(stack_kernel, count=len(inputs), layouts...]
    ppermute x16, starting transfers between devices: 17.3 us -> 19.2 us  [swap(): return lax.ppermute(value, axes, pairs)]
    ppermute x16, waiting for transfers between devices: 30.9 us -> 29.4 us  [swap(): return lax.ppermute(value, axes, pairs)]
    pallas_call x1, Pallas kernels: 0.86 us -> 1.74 us  [dense(): pl.pallas_call(functools.partial(pack_kernel, experts=experts), in_specs=...]
  transfers between devices with their start and end apart: 16 -> 16, of which waited for: 8 -> 10; matrix products, arithmetic and copies ran while one was open for 0% -> 0% of each run, Pallas kernels for 11% -> 11%
where the time goes in v1:
time: 62.9 us; the launch traced here: 62.7 us
  waiting for transfers between devices  29.4 us (47%)
  starting transfers between devices  19.2 us (31%)
  Pallas kernels  13.2 us (21%)
  local copies, waits for them, and re-layouts  0.72 us (1%)
    ppermute x16, waiting for transfers between devices, swap(): return lax.ppermute(value, axes, pairs)  29.4 us
    ppermute x16, starting transfers between devices, swap(): return lax.ppermute(value, axes, pairs)  19.2 us
    pallas_call x3, Pallas kernels, call(): pl.pallas_call(functools.partial(kernel, tok_dev=tok_dev), in_specs=[insi...  11 us
    pallas_call x1, Pallas kernels, dense(): pl.pallas_call(functools.partial(pack_kernel, experts=experts), in_specs=...  1.74 us
  transfers between devices with their start and end apart: 16, of which 10 were waited for; matrix products, arithmetic and copies ran while one was open for 0% of the time, Pallas kernels for 11%

profile of v1, /device:TPU:0, one launch (start us, length us, event | category | flops | bytes accessed | tf_op | source)
XLA Modules:
  0.0 62.7 jit_solution(16472360439584087590)
XLA Ops:
  0.0 1.7 %shard_map.73.refs_0_ = bf16[64,2176]{1,0:T(8,128)(2,1)} custom-call(bf16[32,2048]{1,0:T(8,128)(2,1)} %tok_hbm.1, bf16[32,2048]{1,0:T(8,128)(2,1)} %cot_hbm.1, s32[8,32]{1,0:T(8,128)} %bitcast.16, f32[8,32]{1,0:T(8,128)} %bitcast.17), custom_call_target="tpu_custom_call" | custom-call | tf_op jit(solution)/shard_map/pallas_call | solution.py:238
  1.7 5.1 %collective-permute-start.1 = (bf16[64,2176]{1,0:T(8,128)(2,1)}, bf16[64,2176]{1,0:T(8,128)(2,1)S(1)}, u32[]{:S(2)}, u32[]{:S(2)}) collective-permute-start(bf16[64,2176]{1,0:T(8,128)(2,1)} %shard_map.73.refs_0_), channel_id=1, source_target_pairs={{0,12},{1,13},{2,14},{3,15},{4,8},{5,9},{6,10},{7,11},{8,4},{9,5},... | collective-permute-start | bytes 835592 | tf_op jit(solution)/shard_map/ppermute | solution.py:217
  6.9 2.4 %collective-permute-start.2 = (bf16[64,2176]{1,0:T(8,128)(2,1)}, bf16[64,2176]{1,0:T(8,128)(2,1)S(1)}, u32[]{:S(2)}, u32[]{:S(2)}) collective-permute-start(bf16[64,2176]{1,0:T(8,128)(2,1)} %shard_map.73.refs_0_), channel_id=1, source_target_pairs={{0,18},{1,19},{2,16},{3,17},{4,22},{5,23},{6,20},{7,21},{8,26},{9,... | collective-permute-start | bytes 835592 | tf_op jit(solution)/shard_map/ppermute | solution.py:217
  9.3 0.0 collective-permute-start
  9.3 0.5 collective-permute-start.10
  9.8 0.5 collective-permute-start.11
  10.4 4.2 %collective-permute-done.1.refs_1_.refs_2_ = bf16[64,2176]{1,0:T(8,128)(2,1)S(1)} collective-permute-done((bf16[64,2176]{1,0:T(8,128)(2,1)}, bf16[64,2176]{1,0:T(8,128)(2,1)S(1)}, u32[]{:S(2)}, u32[]{:S(2)}) %collective-permute-start.1) | collective-permute-done | bytes 278560 | tf_op jit(solution)/shard_map/ppermute | solution.py:217
  14.6 3.0 %collective-permute-done.2.refs_2_.refs_3_ = bf16[64,2176]{1,0:T(8,128)(2,1)S(1)} collective-permute-done((bf16[64,2176]{1,0:T(8,128)(2,1)}, bf16[64,2176]{1,0:T(8,128)(2,1)S(1)}, u32[]{:S(2)}, u32[]{:S(2)}) %collective-permute-start.2) | collective-permute-done | bytes 278560 | tf_op jit(solution)/shard_map/ppermute | solution.py:217
  17.6 2.2 %collective-permute-done.refs_0_ = bf16[64,2176]{1,0:T(8,128)(2,1)S(1)} collective-permute-done((bf16[64,2176]{1,0:T(8,128)(2,1)}, bf16[64,2176]{1,0:T(8,128)(2,1)S(1)}, u32[]{:S(2)}, u32[]{:S(2)}) %collective-permute-start) | collective-permute-done | bytes 278560 | tf_op jit(solution)/shard_map/ppermute | solution.py:217
  19.8 0.1 shard_map.74
  19.9 1.8 %collective-permute-start.4 = (bf16[128,2176]{1,0:T(8,128)(2,1)S(1)}, bf16[128,2176]{1,0:T(8,128)(2,1)S(1)}, u32[]{:S(2)}, u32[]{:S(2)}) collective-permute-start(bf16[128,2176]{1,0:T(8,128)(2,1)S(1)} %get-tuple-element.21), channel_id=1, source_target_pairs={{0,4},{1,5},{2,6},{3,7},{4,0},{5,1},{6,2},{7,3},{8,12},{9,13},{10,... | collective-permute-start | bytes 1671176 | tf_op jit(solution)/shard_map/ppermute | solution.py:217
  21.7 0.7 %collective-permute-start.3 = (bf16[128,2176]{1,0:T(8,128)(2,1)S(1)}, bf16[128,2176]{1,0:T(8,128)(2,1)S(1)}, u32[]{:S(2)}, u32[]{:S(2)}) collective-permute-start(bf16[128,2176]{1,0:T(8,128)(2,1)S(1)} %get-tuple-element.20), channel_id=1, source_target_pairs={{4,8},{5,9},{6,10},{7,11},{8,4},{9,5},{10,6},{11,7},{20,24},{21,25... | collective-permute-start | bytes 1671176 | tf_op jit(solution)/shard_map/ppermute | solution.py:217
  22.4 0.0 collective-permute-done.10.refs_1_
  22.4 0.0 collective-permute-done.11.refs_2_
  22.4 1.5 %collective-permute-start.12 = (bf16[128,2176]{1,0:T(8,128)(2,1)S(1)}, bf16[128,2176]{1,0:T(8,128)(2,1)S(1)}, u32[]{:S(2)}, u32[]{:S(2)}) collective-permute-start(bf16[128,2176]{1,0:T(8,128)(2,1)S(1)} %get-tuple-element.26.refs_0_), channel_id=1, source_target_pairs={{0,16},{1,17},{2,18},{3,19},{4,20},{5,21},{6,22},{7,23},{8,24},{9,... | collective-permute-start | bytes 1671176 | tf_op jit(solution)/shard_map/ppermute | solution.py:217
  24.0 1.5 %collective-permute-start.9 = (bf16[128,2176]{1,0:T(8,128)(2,1)S(1)}, bf16[128,2176]{1,0:T(8,128)(2,1)S(1)}, u32[]{:S(2)}, u32[]{:S(2)}) collective-permute-start(bf16[128,2176]{1,0:T(8,128)(2,1)S(1)} %get-tuple-element.26.refs_0_), channel_id=1, source_target_pairs={{0,2},{1,3},{2,0},{3,1},{4,6},{5,7},{6,4},{7,5},{8,10},{9,11},{10,... | collective-permute-start | bytes 1671176 | tf_op jit(solution)/shard_map/ppermute | solution.py:217
  25.5 9.1 %collective-permute-done.4.refs_1_.refs_3_ = bf16[128,2176]{1,0:T(8,128)(2,1)S(1)} collective-permute-done((bf16[128,2176]{1,0:T(8,128)(2,1)S(1)}, bf16[128,2176]{1,0:T(8,128)(2,1)S(1)}, u32[]{:S(2)}, u32[]{:S(2)}) %collective-permute-start.4) | collective-permute-done | bytes 557088 | tf_op jit(solution)/shard_map/ppermute | solution.py:217
  34.5 0.0 collective-permute-done.3.refs_0_.refs_4_
  34.5 0.1 shard_map.75
  34.6 2.0 %collective-permute-done.12.refs_2_ = bf16[128,2176]{1,0:T(8,128)(2,1)S(1)} collective-permute-done((bf16[128,2176]{1,0:T(8,128)(2,1)S(1)}, bf16[128,2176]{1,0:T(8,128)(2,1)S(1)}, u32[]{:S(2)}, u32[]{:S(2)}) %collective-permute-start.12) | collective-permute-done | bytes 557088 | tf_op jit(solution)/shard_map/ppermute | solution.py:217
  36.6 1.2 %collective-permute-done.9.refs_1_ = bf16[128,2176]{1,0:T(8,128)(2,1)S(1)} collective-permute-done((bf16[128,2176]{1,0:T(8,128)(2,1)S(1)}, bf16[128,2176]{1,0:T(8,128)(2,1)S(1)}, u32[]{:S(2)}, u32[]{:S(2)}) %collective-permute-start.9) | collective-permute-done | bytes 557088 | tf_op jit(solution)/shard_map/ppermute | solution.py:217
  37.8 0.0 copy-start.3
  37.8 0.0 copy-start.1
  37.9 0.0 copy-start.2
  37.9 0.2 shard_map.76.mine
  38.0 0.0 copy-start
  38.0 0.1 collective-permute-start.13
  38.1 0.7 %copy-done.3 = bf16[64,2176]{1,0:T(8,128)(2,1)S(1)} copy-done((bf16[64,2176]{1,0:T(8,128)(2,1)S(1)}, bf16[64,2176]{1,0:T(8,128)(2,1)}, u32[]{:S(2)}) %copy-start.3) | copy-done | bytes 278552
  38.8 0.1 shard_map.77.mine
  38.9 0.1 collective-permute-start.14
  39.0 1.6 %collective-permute-start.6 = (bf16[64,2176]{1,0:T(8,128)(2,1)S(1)}, bf16[64,2176]{1,0:T(8,128)(2,1)S(1)}, u32[]{:S(2)}, u32[]{:S(2)}) collective-permute-start(bf16[64,2176]{1,0:T(8,128)(2,1)S(1)} %get-tuple-element.23.refs_4_), channel_id=1, source_target_pairs={{0,2},{1,3},{2,0},{3,1},{4,6},{5,7},{6,4},{7,5},{8,10},{9,11},{10,... | collective-permute-start | bytes 835592 | tf_op jit(solution)/shard_map/ppermute | solution.py:217
  40.5 0.5 collective-permute-start.7
  41.0 1.5 %collective-permute-start.5 = (bf16[64,2176]{1,0:T(8,128)(2,1)S(1)}, bf16[64,2176]{1,0:T(8,128)(2,1)S(1)}, u32[]{:S(2)}, u32[]{:S(2)}) collective-permute-start(bf16[64,2176]{1,0:T(8,128)(2,1)S(1)} %get-tuple-element.22), channel_id=1, source_target_pairs={{0,18},{1,19},{2,16},{3,17},{4,22},{5,23},{6,20},{7,21},{8,26},{9,... | collective-permute-start | bytes 835592 | tf_op jit(solution)/shard_map/ppermute | solution.py:217
  42.5 1.5 %collective-permute-done.14.theirs = bf16[256,2176]{1,0:T(8,128)(2,1)S(1)} collective-permute-done((bf16[256,2176]{1,0:T(8,128)(2,1)S(1)}, bf16[256,2176]{1,0:T(8,128)(2,1)S(1)}, u32[]{:S(2)}, u32[]{:S(2)}) %collective-permute-start.14) | collective-permute-done | bytes 1114144 | tf_op jit(solution)/shard_map/ppermute | solution.py:217
  44.0 1.3 %collective-permute-start.8 = (bf16[64,2176]{1,0:T(8,128)(2,1)S(1)}, bf16[64,2176]{1,0:T(8,128)(2,1)S(1)}, u32[]{:S(2)}, u32[]{:S(2)}) collective-permute-start(bf16[64,2176]{1,0:T(8,128)(2,1)S(1)} %get-tuple-element.24), channel_id=1, source_target_pairs={{4,0},{5,1},{6,2},{7,3},{8,12},{9,13},{10,14},{11,15},{20,16},{21,... | collective-permute-start | bytes 835592 | tf_op jit(solution)/shard_map/ppermute | solution.py:217
  45.3 0.0 copy-done.1
  45.3 0.0 copy-done.2
  45.3 0.0 copy-done
  45.4 1.7 %shard_map.78 = (bf16[256,2048]{1,0:T(8,128)(2,1)S(1)}, bf16[512,256]{1,0:T(8,128)(2,1)S(1)}) custom-call(bf16[256,2176]{1,0:T(8,128)(2,1)S(1)} %shard_map.77.mine, bf16[256,2176]{1,0:T(8,128)(2,1)S(1)} %collective-permute-done.14.theirs, bf16[16,128]{1,0:T(8,128)(2,1)S(1)} %broadcast_in_dim.13.pick_ref, bf16[512,2048]{1,0:T(8,128)(2,1)S(1)} %bitcast.7, ...), custom_call_target="tpu_custom_call" | custom-call | flops 1879048192 | bytes 12582912 | tf_op jit(solution)/shard_map/pallas_call | solution.py:277
  47.0 0.0 collective-permute-done.13.theirs
  47.0 4.8 %shard_map.79.add_ref = f32[512,2048]{1,0:T(8,128)S(1)} custom-call(bf16[512,2176]{1,0:T(8,128)(2,1)S(1)} %shard_map.76.mine, bf16[512,2176]{1,0:T(8,128)(2,1)S(1)} %collective-permute-done.13.theirs, bf16[16,128]{1,0:T(8,128)(2,1)S(1)} %broadcast_in_dim.13.pick_ref, bf16[512,2048]{1,0:T(8,128)(2,1)S(1)} %bitcast.8, bf16[512,2048]{1,0:T(8,128)(2,1)S(1)} %bitcast.11, ...), custom_call_target="tpu_custom_call" | custom-call | flops 3758096384 | bytes 12582912 | tf_op jit(solution)/shard_map/pallas_call | solution.py:277
  51.8 2.3 %collective-permute-done.5.refs_0_ = bf16[64,2176]{1,0:T(8,128)(2,1)S(1)} collective-permute-done((bf16[64,2176]{1,0:T(8,128)(2,1)S(1)}, bf16[64,2176]{1,0:T(8,128)(2,1)S(1)}, u32[]{:S(2)}, u32[]{:S(2)}) %collective-permute-start.5) | collective-permute-done | bytes 278560 | tf_op jit(solution)/shard_map/ppermute | solution.py:217
  54.1 0.0 collective-permute-done.6.refs_1_
  54.1 1.2 %collective-permute-done.7.refs_2_ = bf16[64,2176]{1,0:T(8,128)(2,1)S(1)} collective-permute-done((bf16[64,2176]{1,0:T(8,128)(2,1)S(1)}, bf16[64,2176]{1,0:T(8,128)(2,1)S(1)}, u32[]{:S(2)}, u32[]{:S(2)}) %collective-permute-start.7) | collective-permute-done | bytes 278560 | tf_op jit(solution)/shard_map/ppermute | solution.py:217
  55.2 0.0 collective-permute-done.8.refs_3_
  55.2 0.1 shard_map.80.mine
  55.3 0.1 collective-permute-start.15
  55.4 2.7 %collective-permute-done.15.theirs = bf16[256,2176]{1,0:T(8,128)(2,1)S(1)} collective-permute-done((bf16[256,2176]{1,0:T(8,128)(2,1)S(1)}, bf16[256,2176]{1,0:T(8,128)(2,1)S(1)}, u32[]{:S(2)}, u32[]{:S(2)}) %collective-permute-start.15) | collective-permute-done | bytes 1114144 | tf_op jit(solution)/shard_map/ppermute | solution.py:217
  58.1 4.5 %shard_map.81 = f32[512,2048]{1,0:T(8,128)} custom-call(bf16[256,2176]{1,0:T(8,128)(2,1)S(1)} %shard_map.80.mine, bf16[256,2176]{1,0:T(8,128)(2,1)S(1)} %collective-permute-done.15.theirs, bf16[16,128]{1,0:T(8,128)(2,1)S(1)} %broadcast_in_dim.13.pick_ref, bf16[512,2048]{1,0:T(8,128)(2,1)S(1)} %bitcast.9, bf16[512,2048]{1,0:T(8,128)(2,1)S(1)} %bitcast.12, ...), custom_call_target="tpu_custom_call" | custom-call | flops 1879048192 | bytes 12582912 | tf_op jit(solution)/shard_map/pallas_call | solution.py:277
  (2 shorter events, 0.0 us)
Async XLA Ops:
  1.7 12.9 %collective-permute-start.1 = (bf16[64,2176]{1,0:T(8,128)(2,1)}, bf16[64,2176]{1,0:T(8,128)(2,1)S(1)}, u32[]{:S(2)}, u32[]{:S(2)}) collective-permute-start(bf16[64,2176]{1,0:T(8,128)(2,1)} %shard_map.73.refs_0_), channel_id=1, source_target_pairs={{0,12},{1,13},{2,14},{3,15},{4,8},{5,9},{6,10},{7,11},{8,4},{9,5},... | collective-permute-start | bytes 835592 | tf_op jit(solution)/shard_map/ppermute | solution.py:217
  6.9 10.7 %collective-permute-start.2 = (bf16[64,2176]{1,0:T(8,128)(2,1)}, bf16[64,2176]{1,0:T(8,128)(2,1)S(1)}, u32[]{:S(2)}, u32[]{:S(2)}) collective-permute-start(bf16[64,2176]{1,0:T(8,128)(2,1)} %shard_map.73.refs_0_), channel_id=1, source_target_pairs={{0,18},{1,19},{2,16},{3,17},{4,22},{5,23},{6,20},{7,21},{8,26},{9,... | collective-permute-start | bytes 835592 | tf_op jit(solution)/shard_map/ppermute | solution.py:217
  9.3 10.5 %collective-permute-start = (bf16[64,2176]{1,0:T(8,128)(2,1)}, bf16[64,2176]{1,0:T(8,128)(2,1)S(1)}, u32[]{:S(2)}, u32[]{:S(2)}) collective-permute-start(bf16[64,2176]{1,0:T(8,128)(2,1)} %shard_map.73.refs_0_), channel_id=1, source_target_pairs={{0,4},{1,5},{2,6},{3,7},{4,0},{5,1},{6,2},{7,3},{8,12},{9,13},{10,... | collective-permute-start | bytes 835592 | tf_op jit(solution)/shard_map/ppermute | solution.py:217
  9.3 13.1 %collective-permute-start.10 = (bf16[64,2176]{1,0:T(8,128)(2,1)}, bf16[64,2176]{1,0:T(8,128)(2,1)S(1)}, u32[]{:S(2)}, u32[]{:S(2)}) collective-permute-start(bf16[64,2176]{1,0:T(8,128)(2,1)} %shard_map.73.refs_0_), channel_id=1, source_target_pairs={{0,2},{1,3},{2,0},{3,1},{4,6},{5,7},{6,4},{7,5},{8,10},{9,11},{10,... | collective-permute-start | bytes 835592 | tf_op jit(solution)/shard_map/ppermute | solution.py:217
  9.8 12.6 %collective-permute-start.11 = (bf16[64,2176]{1,0:T(8,128)(2,1)}, bf16[64,2176]{1,0:T(8,128)(2,1)S(1)}, u32[]{:S(2)}, u32[]{:S(2)}) collective-permute-start(bf16[64,2176]{1,0:T(8,128)(2,1)} %shard_map.73.refs_0_), channel_id=1, source_target_pairs={{0,16},{1,17},{2,18},{3,19},{4,20},{5,21},{6,22},{7,23},{8,24},{9,... | collective-permute-start | bytes 835592 | tf_op jit(solution)/shard_map/ppermute | solution.py:217
  19.9 14.6 %collective-permute-start.4 = (bf16[128,2176]{1,0:T(8,128)(2,1)S(1)}, bf16[128,2176]{1,0:T(8,128)(2,1)S(1)}, u32[]{:S(2)}, u32[]{:S(2)}) collective-permute-start(bf16[128,2176]{1,0:T(8,128)(2,1)S(1)} %get-tuple-element.21), channel_id=1, source_target_pairs={{0,4},{1,5},{2,6},{3,7},{4,0},{5,1},{6,2},{7,3},{8,12},{9,13},{10,... | collective-permute-start | bytes 1671176 | tf_op jit(solution)/shard_map/ppermute | solution.py:217
  21.7 12.8 %collective-permute-start.3 = (bf16[128,2176]{1,0:T(8,128)(2,1)S(1)}, bf16[128,2176]{1,0:T(8,128)(2,1)S(1)}, u32[]{:S(2)}, u32[]{:S(2)}) collective-permute-start(bf16[128,2176]{1,0:T(8,128)(2,1)S(1)} %get-tuple-element.20), channel_id=1, source_target_pairs={{4,8},{5,9},{6,10},{7,11},{8,4},{9,5},{10,6},{11,7},{20,24},{21,25... | collective-permute-start | bytes 1671176 | tf_op jit(solution)/shard_map/ppermute | solution.py:217
  22.4 14.2 %collective-permute-start.12 = (bf16[128,2176]{1,0:T(8,128)(2,1)S(1)}, bf16[128,2176]{1,0:T(8,128)(2,1)S(1)}, u32[]{:S(2)}, u32[]{:S(2)}) collective-permute-start(bf16[128,2176]{1,0:T(8,128)(2,1)S(1)} %get-tuple-element.26.refs_0_), channel_id=1, source_target_pairs={{0,16},{1,17},{2,18},{3,19},{4,20},{5,21},{6,22},{7,23},{8,24},{9,... | collective-permute-start | bytes 1671176 | tf_op jit(solution)/shard_map/ppermute | solution.py:217
  24.0 13.9 %collective-permute-start.9 = (bf16[128,2176]{1,0:T(8,128)(2,1)S(1)}, bf16[128,2176]{1,0:T(8,128)(2,1)S(1)}, u32[]{:S(2)}, u32[]{:S(2)}) collective-permute-start(bf16[128,2176]{1,0:T(8,128)(2,1)S(1)} %get-tuple-element.26.refs_0_), channel_id=1, source_target_pairs={{0,2},{1,3},{2,0},{3,1},{4,6},{5,7},{6,4},{7,5},{8,10},{9,11},{10,... | collective-permute-start | bytes 1671176 | tf_op jit(solution)/shard_map/ppermute | solution.py:217
  37.8 1.0 %copy-start.3 = (bf16[64,2176]{1,0:T(8,128)(2,1)S(1)}, bf16[64,2176]{1,0:T(8,128)(2,1)}, u32[]{:S(2)}) copy-start(bf16[64,2176]{1,0:T(8,128)(2,1)} %shard_map.73.refs_0_) | copy-start | bytes 835588
  37.8 7.5 %copy-start.1 = (bf16[1,2,256,2048]{3,2,1,0:T(8,128)(2,1)S(1)}, bf16[1,2,256,2048]{3,2,1,0:T(8,128)(2,1)}, u32[]{:S(2)}) copy-start(bf16[1,2,256,2048]{3,2,1,0:T(8,128)(2,1)} %param.13) | copy-start | bytes 6291460
  37.9 7.5 %copy-start.2 = (bf16[1,256,2048]{2,1,0:T(8,128)(2,1)S(1)}, bf16[1,256,2048]{2,1,0:T(8,128)(2,1)}, u32[]{:S(2)}) copy-start(bf16[1,256,2048]{2,1,0:T(8,128)(2,1)} %param.12) | copy-start | bytes 3145732
  38.0 7.3 %copy-start = (bf16[1,2,256,2048]{3,2,1,0:T(8,128)(2,1)S(1)}, bf16[1,2,256,2048]{3,2,1,0:T(8,128)(2,1)}, u32[]{:S(2)}) copy-start(bf16[1,2,256,2048]{3,2,1,0:T(8,128)(2,1)} %param.11) | copy-start | bytes 6291460
  38.0 9.0 %collective-permute-start.13 = (bf16[512,2176]{1,0:T(8,128)(2,1)S(1)}, bf16[512,2176]{1,0:T(8,128)(2,1)S(1)}, u32[]{:S(2)}, u32[]{:S(2)}) collective-permute-start(bf16[512,2176]{1,0:T(8,128)(2,1)S(1)} %shard_map.76.mine), channel_id=1, source_target_pairs={{0,1},{1,0},{2,3},{3,2},{4,5},{5,4},{6,7},{7,6},{8,9},{9,8},{10,11... | collective-permute-start | bytes 6684680 | tf_op jit(solution)/shard_map/ppermute | solution.py:217
  38.9 5.1 %collective-permute-start.14 = (bf16[256,2176]{1,0:T(8,128)(2,1)S(1)}, bf16[256,2176]{1,0:T(8,128)(2,1)S(1)}, u32[]{:S(2)}, u32[]{:S(2)}) collective-permute-start(bf16[256,2176]{1,0:T(8,128)(2,1)S(1)} %shard_map.77.mine), channel_id=1, source_target_pairs={{0,1},{1,0},{2,3},{3,2},{4,5},{5,4},{6,7},{7,6},{8,9},{9,8},{10,11... | collective-permute-start | bytes 3342344 | tf_op jit(solution)/shard_map/ppermute | solution.py:217
  39.0 15.1 %collective-permute-start.6 = (bf16[64,2176]{1,0:T(8,128)(2,1)S(1)}, bf16[64,2176]{1,0:T(8,128)(2,1)S(1)}, u32[]{:S(2)}, u32[]{:S(2)}) collective-permute-start(bf16[64,2176]{1,0:T(8,128)(2,1)S(1)} %get-tuple-element.23.refs_4_), channel_id=1, source_target_pairs={{0,2},{1,3},{2,0},{3,1},{4,6},{5,7},{6,4},{7,5},{8,10},{9,11},{10,... | collective-permute-start | bytes 835592 | tf_op jit(solution)/shard_map/ppermute | solution.py:217
  40.5 14.7 %collective-permute-start.7 = (bf16[64,2176]{1,0:T(8,128)(2,1)S(1)}, bf16[64,2176]{1,0:T(8,128)(2,1)S(1)}, u32[]{:S(2)}, u32[]{:S(2)}) collective-permute-start(bf16[64,2176]{1,0:T(8,128)(2,1)S(1)} %get-tuple-element.23.refs_4_), channel_id=1, source_target_pairs={{0,16},{1,17},{2,18},{3,19},{4,20},{5,21},{6,22},{7,23},{8,24},{9,... | collective-permute-start | bytes 835592 | tf_op jit(solution)/shard_map/ppermute | solution.py:217
  41.0 13.0 %collective-permute-start.5 = (bf16[64,2176]{1,0:T(8,128)(2,1)S(1)}, bf16[64,2176]{1,0:T(8,128)(2,1)S(1)}, u32[]{:S(2)}, u32[]{:S(2)}) collective-permute-start(bf16[64,2176]{1,0:T(8,128)(2,1)S(1)} %get-tuple-element.22), channel_id=1, source_target_pairs={{0,18},{1,19},{2,16},{3,17},{4,22},{5,23},{6,20},{7,21},{8,26},{9,... | collective-permute-start | bytes 835592 | tf_op jit(solution)/shard_map/ppermute | solution.py:217
  44.0 11.2 %collective-permute-start.8 = (bf16[64,2176]{1,0:T(8,128)(2,1)S(1)}, bf16[64,2176]{1,0:T(8,128)(2,1)S(1)}, u32[]{:S(2)}, u32[]{:S(2)}) collective-permute-start(bf16[64,2176]{1,0:T(8,128)(2,1)S(1)} %get-tuple-element.24), channel_id=1, source_target_pairs={{4,0},{5,1},{6,2},{7,3},{8,12},{9,13},{10,14},{11,15},{20,16},{21,... | collective-permute-start | bytes 835592 | tf_op jit(solution)/shard_map/ppermute | solution.py:217
  55.3 2.8 %collective-permute-start.15 = (bf16[256,2176]{1,0:T(8,128)(2,1)S(1)}, bf16[256,2176]{1,0:T(8,128)(2,1)S(1)}, u32[]{:S(2)}, u32[]{:S(2)}) collective-permute-start(bf16[256,2176]{1,0:T(8,128)(2,1)S(1)} %shard_map.80.mine), channel_id=1, source_target_pairs={{0,1},{1,0},{2,3},{3,2},{4,5},{5,4},{6,7},{7,6},{8,9},{9,8},{10,11... | collective-permute-start | bytes 3342344 | tf_op jit(solution)/shard_map/ppermute | solution.py:217

commit v2 on v1

--- a/solution.py
+++ b/solution.py
@@ -145,50 +145,46 @@
 
 def unpack(pieces, x_ref, c_ref, wt_ref, tok_dev):
     model_dim = x_ref.shape[1]
-    row = 0
-    for piece in pieces:
-        for first in range(0, piece.shape[0], 2 * tok_dev):
-            at = pl.ds(row, tok_dev)
-            x_ref[at, :] = piece[first : first + tok_dev, 0:model_dim]
-            wt_ref[at, :] = piece[first : first + tok_dev, model_dim:]
-            c_ref[at, :] = piece[first + tok_dev : first + 2 * tok_dev, 0:model_dim]
-            row += tok_dev
-
-
-def unit_dirs(weight, w_ref, v_ref, wo_ref, x_ref, c_ref, dir_ref):
+    for row, (piece, first) in enumerate(pieces):
+        at = pl.ds(row * tok_dev, tok_dev)
+        x_ref[at, :] = piece[first : first + tok_dev, 0:model_dim]
+        wt_ref[at, :] = piece[first : first + tok_dev, model_dim:]
+        c_ref[at, :] = piece[first + tok_dev : first + 2 * tok_dev, 0:model_dim]
+
+
+COLUMNS = 512
+ROWS = 256
+
+
+def rows_to_dirs(stacks, pick_ref, shards, x_ref, c_ref, wt_ref, dir_ref, tok_dev):
+    w_ref, v_ref, wo_ref = shards
     half = wo_ref.shape[0]
-    both = jnp.concatenate([w_ref[...], v_ref[...]], axis=0)
-    seen = lax.dot_general(both, x_ref[...], NT, preferred_element_type=jnp.float32)
-    back = lax.dot_general(wo_ref[...], c_ref[...], NT, preferred_element_type=jnp.float32)
-    parts = [seen[n * half : (n + 1) * half] for n in range(4)]
-    gate_dir, up_dir = directions(*parts, back * weight)
-    dir_ref[0:half, :] = gate_dir
-    dir_ref[half:, :] = up_dir
-
-
-def rows_to_dirs(stacks, pick_ref, shards, x_ref, c_ref, wt_ref, dir_ref, tok_dev):
-    unpack(stacks, x_ref, c_ref, wt_ref, tok_dev)
-    weight = lax.dot_general(pick_ref[...], wt_ref[...], NT, preferred_element_type=jnp.float32)
-    unit_dirs(weight[0:1], *shards, x_ref, c_ref, dir_ref)
-
-
-def first_kernel(mine, theirs, pick_ref, w, v, wo, x_ref, dir_ref, c_ref, wt_ref, *, tok_dev):
-    rows_to_dirs((mine, theirs), pick_ref, (w, v, wo), x_ref, c_ref, wt_ref, dir_ref, tok_dev)
-
-
-COLUMNS = 512
-
-
-def second_kernel(
-    mine, theirs, pick_ref, w, v, wo, early_x, early_dir, sum_ref, x_ref, dir_ref, c_ref, wt_ref,
-    *, tok_dev
+    pieces = [(s, first) for s in stacks for first in range(0, s.shape[0], 2 * tok_dev)]
+    for start in range(0, x_ref.shape[0], ROWS):
+        part = pieces[start // tok_dev : (start + ROWS) // tok_dev]
+        x_at = x_ref.at[pl.ds(start, ROWS)]
+        unpack(part, x_at, c_ref, wt_ref, tok_dev)
+        weight = lax.dot_general(
+            pick_ref[...], wt_ref[...], NT, preferred_element_type=jnp.float32
+        )
+        both = jnp.concatenate([w_ref[...], v_ref[...]], axis=0)
+        seen = lax.dot_general(both, x_at[...], NT, preferred_element_type=jnp.float32)
+        back = lax.dot_general(wo_ref[...], c_ref[...], NT, preferred_element_type=jnp.float32)
+        parts = [seen[n * half : (n + 1) * half] for n in range(4)]
+        gate_dir, up_dir = directions(*parts, back * weight[0:1])
+        dir_ref[0:half, start : start + ROWS] = gate_dir
+        dir_ref[half:, start : start + ROWS] = up_dir
+
+
+def early_kernel(
+    mine, theirs, pick_ref, w, v, wo, sum_ref, x_ref, dir_ref, c_ref, wt_ref, *, tok_dev
 ):
     rows_to_dirs((mine, theirs), pick_ref, (w, v, wo), x_ref, c_ref, wt_ref, dir_ref, tok_dev)
-    dirs = jnp.concatenate([early_dir[...], dir_ref[...]], axis=1)
     for n in range(sum_ref.shape[1] // COLUMNS):
         at = pl.ds(n * COLUMNS, COLUMNS)
-        rows = jnp.concatenate([early_x[:, at], x_ref[:, at]], axis=0)
-        sum_ref[:, at] = lax.dot_general(dirs, rows, NN, preferred_element_type=jnp.float32)
+        sum_ref[:, at] = lax.dot_general(
+            dir_ref[...], x_ref[:, at], NN, preferred_element_type=jnp.float32
+        )
 
 
 def last_kernel(
@@ -245,7 +241,7 @@
             pltpu.VMEM(combine.shape[::-1], jnp.float32),
             pltpu.SemaphoreType.DMA((4,)),
         ],
-        compiler_params=pltpu.CompilerParams(vmem_limit_bytes=63_190_000),
+        compiler_params=pltpu.CompilerParams(vmem_limit_bytes=63_120_000),
     )(tokens, cotangent, routes.T, combine.T)
 
     lane = jnp.arange(LANES, dtype=jnp.int32)[None, :]
@@ -259,27 +255,21 @@
         w_out.reshape(half, model_dim),
     )
 
-    def call(kernel, stack, theirs, more, outs, scratch, limit):
+    def call(kernel, stack, theirs, more, out_spec, scratch, limit):
         rows = stack.shape[0]
         operands = (stack, theirs, pick, *shards, *more)
-        held = [
-            ((rows, model_dim), jnp.bfloat16),
-            ((2 * half, rows), jnp.bfloat16),
-            ((rows, model_dim), jnp.bfloat16),
-            ((rows, LANES), jnp.bfloat16),
-        ]
-        if outs is None:
-            outs, held = held[:2], held[2:]
-            out_specs = [inside] * 2
-        else:
-            out_specs = [inside if outs[1] else pl.BlockSpec(memory_space=pl.ANY)]
-            outs = [((2 * half, model_dim), jnp.float32)]
         return pl.pallas_call(
             functools.partial(kernel, tok_dev=tok_dev),
             in_specs=[inside] * len(operands),
-            out_specs=out_specs,
-            out_shape=[jax.ShapeDtypeStruct(*o) for o in outs],
-            scratch_shapes=[pltpu.VMEM(*h) for h in held] + scratch,
+            out_specs=out_spec,
+            out_shape=jax.ShapeDtypeStruct((2 * half, model_dim), jnp.float32),
+            scratch_shapes=[
+                pltpu.VMEM((rows, model_dim), jnp.bfloat16),
+                pltpu.VMEM((2 * half, rows), jnp.bfloat16),
+                pltpu.VMEM((ROWS, model_dim), jnp.bfloat16),
+                pltpu.VMEM((ROWS, LANES), jnp.bfloat16),
+            ]
+            + scratch,
             compiler_params=pltpu.CompilerParams(vmem_limit_bytes=limit * 2**20),
             cost_estimate=pl.CostEstimate(
                 flops=2 * rows * model_dim * 7 * half,
@@ -312,41 +302,39 @@
     order = (Z_NEAR ^ Z_FAR, X ^ Y, X, Y, Z_NEAR)
     middle, across, beside_x, beside_y, near = (swap(own, m) for m in order)
 
-    through, outward, pair = stack(
-        [near, middle, across],
-        [rows_of(0), rows_of(2)],
-        [rows_of(1), rows_of(2)],
-        [rows_of(0), rows_of(1)],
-    )
-    through = swap(through, Z_NEAR ^ Z_FAR, inner)
-    outward = swap(outward, Z_NEAR)
+    (pair,) = stack([near, middle], [rows_of(0), rows_of(1)])
     pair_x, pair_y = swap(pair, X), swap(after(pair, beside_x, beside_y), Y)
-    (stack_a,) = stack([after(own, outward), beside_x, beside_y, across], [rows_of(n) for n in range(4)])
-    early = call(first_kernel, stack_a, swap(stack_a, CORE), (), None, [], 6)
-
-    far, beyond, relayed = stack(
+    through = swap(near, Z_NEAR ^ Z_FAR, inner)
+    outward = swap(middle, Z_NEAR, inner)
+    near_across = swap(after(across, pair), Z_NEAR)
+    through_across = swap(after(across, pair), Z_NEAR ^ Z_FAR, inner)
+
+    far, beyond = stack(
         [through, outward, middle],
         [(rows_of(0), rows_of(1))],
         [(rows_of(0), rows_of(2))],
-        [rows_of(0, 1)],
-    )
-    third = [swap(beyond, X ^ Y), swap(far, X), swap(far, Y), swap(relayed, Z_NEAR, inner)]
+    )
+    third = [swap(beyond, X ^ Y), swap(far, X), swap(far, Y)]
+    third += [swap(through_across, Z_NEAR, inner)]
+    (stack_a,) = stack(
+        [own, beside_x, beside_y, across, pair, pair_x, pair_y, far, near_across],
+        [rows_of(n) for n in range(4)]
+        + [rows_of(n, 0, 2) for n in range(4, 7)]
+        + [rows_of(7), rows_of(8)],
+    )
+    total = call(early_kernel, stack_a, swap(stack_a, CORE), (), inside, [], 14)
+    *third, total = tied([*third, total])
+
     (stack_b,) = stack(
-        [pair, pair_x, pair_y, outward, far],
-        [rows_of(0, 0, 2), rows_of(1, 0, 2), rows_of(2, 0, 2), rows_of(3, 1), rows_of(4)],
-    )
-    (total,) = call(second_kernel, stack_b, swap(stack_b, CORE), early, (0, True), [], 11)
-    *third, total = tied([*third, total])
-
-    (stack_c,) = stack(
-        [*third, through],
-        [rows_of(0), rows_of(1), rows_of(2), (rows_of(4, 1), rows_of(3))],
+        [*third, through_across],
+        [rows_of(0), rows_of(1), rows_of(2), (rows_of(4), rows_of(3))],
     )
     scratch = [
         pltpu.VMEM((2 * half, model_dim), jnp.float32),
         pltpu.SemaphoreType.DMA((model_dim // COLUMNS,)),
     ]
-    (out,) = call(last_kernel, stack_c, swap(stack_c, CORE), (total,), (0, False), scratch, 11)
+    outside = pl.BlockSpec(memory_space=pl.ANY)
+    out = call(last_kernel, stack_b, swap(stack_b, CORE), (total,), outside, scratch, 11)
     return out.reshape(1, 2, half, model_dim)
 
 

time: 62.9 us -> 65.7 us (1.045)
  starting transfers between devices: 19.2 us -> 22.4 us
  waiting for transfers between devices: 29.4 us -> 27.9 us
  Pallas kernels: 13.2 us -> 14.1 us
    ppermute x16 -> x17, starting transfers between devices: 19.2 us -> 22.4 us  [swap(): return lax.ppermute(value, axes, pairs)]
    ppermute x16 -> x17, waiting for transfers between devices: 29.4 us -> 27.9 us  [swap(): return lax.ppermute(value, axes, pairs)]
    pallas_call x3 -> x2, Pallas kernels: 11 us -> 12 us  [call(): pl.pallas_call(functools.partial(kernel, tok_dev=tok_dev), in_specs=[insi...]
  transfers between devices with their start and end apart: 16 -> 17, of which waited for: 10 -> 8; matrix products, arithmetic and copies ran while one was open for 0% -> 0% of each run, Pallas kernels for 11% -> 12%
where the time goes in v2:
time: 65.7 us; the launch traced here: 65.5 us
  waiting for transfers between devices  27.9 us (42%)
  starting transfers between devices  22.4 us (34%)
  Pallas kernels  14.1 us (21%)
  local copies, waits for them, and re-layouts  0.97 us (1%)
    ppermute x17, waiting for transfers between devices, swap(): return lax.ppermute(value, axes, pairs)  27.9 us
    ppermute x17, starting transfers between devices, swap(): return lax.ppermute(value, axes, pairs)  22.4 us
    pallas_call x2, Pallas kernels, call(): pl.pallas_call(functools.partial(kernel, tok_dev=tok_dev), in_specs=[insi...  12 us
    pallas_call x1, Pallas kernels, dense(): pl.pallas_call(functools.partial(pack_kernel, experts=experts), in_specs=...  1.74 us
  transfers between devices with their start and end apart: 17, of which 8 were waited for; matrix products, arithmetic and copies ran while one was open for 0% of the time, Pallas kernels for 12%

profile of v2, /device:TPU:0, one launch (start us, length us, event | category | flops | bytes accessed | tf_op | source)
XLA Modules:
  0.0 65.5 jit_solution(9330449462201387151)
XLA Ops:
  0.0 1.7 %shard_map.73.refs_0_ = bf16[64,2176]{1,0:T(8,128)(2,1)} custom-call(bf16[32,2048]{1,0:T(8,128)(2,1)} %tok_hbm.1, bf16[32,2048]{1,0:T(8,128)(2,1)} %cot_hbm.1, s32[8,32]{1,0:T(8,128)} %bitcast.13, f32[8,32]{1,0:T(8,128)} %bitcast.14), custom_call_target="tpu_custom_call" | custom-call | tf_op jit(solution)/shard_map/pallas_call | solution.py:234
  1.7 5.1 %collective-permute-start.2 = (bf16[64,2176]{1,0:T(8,128)(2,1)}, bf16[64,2176]{1,0:T(8,128)(2,1)S(1)}, u32[]{:S(2)}, u32[]{:S(2)}) collective-permute-start(bf16[64,2176]{1,0:T(8,128)(2,1)} %shard_map.73.refs_0_), channel_id=1, source_target_pairs={{0,12},{1,13},{2,14},{3,15},{4,8},{5,9},{6,10},{7,11},{8,4},{9,5},... | collective-permute-start | bytes 835592 | tf_op jit(solution)/shard_map/ppermute | solution.py:213
  6.9 0.0 collective-permute-start
  6.9 1.5 %collective-permute-start.10 = (bf16[64,2176]{1,0:T(8,128)(2,1)}, bf16[64,2176]{1,0:T(8,128)(2,1)S(1)}, u32[]{:S(2)}, u32[]{:S(2)}) collective-permute-start(bf16[64,2176]{1,0:T(8,128)(2,1)} %shard_map.73.refs_0_), channel_id=1, source_target_pairs={{0,2},{1,3},{2,0},{3,1},{4,6},{5,7},{6,4},{7,5},{8,10},{9,11},{10,... | collective-permute-start | bytes 835592 | tf_op jit(solution)/shard_map/ppermute | solution.py:213
  8.4 1.5 %collective-permute-start.11 = (bf16[64,2176]{1,0:T(8,128)(2,1)}, bf16[64,2176]{1,0:T(8,128)(2,1)S(1)}, u32[]{:S(2)}, u32[]{:S(2)}) collective-permute-start(bf16[64,2176]{1,0:T(8,128)(2,1)} %shard_map.73.refs_0_), channel_id=1, source_target_pairs={{0,16},{1,17},{2,18},{3,19},{4,20},{5,21},{6,22},{7,23},{8,24},{9,... | collective-permute-start | bytes 835592 | tf_op jit(solution)/shard_map/ppermute | solution.py:213
  9.9 0.5 collective-permute-start.7
  10.4 4.3 %collective-permute-done.2.refs_2_.refs_1_ = bf16[64,2176]{1,0:T(8,128)(2,1)S(1)} collective-permute-done((bf16[64,2176]{1,0:T(8,128)(2,1)}, bf16[64,2176]{1,0:T(8,128)(2,1)S(1)}, u32[]{:S(2)}, u32[]{:S(2)}) %collective-permute-start.2) | collective-permute-done | bytes 278560 | tf_op jit(solution)/shard_map/ppermute | solution.py:213
  14.6 5.2 %collective-permute-done.refs_0_ = bf16[64,2176]{1,0:T(8,128)(2,1)S(1)} collective-permute-done((bf16[64,2176]{1,0:T(8,128)(2,1)}, bf16[64,2176]{1,0:T(8,128)(2,1)S(1)}, u32[]{:S(2)}, u32[]{:S(2)}) %collective-permute-start) | collective-permute-done | bytes 278560 | tf_op jit(solution)/shard_map/ppermute | solution.py:213
  19.8 0.0 collective-permute-done.10.refs_1_
  19.9 2.5 %collective-permute-done.11.refs_2_ = bf16[64,2176]{1,0:T(8,128)(2,1)S(1)} collective-permute-done((bf16[64,2176]{1,0:T(8,128)(2,1)}, bf16[64,2176]{1,0:T(8,128)(2,1)S(1)}, u32[]{:S(2)}, u32[]{:S(2)}) %collective-permute-start.11) | collective-permute-done | bytes 278560 | tf_op jit(solution)/shard_map/ppermute | solution.py:213
  22.4 1.5 %collective-permute-start.13 = (bf16[128,2176]{1,0:T(8,128)(2,1)S(1)}, bf16[128,2176]{1,0:T(8,128)(2,1)S(1)}, u32[]{:S(2)}, u32[]{:S(2)}) collective-permute-start(bf16[128,2176]{1,0:T(8,128)(2,1)S(1)} %shard_map.75.refs_4_), channel_id=1, source_target_pairs={{0,16},{1,17},{2,18},{3,19},{4,20},{5,21},{6,22},{7,23},{8,24},{9,... | collective-permute-start | bytes 1671176 | tf_op jit(solution)/shard_map/ppermute | solution.py:213
  23.9 0.5 collective-permute-start.12
  24.4 0.0 collective-permute-done.7.refs_3_
  24.4 1.3 %collective-permute-start.3 = (bf16[64,2176]{1,0:T(8,128)(2,1)S(1)}, bf16[64,2176]{1,0:T(8,128)(2,1)S(1)}, u32[]{:S(2)}, u32[]{:S(2)}) collective-permute-start(bf16[64,2176]{1,0:T(8,128)(2,1)S(1)} %collective-permute-done.2.refs_2_.refs_1_), channel_id=1, source_target_pairs={{4,0},{5,1},{6,2},{7,3},{8,12},{9,13},{10,14},{11,15},{20,16},{21,... | collective-permute-start | bytes 835592 | tf_op jit(solution)/shard_map/ppermute | solution.py:213
  25.7 0.7 %collective-permute-start.1 = (bf16[64,2176]{1,0:T(8,128)(2,1)S(1)}, bf16[64,2176]{1,0:T(8,128)(2,1)S(1)}, u32[]{:S(2)}, u32[]{:S(2)}) collective-permute-start(bf16[64,2176]{1,0:T(8,128)(2,1)S(1)} %collective-permute-done.refs_0_), channel_id=1, source_target_pairs={{4,8},{5,9},{6,10},{7,11},{8,4},{9,5},{10,6},{11,7},{20,24},{21,25... | collective-permute-start | bytes 835592 | tf_op jit(solution)/shard_map/ppermute | solution.py:213
  26.4 4.0 %collective-permute-start.14 = (bf16[64,2176]{1,0:T(8,128)(2,1)S(1)}, bf16[64,2176]{1,0:T(8,128)(2,1)S(1)}, u32[]{:S(2)}, u32[]{:S(2)}) collective-permute-start(bf16[64,2176]{1,0:T(8,128)(2,1)S(1)} %collective-permute-done.7.refs_3_), channel_id=1, source_target_pairs={{0,4},{1,5},{2,6},{3,7},{4,0},{5,1},{6,2},{7,3},{8,12},{9,13},{10,... | collective-permute-start | bytes 835592 | tf_op jit(solution)/shard_map/ppermute | solution.py:213
  30.4 5.5 %collective-permute-done.3.refs_1_ = bf16[64,2176]{1,0:T(8,128)(2,1)S(1)} collective-permute-done((bf16[64,2176]{1,0:T(8,128)(2,1)S(1)}, bf16[64,2176]{1,0:T(8,128)(2,1)S(1)}, u32[]{:S(2)}, u32[]{:S(2)}) %collective-permute-start.3) | collective-permute-done | bytes 278560 | tf_op jit(solution)/shard_map/ppermute | solution.py:213
  35.8 0.0 collective-permute-done.1.refs_0_
  35.9 2.9 %collective-permute-done.14.refs_8_ = bf16[64,2176]{1,0:T(8,128)(2,1)S(1)} collective-permute-done((bf16[64,2176]{1,0:T(8,128)(2,1)S(1)}, bf16[64,2176]{1,0:T(8,128)(2,1)S(1)}, u32[]{:S(2)}, u32[]{:S(2)}) %collective-permute-start.14) | collective-permute-done | bytes 278560 | tf_op jit(solution)/shard_map/ppermute | solution.py:213
  38.8 0.0 collective-permute-done.13.refs_6_
  38.8 0.0 collective-permute-done.12.refs_5_
  38.8 0.0 copy-start.2
  38.8 1.0 %copy-done.2 = bf16[64,2176]{1,0:T(8,128)(2,1)S(1)} copy-done((bf16[64,2176]{1,0:T(8,128)(2,1)S(1)}, bf16[64,2176]{1,0:T(8,128)(2,1)}, u32[]{:S(2)}) %copy-start.2) | copy-done | bytes 278552
  39.8 0.0 copy-start
  39.8 0.0 copy-start.1
  39.8 0.0 copy-start.3
  39.8 0.2 shard_map.76.mine
  40.0 0.1 collective-permute-start.15
  40.1 0.8 %collective-permute-start.8 = (bf16[64,2176]{1,0:T(8,128)(2,1)S(1)}, bf16[64,2176]{1,0:T(8,128)(2,1)S(1)}, u32[]{:S(2)}, u32[]{:S(2)}) collective-permute-start(bf16[64,2176]{1,0:T(8,128)(2,1)S(1)} %collective-permute-done.7.refs_3_), channel_id=1, source_target_pairs={{4,8},{5,9},{6,10},{7,11},{8,4},{9,5},{10,6},{11,7},{20,24},{21,25... | collective-permute-start | bytes 835592 | tf_op jit(solution)/shard_map/ppermute | solution.py:213
  40.9 0.6 collective-permute-start.5
  41.5 0.5 collective-permute-start.6
  42.0 2.4 %collective-permute-start.4 = (bf16[64,2176]{1,0:T(8,128)(2,1)S(1)}, bf16[64,2176]{1,0:T(8,128)(2,1)S(1)}, u32[]{:S(2)}, u32[]{:S(2)}) collective-permute-start(bf16[64,2176]{1,0:T(8,128)(2,1)S(1)} %get-tuple-element.14), channel_id=1, source_target_pairs={{0,18},{1,19},{2,16},{3,17},{4,22},{5,23},{6,20},{7,21},{8,26},{9,... | collective-permute-start | bytes 835592 | tf_op jit(solution)/shard_map/ppermute | solution.py:213
  44.5 0.0 collective-permute-done.8.refs_4_
  44.5 1.3 %collective-permute-start.9 = (bf16[64,2176]{1,0:T(8,128)(2,1)S(1)}, bf16[64,2176]{1,0:T(8,128)(2,1)S(1)}, u32[]{:S(2)}, u32[]{:S(2)}) collective-permute-start(bf16[64,2176]{1,0:T(8,128)(2,1)S(1)} %collective-permute-done.8.refs_4_), channel_id=1, source_target_pairs={{4,0},{5,1},{6,2},{7,3},{8,12},{9,13},{10,14},{11,15},{20,16},{21,... | collective-permute-start | bytes 835592 | tf_op jit(solution)/shard_map/ppermute | solution.py:213
  45.8 0.2 collective-permute-done.15.theirs
  46.0 0.0 copy-done
  46.0 0.0 copy-done.1
  46.0 0.0 copy-done.3
  46.0 7.5 %shard_map.77.add_ref = f32[512,2048]{1,0:T(8,128)S(1)} custom-call(bf16[768,2176]{1,0:T(8,128)(2,1)S(1)} %shard_map.76.mine, bf16[768,2176]{1,0:T(8,128)(2,1)S(1)} %collective-permute-done.15.theirs, bf16[16,128]{1,0:T(8,128)(2,1)S(1)} %broadcast_in_dim.13.pick_ref, bf16[512,2048]{1,0:T(8,128)(2,1)S(1)} %bitcast.7, bf16[512,2048]{1,0:T(8,128)(2,1)S(1)} %bitcast.9, ...), custom_call_target="tpu_custom_call" | custom-call | flops 5637144576 | bytes 12582912 | tf_op jit(solution)/shard_map/pallas_call | solution.py:261
  53.5 4.6 %collective-permute-done.9.refs_3_ = bf16[64,2176]{1,0:T(8,128)(2,1)S(1)} collective-permute-done((bf16[64,2176]{1,0:T(8,128)(2,1)S(1)}, bf16[64,2176]{1,0:T(8,128)(2,1)S(1)}, u32[]{:S(2)}, u32[]{:S(2)}) %collective-permute-start.9) | collective-permute-done | bytes 278560 | tf_op jit(solution)/shard_map/ppermute | solution.py:213
  58.1 0.0 collective-permute-done.4.refs_0_
  58.1 0.0 collective-permute-done.5.refs_1_
  58.1 0.0 collective-permute-done.6.refs_2_
  58.1 0.1 shard_map.78.mine
  58.2 0.1 collective-permute-start.16
  58.3 2.7 %collective-permute-done.16.theirs = bf16[256,2176]{1,0:T(8,128)(2,1)S(1)} collective-permute-done((bf16[256,2176]{1,0:T(8,128)(2,1)S(1)}, bf16[256,2176]{1,0:T(8,128)(2,1)S(1)}, u32[]{:S(2)}, u32[]{:S(2)}) %collective-permute-start.16) | collective-permute-done | bytes 1114144 | tf_op jit(solution)/shard_map/ppermute | solution.py:213
  61.0 4.5 %shard_map.79 = f32[512,2048]{1,0:T(8,128)} custom-call(bf16[256,2176]{1,0:T(8,128)(2,1)S(1)} %shard_map.78.mine, bf16[256,2176]{1,0:T(8,128)(2,1)S(1)} %collective-permute-done.16.theirs, bf16[16,128]{1,0:T(8,128)(2,1)S(1)} %broadcast_in_dim.13.pick_ref, bf16[512,2048]{1,0:T(8,128)(2,1)S(1)} %bitcast.8, bf16[512,2048]{1,0:T(8,128)(2,1)S(1)} %bitcast.10, ...), custom_call_target="tpu_custom_call" | custom-call | flops 1879048192 | bytes 12582912 | tf_op jit(solution)/shard_map/pallas_call | solution.py:261
  (4 shorter events, 0.1 us)
Async XLA Ops:
  1.7 12.9 %collective-permute-start.2 = (bf16[64,2176]{1,0:T(8,128)(2,1)}, bf16[64,2176]{1,0:T(8,128)(2,1)S(1)}, u32[]{:S(2)}, u32[]{:S(2)}) collective-permute-start(bf16[64,2176]{1,0:T(8,128)(2,1)} %shard_map.73.refs_0_), channel_id=1, source_target_pairs={{0,12},{1,13},{2,14},{3,15},{4,8},{5,9},{6,10},{7,11},{8,4},{9,5},... | collective-permute-start | bytes 835592 | tf_op jit(solution)/shard_map/ppermute | solution.py:213
  6.9 12.9 %collective-permute-start = (bf16[64,2176]{1,0:T(8,128)(2,1)}, bf16[64,2176]{1,0:T(8,128)(2,1)S(1)}, u32[]{:S(2)}, u32[]{:S(2)}) collective-permute-start(bf16[64,2176]{1,0:T(8,128)(2,1)} %shard_map.73.refs_0_), channel_id=1, source_target_pairs={{0,4},{1,5},{2,6},{3,7},{4,0},{5,1},{6,2},{7,3},{8,12},{9,13},{10,... | collective-permute-start | bytes 835592 | tf_op jit(solution)/shard_map/ppermute | solution.py:213
  6.9 13.0 %collective-permute-start.10 = (bf16[64,2176]{1,0:T(8,128)(2,1)}, bf16[64,2176]{1,0:T(8,128)(2,1)S(1)}, u32[]{:S(2)}, u32[]{:S(2)}) collective-permute-start(bf16[64,2176]{1,0:T(8,128)(2,1)} %shard_map.73.refs_0_), channel_id=1, source_target_pairs={{0,2},{1,3},{2,0},{3,1},{4,6},{5,7},{6,4},{7,5},{8,10},{9,11},{10,... | collective-permute-start | bytes 835592 | tf_op jit(solution)/shard_map/ppermute | solution.py:213
  8.4 14.0 %collective-permute-start.11 = (bf16[64,2176]{1,0:T(8,128)(2,1)}, bf16[64,2176]{1,0:T(8,128)(2,1)S(1)}, u32[]{:S(2)}, u32[]{:S(2)}) collective-permute-start(bf16[64,2176]{1,0:T(8,128)(2,1)} %shard_map.73.refs_0_), channel_id=1, source_target_pairs={{0,16},{1,17},{2,18},{3,19},{4,20},{5,21},{6,22},{7,23},{8,24},{9,... | collective-permute-start | bytes 835592 | tf_op jit(solution)/shard_map/ppermute | solution.py:213
  9.9 14.6 %collective-permute-start.7 = (bf16[64,2176]{1,0:T(8,128)(2,1)}, bf16[64,2176]{1,0:T(8,128)(2,1)S(1)}, u32[]{:S(2)}, u32[]{:S(2)}) collective-permute-start(bf16[64,2176]{1,0:T(8,128)(2,1)} %shard_map.73.refs_0_), channel_id=1, source_target_pairs={{0,18},{1,19},{2,16},{3,17},{4,22},{5,23},{6,20},{7,21},{8,26},{9,... | collective-permute-start | bytes 835592 | tf_op jit(solution)/shard_map/ppermute | solution.py:213
  22.4 16.4 %collective-permute-start.13 = (bf16[128,2176]{1,0:T(8,128)(2,1)S(1)}, bf16[128,2176]{1,0:T(8,128)(2,1)S(1)}, u32[]{:S(2)}, u32[]{:S(2)}) collective-permute-start(bf16[128,2176]{1,0:T(8,128)(2,1)S(1)} %shard_map.75.refs_4_), channel_id=1, source_target_pairs={{0,16},{1,17},{2,18},{3,19},{4,20},{5,21},{6,22},{7,23},{8,24},{9,... | collective-permute-start | bytes 1671176 | tf_op jit(solution)/shard_map/ppermute | solution.py:213
  23.9 14.9 %collective-permute-start.12 = (bf16[128,2176]{1,0:T(8,128)(2,1)S(1)}, bf16[128,2176]{1,0:T(8,128)(2,1)S(1)}, u32[]{:S(2)}, u32[]{:S(2)}) collective-permute-start(bf16[128,2176]{1,0:T(8,128)(2,1)S(1)} %shard_map.75.refs_4_), channel_id=1, source_target_pairs={{0,2},{1,3},{2,0},{3,1},{4,6},{5,7},{6,4},{7,5},{8,10},{9,11},{10,... | collective-permute-start | bytes 1671176 | tf_op jit(solution)/shard_map/ppermute | solution.py:213
  24.4 11.4 %collective-permute-start.3 = (bf16[64,2176]{1,0:T(8,128)(2,1)S(1)}, bf16[64,2176]{1,0:T(8,128)(2,1)S(1)}, u32[]{:S(2)}, u32[]{:S(2)}) collective-permute-start(bf16[64,2176]{1,0:T(8,128)(2,1)S(1)} %collective-permute-done.2.refs_2_.refs_1_), channel_id=1, source_target_pairs={{4,0},{5,1},{6,2},{7,3},{8,12},{9,13},{10,14},{11,15},{20,16},{21,... | collective-permute-start | bytes 835592 | tf_op jit(solution)/shard_map/ppermute | solution.py:213
  25.7 10.1 %collective-permute-start.1 = (bf16[64,2176]{1,0:T(8,128)(2,1)S(1)}, bf16[64,2176]{1,0:T(8,128)(2,1)S(1)}, u32[]{:S(2)}, u32[]{:S(2)}) collective-permute-start(bf16[64,2176]{1,0:T(8,128)(2,1)S(1)} %collective-permute-done.refs_0_), channel_id=1, source_target_pairs={{4,8},{5,9},{6,10},{7,11},{8,4},{9,5},{10,6},{11,7},{20,24},{21,25... | collective-permute-start | bytes 835592 | tf_op jit(solution)/shard_map/ppermute | solution.py:213
  26.4 12.4 %collective-permute-start.14 = (bf16[64,2176]{1,0:T(8,128)(2,1)S(1)}, bf16[64,2176]{1,0:T(8,128)(2,1)S(1)}, u32[]{:S(2)}, u32[]{:S(2)}) collective-permute-start(bf16[64,2176]{1,0:T(8,128)(2,1)S(1)} %collective-permute-done.7.refs_3_), channel_id=1, source_target_pairs={{0,4},{1,5},{2,6},{3,7},{4,0},{5,1},{6,2},{7,3},{8,12},{9,13},{10,... | collective-permute-start | bytes 835592 | tf_op jit(solution)/shard_map/ppermute | solution.py:213
  38.8 1.0 %copy-start.2 = (bf16[64,2176]{1,0:T(8,128)(2,1)S(1)}, bf16[64,2176]{1,0:T(8,128)(2,1)}, u32[]{:S(2)}) copy-start(bf16[64,2176]{1,0:T(8,128)(2,1)} %shard_map.73.refs_0_) | copy-start | bytes 835588
  39.8 6.3 %copy-start = (bf16[1,2,256,2048]{3,2,1,0:T(8,128)(2,1)S(1)}, bf16[1,2,256,2048]{3,2,1,0:T(8,128)(2,1)}, u32[]{:S(2)}) copy-start(bf16[1,2,256,2048]{3,2,1,0:T(8,128)(2,1)} %param.11) | copy-start | bytes 6291460
  39.8 6.3 %copy-start.1 = (bf16[1,2,256,2048]{3,2,1,0:T(8,128)(2,1)S(1)}, bf16[1,2,256,2048]{3,2,1,0:T(8,128)(2,1)}, u32[]{:S(2)}) copy-start(bf16[1,2,256,2048]{3,2,1,0:T(8,128)(2,1)} %param.13) | copy-start | bytes 6291460
  39.8 6.3 %copy-start.3 = (bf16[1,256,2048]{2,1,0:T(8,128)(2,1)S(1)}, bf16[1,256,2048]{2,1,0:T(8,128)(2,1)}, u32[]{:S(2)}) copy-start(bf16[1,256,2048]{2,1,0:T(8,128)(2,1)} %param.12) | copy-start | bytes 3145732
  40.0 6.0 %collective-permute-start.15 = (bf16[768,2176]{1,0:T(8,128)(2,1)S(1)}, bf16[768,2176]{1,0:T(8,128)(2,1)S(1)}, u32[]{:S(2)}, u32[]{:S(2)}) collective-permute-start(bf16[768,2176]{1,0:T(8,128)(2,1)S(1)} %shard_map.76.mine), channel_id=1, source_target_pairs={{0,1},{1,0},{2,3},{3,2},{4,5},{5,4},{6,7},{7,6},{8,9},{9,8},{10,11... | collective-permute-start | bytes 10027016 | tf_op jit(solution)/shard_map/ppermute | solution.py:213
  40.1 4.4 %collective-permute-start.8 = (bf16[64,2176]{1,0:T(8,128)(2,1)S(1)}, bf16[64,2176]{1,0:T(8,128)(2,1)S(1)}, u32[]{:S(2)}, u32[]{:S(2)}) collective-permute-start(bf16[64,2176]{1,0:T(8,128)(2,1)S(1)} %collective-permute-done.7.refs_3_), channel_id=1, source_target_pairs={{4,8},{5,9},{6,10},{7,11},{8,4},{9,5},{10,6},{11,7},{20,24},{21,25... | collective-permute-start | bytes 835592 | tf_op jit(solution)/shard_map/ppermute | solution.py:213
  40.9 17.1 %collective-permute-start.5 = (bf16[64,2176]{1,0:T(8,128)(2,1)S(1)}, bf16[64,2176]{1,0:T(8,128)(2,1)S(1)}, u32[]{:S(2)}, u32[]{:S(2)}) collective-permute-start(bf16[64,2176]{1,0:T(8,128)(2,1)S(1)} %get-tuple-element.15.refs_7_), channel_id=1, source_target_pairs={{0,2},{1,3},{2,0},{3,1},{4,6},{5,7},{6,4},{7,5},{8,10},{9,11},{10,... | collective-permute-start | bytes 835592 | tf_op jit(solution)/shard_map/ppermute | solution.py:213
  41.5 16.5 %collective-permute-start.6 = (bf16[64,2176]{1,0:T(8,128)(2,1)S(1)}, bf16[64,2176]{1,0:T(8,128)(2,1)S(1)}, u32[]{:S(2)}, u32[]{:S(2)}) collective-permute-start(bf16[64,2176]{1,0:T(8,128)(2,1)S(1)} %get-tuple-element.15.refs_7_), channel_id=1, source_target_pairs={{0,16},{1,17},{2,18},{3,19},{4,20},{5,21},{6,22},{7,23},{8,24},{9,... | collective-permute-start | bytes 835592 | tf_op jit(solution)/shard_map/ppermute | solution.py:213
  42.0 16.0 %collective-permute-start.4 = (bf16[64,2176]{1,0:T(8,128)(2,1)S(1)}, bf16[64,2176]{1,0:T(8,128)(2,1)S(1)}, u32[]{:S(2)}, u32[]{:S(2)}) collective-permute-start(bf16[64,2176]{1,0:T(8,128)(2,1)S(1)} %get-tuple-element.14), channel_id=1, source_target_pairs={{0,18},{1,19},{2,16},{3,17},{4,22},{5,23},{6,20},{7,21},{8,26},{9,... | collective-permute-start | bytes 835592 | tf_op jit(solution)/shard_map/ppermute | solution.py:213
  44.5 13.6 %collective-permute-start.9 = (bf16[64,2176]{1,0:T(8,128)(2,1)S(1)}, bf16[64,2176]{1,0:T(8,128)(2,1)S(1)}, u32[]{:S(2)}, u32[]{:S(2)}) collective-permute-start(bf16[64,2176]{1,0:T(8,128)(2,1)S(1)} %collective-permute-done.8.refs_4_), channel_id=1, source_target_pairs={{4,0},{5,1},{6,2},{7,3},{8,12},{9,13},{10,14},{11,15},{20,16},{21,... | collective-permute-start | bytes 835592 | tf_op jit(solution)/shard_map/ppermute | solution.py:213
  58.2 2.8 %collective-permute-start.16 = (bf16[256,2176]{1,0:T(8,128)(2,1)S(1)}, bf16[256,2176]{1,0:T(8,128)(2,1)S(1)}, u32[]{:S(2)}, u32[]{:S(2)}) collective-permute-start(bf16[256,2176]{1,0:T(8,128)(2,1)S(1)} %shard_map.78.mine), channel_id=1, source_target_pairs={{0,1},{1,0},{2,3},{3,2},{4,5},{5,4},{6,7},{7,6},{8,9},{9,8},{10,11... | collective-permute-start | bytes 3342344 | tf_op jit(solution)/shard_map/ppermute | solution.py:213

commit v3 on v2

--- a/solution.py
+++ b/solution.py
@@ -302,32 +302,38 @@
     order = (Z_NEAR ^ Z_FAR, X ^ Y, X, Y, Z_NEAR)
     middle, across, beside_x, beside_y, near = (swap(own, m) for m in order)
 
-    (pair,) = stack([near, middle], [rows_of(0), rows_of(1)])
+    through, outward, pair = stack(
+        [near, middle, across],
+        [rows_of(0), rows_of(2)],
+        [rows_of(1), rows_of(2)],
+        [rows_of(0), rows_of(1)],
+    )
+    through = swap(through, Z_NEAR ^ Z_FAR, inner)
+    outward = swap(outward, Z_NEAR)
     pair_x, pair_y = swap(pair, X), swap(after(pair, beside_x, beside_y), Y)
-    through = swap(near, Z_NEAR ^ Z_FAR, inner)
-    outward = swap(middle, Z_NEAR, inner)
-    near_across = swap(after(across, pair), Z_NEAR)
-    through_across = swap(after(across, pair), Z_NEAR ^ Z_FAR, inner)
-
-    far, beyond = stack(
+
+    (held,) = stack([after(own, pair)], [rows_of(0)])
+    through, held = tied([through, held])
+
+    beyond, far, relayed = stack(
         [through, outward, middle],
+        [(rows_of(0), rows_of(2))],
         [(rows_of(0), rows_of(1))],
-        [(rows_of(0), rows_of(2))],
-    )
-    third = [swap(beyond, X ^ Y), swap(far, X), swap(far, Y)]
-    third += [swap(through_across, Z_NEAR, inner)]
+        [rows_of(0, 1)],
+    )
+    third = [swap(beyond, X ^ Y), swap(far, X), swap(far, Y), swap(relayed, Z_NEAR, inner)]
     (stack_a,) = stack(
-        [own, beside_x, beside_y, across, pair, pair_x, pair_y, far, near_across],
+        [held, beside_x, beside_y, across, pair, pair_x, pair_y, far, outward],
         [rows_of(n) for n in range(4)]
         + [rows_of(n, 0, 2) for n in range(4, 7)]
-        + [rows_of(7), rows_of(8)],
+        + [rows_of(7), rows_of(8, 1)],
     )
     total = call(early_kernel, stack_a, swap(stack_a, CORE), (), inside, [], 14)
     *third, total = tied([*third, total])
 
     (stack_b,) = stack(
-        [*third, through_across],
-        [rows_of(0), rows_of(1), rows_of(2), (rows_of(4), rows_of(3))],
+        [*third, through],
+        [rows_of(0), rows_of(1), rows_of(2), (rows_of(4, 1), rows_of(3))],
     )
     scratch = [
         pltpu.VMEM((2 * half, model_dim), jnp.float32),

time: 65.7 us -> 62.4 us (0.950)
  starting transfers between devices: 22.4 us -> 20.3 us
  waiting for transfers between devices: 27.9 us -> 26.6 us
    ppermute x17 -> x15, starting transfers between devices: 22.4 us -> 20.3 us  [swap(): return lax.ppermute(value, axes, pairs)]
    ppermute x17 -> x15, waiting for transfers between devices: 27.9 us -> 26.6 us  [swap(): return lax.ppermute(value, axes, pairs)]
  transfers between devices with their start and end apart: 17 -> 15, of which waited for: 8 -> 9; matrix products, arithmetic and copies ran while one was open for 0% -> 0% of each run, Pallas kernels for 12% -> 12%
where the time goes in v3:
time: 62.4 us; the launch traced here: 62.2 us
  waiting for transfers between devices  26.6 us (43%)
  starting transfers between devices  20.3 us (33%)
  Pallas kernels  14.2 us (23%)
  local copies, waits for them, and re-layouts  0.97 us (2%)
    ppermute x15, waiting for transfers between devices, swap(): return lax.ppermute(value, axes, pairs)  26.6 us
    ppermute x15, starting transfers between devices, swap(): return lax.ppermute(value, axes, pairs)  20.3 us
    pallas_call x2, Pallas kernels, call(): pl.pallas_call(functools.partial(kernel, tok_dev=tok_dev), in_specs=[insi...  12 us
    pallas_call x1, Pallas kernels, dense(): pl.pallas_call(functools.partial(pack_kernel, experts=experts), in_specs=...  1.74 us
  transfers between devices with their start and end apart: 15, of which 9 were waited for; matrix products, arithmetic and copies ran while one was open for 0% of the time, Pallas kernels for 12%

profile of v3, /device:TPU:0, one launch (start us, length us, event | category | flops | bytes accessed | tf_op | source)
XLA Modules:
  0.0 62.2 jit_solution(11763925747413769157)
XLA Ops:
  0.0 1.7 %shard_map.73.refs_0_ = bf16[64,2176]{1,0:T(8,128)(2,1)} custom-call(bf16[32,2048]{1,0:T(8,128)(2,1)} %tok_hbm.1, bf16[32,2048]{1,0:T(8,128)(2,1)} %cot_hbm.1, s32[8,32]{1,0:T(8,128)} %bitcast.13, f32[8,32]{1,0:T(8,128)} %bitcast.14), custom_call_target="tpu_custom_call" | custom-call | tf_op jit(solution)/shard_map/pallas_call | solution.py:234
  1.7 5.1 %collective-permute-start.1 = (bf16[64,2176]{1,0:T(8,128)(2,1)}, bf16[64,2176]{1,0:T(8,128)(2,1)S(1)}, u32[]{:S(2)}, u32[]{:S(2)}) collective-permute-start(bf16[64,2176]{1,0:T(8,128)(2,1)} %shard_map.73.refs_0_), channel_id=1, source_target_pairs={{0,12},{1,13},{2,14},{3,15},{4,8},{5,9},{6,10},{7,11},{8,4},{9,5},... | collective-permute-start | bytes 835592 | tf_op jit(solution)/shard_map/ppermute | solution.py:213
  6.9 2.4 %collective-permute-start.2 = (bf16[64,2176]{1,0:T(8,128)(2,1)}, bf16[64,2176]{1,0:T(8,128)(2,1)S(1)}, u32[]{:S(2)}, u32[]{:S(2)}) collective-permute-start(bf16[64,2176]{1,0:T(8,128)(2,1)} %shard_map.73.refs_0_), channel_id=1, source_target_pairs={{0,18},{1,19},{2,16},{3,17},{4,22},{5,23},{6,20},{7,21},{8,26},{9,... | collective-permute-start | bytes 835592 | tf_op jit(solution)/shard_map/ppermute | solution.py:213
  9.3 0.0 collective-permute-start
  9.3 0.5 collective-permute-start.10
  9.8 0.5 collective-permute-start.9
  10.4 4.2 %collective-permute-done.1.refs_1_.refs_2_ = bf16[64,2176]{1,0:T(8,128)(2,1)S(1)} collective-permute-done((bf16[64,2176]{1,0:T(8,128)(2,1)}, bf16[64,2176]{1,0:T(8,128)(2,1)S(1)}, u32[]{:S(2)}, u32[]{:S(2)}) %collective-permute-start.1) | collective-permute-done | bytes 278560 | tf_op jit(solution)/shard_map/ppermute | solution.py:213
  14.6 3.0 %collective-permute-done.2.refs_2_.refs_3_ = bf16[64,2176]{1,0:T(8,128)(2,1)S(1)} collective-permute-done((bf16[64,2176]{1,0:T(8,128)(2,1)}, bf16[64,2176]{1,0:T(8,128)(2,1)S(1)}, u32[]{:S(2)}, u32[]{:S(2)}) %collective-permute-start.2) | collective-permute-done | bytes 278560 | tf_op jit(solution)/shard_map/ppermute | solution.py:213
  17.6 2.2 %collective-permute-done.refs_0_ = bf16[64,2176]{1,0:T(8,128)(2,1)S(1)} collective-permute-done((bf16[64,2176]{1,0:T(8,128)(2,1)}, bf16[64,2176]{1,0:T(8,128)(2,1)S(1)}, u32[]{:S(2)}, u32[]{:S(2)}) %collective-permute-start) | collective-permute-done | bytes 278560 | tf_op jit(solution)/shard_map/ppermute | solution.py:213
  19.8 0.1 shard_map.74
  19.9 0.7 %collective-permute-start.3 = (bf16[128,2176]{1,0:T(8,128)(2,1)S(1)}, bf16[128,2176]{1,0:T(8,128)(2,1)S(1)}, u32[]{:S(2)}, u32[]{:S(2)}) collective-permute-start(bf16[128,2176]{1,0:T(8,128)(2,1)S(1)} %get-tuple-element.20), channel_id=1, source_target_pairs={{4,8},{5,9},{6,10},{7,11},{8,4},{9,5},{10,6},{11,7},{20,24},{21,25... | collective-permute-start | bytes 1671176 | tf_op jit(solution)/shard_map/ppermute | solution.py:213
  20.6 3.6 %collective-permute-start.4 = (bf16[128,2176]{1,0:T(8,128)(2,1)S(1)}, bf16[128,2176]{1,0:T(8,128)(2,1)S(1)}, u32[]{:S(2)}, u32[]{:S(2)}) collective-permute-start(bf16[128,2176]{1,0:T(8,128)(2,1)S(1)} %get-tuple-element.24), channel_id=1, source_target_pairs={{0,4},{1,5},{2,6},{3,7},{4,0},{5,1},{6,2},{7,3},{8,12},{9,13},{10,... | collective-permute-start | bytes 1671176 | tf_op jit(solution)/shard_map/ppermute | solution.py:213
  24.2 0.0 collective-permute-done.10.refs_2_
  24.2 0.0 collective-permute-done.9.refs_1_
  24.2 0.9 %collective-permute-start.12 = (bf16[128,2176]{1,0:T(8,128)(2,1)S(1)}, bf16[128,2176]{1,0:T(8,128)(2,1)S(1)}, u32[]{:S(2)}, u32[]{:S(2)}) collective-permute-start(bf16[128,2176]{1,0:T(8,128)(2,1)S(1)} %get-tuple-element.29.refs_4_), channel_id=1, source_target_pairs={{0,16},{1,17},{2,18},{3,19},{4,20},{5,21},{6,22},{7,23},{8,24},{9,... | collective-permute-start | bytes 1671176 | tf_op jit(solution)/shard_map/ppermute | solution.py:213
  25.1 1.5 %collective-permute-start.11 = (bf16[128,2176]{1,0:T(8,128)(2,1)S(1)}, bf16[128,2176]{1,0:T(8,128)(2,1)S(1)}, u32[]{:S(2)}, u32[]{:S(2)}) collective-permute-start(bf16[128,2176]{1,0:T(8,128)(2,1)S(1)} %get-tuple-element.29.refs_4_), channel_id=1, source_target_pairs={{0,2},{1,3},{2,0},{3,1},{4,6},{5,7},{6,4},{7,5},{8,10},{9,11},{10,... | collective-permute-start | bytes 1671176 | tf_op jit(solution)/shard_map/ppermute | solution.py:213
  26.6 0.0 copy-start.2
  26.6 1.0 %copy-done.2 = bf16[64,2176]{1,0:T(8,128)(2,1)S(1)} copy-done((bf16[64,2176]{1,0:T(8,128)(2,1)S(1)}, bf16[64,2176]{1,0:T(8,128)(2,1)}, u32[]{:S(2)}) %copy-start.2) | copy-done | bytes 278552
  27.6 0.0 collective-permute-done.3.refs_0_.refs_4_
  27.6 9.1 %collective-permute-done.4.refs_1_.refs_8_ = bf16[128,2176]{1,0:T(8,128)(2,1)S(1)} collective-permute-done((bf16[128,2176]{1,0:T(8,128)(2,1)S(1)}, bf16[128,2176]{1,0:T(8,128)(2,1)S(1)}, u32[]{:S(2)}, u32[]{:S(2)}) %collective-permute-start.4) | collective-permute-done | bytes 557088 | tf_op jit(solution)/shard_map/ppermute | solution.py:213
  36.7 0.1 shard_map.76
  36.8 1.4 %collective-permute-done.12.refs_6_ = bf16[128,2176]{1,0:T(8,128)(2,1)S(1)} collective-permute-done((bf16[128,2176]{1,0:T(8,128)(2,1)S(1)}, bf16[128,2176]{1,0:T(8,128)(2,1)S(1)}, u32[]{:S(2)}, u32[]{:S(2)}) %collective-permute-start.12) | collective-permute-done | bytes 557088 | tf_op jit(solution)/shard_map/ppermute | solution.py:213
  38.2 0.1 collective-permute-done.11.refs_5_
  38.3 0.0 copy-start
  38.3 0.0 copy-start.1
  38.3 0.0 copy-start.3
  38.3 0.2 shard_map.77.mine
  38.5 0.1 collective-permute-start.13
  38.6 1.4 %collective-permute-start.6 = (bf16[64,2176]{1,0:T(8,128)(2,1)S(1)}, bf16[64,2176]{1,0:T(8,128)(2,1)S(1)}, u32[]{:S(2)}, u32[]{:S(2)}) collective-permute-start(bf16[64,2176]{1,0:T(8,128)(2,1)S(1)} %get-tuple-element.26.refs_7_), channel_id=1, source_target_pairs={{0,2},{1,3},{2,0},{3,1},{4,6},{5,7},{6,4},{7,5},{8,10},{9,11},{10,... | collective-permute-start | bytes 835592 | tf_op jit(solution)/shard_map/ppermute | solution.py:213
  40.0 0.6 collective-permute-start.7
  40.6 1.5 %collective-permute-start.5 = (bf16[64,2176]{1,0:T(8,128)(2,1)S(1)}, bf16[64,2176]{1,0:T(8,128)(2,1)S(1)}, u32[]{:S(2)}, u32[]{:S(2)}) collective-permute-start(bf16[64,2176]{1,0:T(8,128)(2,1)S(1)} %get-tuple-element.25), channel_id=1, source_target_pairs={{0,18},{1,19},{2,16},{3,17},{4,22},{5,23},{6,20},{7,21},{8,26},{9,... | collective-permute-start | bytes 835592 | tf_op jit(solution)/shard_map/ppermute | solution.py:213
  42.1 1.3 %collective-permute-start.8 = (bf16[64,2176]{1,0:T(8,128)(2,1)S(1)}, bf16[64,2176]{1,0:T(8,128)(2,1)S(1)}, u32[]{:S(2)}, u32[]{:S(2)}) collective-permute-start(bf16[64,2176]{1,0:T(8,128)(2,1)S(1)} %get-tuple-element.27), channel_id=1, source_target_pairs={{4,0},{5,1},{6,2},{7,3},{8,12},{9,13},{10,14},{11,15},{20,16},{21,... | collective-permute-start | bytes 835592 | tf_op jit(solution)/shard_map/ppermute | solution.py:213
  43.4 1.1 %collective-permute-done.13.theirs = bf16[768,2176]{1,0:T(8,128)(2,1)S(1)} collective-permute-done((bf16[768,2176]{1,0:T(8,128)(2,1)S(1)}, bf16[768,2176]{1,0:T(8,128)(2,1)S(1)}, u32[]{:S(2)}, u32[]{:S(2)}) %collective-permute-start.13) | collective-permute-done | bytes 3342368 | tf_op jit(solution)/shard_map/ppermute | solution.py:213
  44.5 0.0 copy-done
  44.5 0.0 copy-done.1
  44.5 0.0 copy-done.3
  44.5 7.5 %shard_map.78.add_ref = f32[512,2048]{1,0:T(8,128)S(1)} custom-call(bf16[768,2176]{1,0:T(8,128)(2,1)S(1)} %shard_map.77.mine, bf16[768,2176]{1,0:T(8,128)(2,1)S(1)} %collective-permute-done.13.theirs, bf16[16,128]{1,0:T(8,128)(2,1)S(1)} %broadcast_in_dim.13.pick_ref, bf16[512,2048]{1,0:T(8,128)(2,1)S(1)} %bitcast.7, bf16[512,2048]{1,0:T(8,128)(2,1)S(1)} %bitcast.9, ...), custom_call_target="tpu_custom_call" | custom-call | flops 5637144576 | bytes 12582912 | tf_op jit(solution)/shard_map/pallas_call | solution.py:261
  52.0 2.7 %collective-permute-done.5.refs_0_ = bf16[64,2176]{1,0:T(8,128)(2,1)S(1)} collective-permute-done((bf16[64,2176]{1,0:T(8,128)(2,1)S(1)}, bf16[64,2176]{1,0:T(8,128)(2,1)S(1)}, u32[]{:S(2)}, u32[]{:S(2)}) %collective-permute-start.5) | collective-permute-done | bytes 278560 | tf_op jit(solution)/shard_map/ppermute | solution.py:213
  54.7 0.0 collective-permute-done.6.refs_1_
  54.7 0.0 collective-permute-done.7.refs_2_
  54.7 0.0 collective-permute-done.8.refs_3_
  54.7 0.1 shard_map.79.mine
  54.8 0.1 collective-permute-start.14
  54.9 2.7 %collective-permute-done.14.theirs = bf16[256,2176]{1,0:T(8,128)(2,1)S(1)} collective-permute-done((bf16[256,2176]{1,0:T(8,128)(2,1)S(1)}, bf16[256,2176]{1,0:T(8,128)(2,1)S(1)}, u32[]{:S(2)}, u32[]{:S(2)}) %collective-permute-start.14) | collective-permute-done | bytes 1114144 | tf_op jit(solution)/shard_map/ppermute | solution.py:213
  57.7 4.5 %shard_map.80 = f32[512,2048]{1,0:T(8,128)} custom-call(bf16[256,2176]{1,0:T(8,128)(2,1)S(1)} %shard_map.79.mine, bf16[256,2176]{1,0:T(8,128)(2,1)S(1)} %collective-permute-done.14.theirs, bf16[16,128]{1,0:T(8,128)(2,1)S(1)} %broadcast_in_dim.13.pick_ref, bf16[512,2048]{1,0:T(8,128)(2,1)S(1)} %bitcast.8, bf16[512,2048]{1,0:T(8,128)(2,1)S(1)} %bitcast.10, ...), custom_call_target="tpu_custom_call" | custom-call | flops 1879048192 | bytes 12582912 | tf_op jit(solution)/shard_map/pallas_call | solution.py:261
  (3 shorter events, 0.0 us)
Async XLA Ops:
  1.7 12.9 %collective-permute-start.1 = (bf16[64,2176]{1,0:T(8,128)(2,1)}, bf16[64,2176]{1,0:T(8,128)(2,1)S(1)}, u32[]{:S(2)}, u32[]{:S(2)}) collective-permute-start(bf16[64,2176]{1,0:T(8,128)(2,1)} %shard_map.73.refs_0_), channel_id=1, source_target_pairs={{0,12},{1,13},{2,14},{3,15},{4,8},{5,9},{6,10},{7,11},{8,4},{9,5},... | collective-permute-start | bytes 835592 | tf_op jit(solution)/shard_map/ppermute | solution.py:213
  6.9 10.7 %collective-permute-start.2 = (bf16[64,2176]{1,0:T(8,128)(2,1)}, bf16[64,2176]{1,0:T(8,128)(2,1)S(1)}, u32[]{:S(2)}, u32[]{:S(2)}) collective-permute-start(bf16[64,2176]{1,0:T(8,128)(2,1)} %shard_map.73.refs_0_), channel_id=1, source_target_pairs={{0,18},{1,19},{2,16},{3,17},{4,22},{5,23},{6,20},{7,21},{8,26},{9,... | collective-permute-start | bytes 835592 | tf_op jit(solution)/shard_map/ppermute | solution.py:213
  9.3 10.5 %collective-permute-start = (bf16[64,2176]{1,0:T(8,128)(2,1)}, bf16[64,2176]{1,0:T(8,128)(2,1)S(1)}, u32[]{:S(2)}, u32[]{:S(2)}) collective-permute-start(bf16[64,2176]{1,0:T(8,128)(2,1)} %shard_map.73.refs_0_), channel_id=1, source_target_pairs={{0,4},{1,5},{2,6},{3,7},{4,0},{5,1},{6,2},{7,3},{8,12},{9,13},{10,... | collective-permute-start | bytes 835592 | tf_op jit(solution)/shard_map/ppermute | solution.py:213
  9.3 14.9 %collective-permute-start.10 = (bf16[64,2176]{1,0:T(8,128)(2,1)}, bf16[64,2176]{1,0:T(8,128)(2,1)S(1)}, u32[]{:S(2)}, u32[]{:S(2)}) collective-permute-start(bf16[64,2176]{1,0:T(8,128)(2,1)} %shard_map.73.refs_0_), channel_id=1, source_target_pairs={{0,16},{1,17},{2,18},{3,19},{4,20},{5,21},{6,22},{7,23},{8,24},{9,... | collective-permute-start | bytes 835592 | tf_op jit(solution)/shard_map/ppermute | solution.py:213
  9.8 14.4 %collective-permute-start.9 = (bf16[64,2176]{1,0:T(8,128)(2,1)}, bf16[64,2176]{1,0:T(8,128)(2,1)S(1)}, u32[]{:S(2)}, u32[]{:S(2)}) collective-permute-start(bf16[64,2176]{1,0:T(8,128)(2,1)} %shard_map.73.refs_0_), channel_id=1, source_target_pairs={{0,2},{1,3},{2,0},{3,1},{4,6},{5,7},{6,4},{7,5},{8,10},{9,11},{10,... | collective-permute-start | bytes 835592 | tf_op jit(solution)/shard_map/ppermute | solution.py:213
  19.9 7.7 %collective-permute-start.3 = (bf16[128,2176]{1,0:T(8,128)(2,1)S(1)}, bf16[128,2176]{1,0:T(8,128)(2,1)S(1)}, u32[]{:S(2)}, u32[]{:S(2)}) collective-permute-start(bf16[128,2176]{1,0:T(8,128)(2,1)S(1)} %get-tuple-element.20), channel_id=1, source_target_pairs={{4,8},{5,9},{6,10},{7,11},{8,4},{9,5},{10,6},{11,7},{20,24},{21,25... | collective-permute-start | bytes 1671176 | tf_op jit(solution)/shard_map/ppermute | solution.py:213
  20.6 16.1 %collective-permute-start.4 = (bf16[128,2176]{1,0:T(8,128)(2,1)S(1)}, bf16[128,2176]{1,0:T(8,128)(2,1)S(1)}, u32[]{:S(2)}, u32[]{:S(2)}) collective-permute-start(bf16[128,2176]{1,0:T(8,128)(2,1)S(1)} %get-tuple-element.24), channel_id=1, source_target_pairs={{0,4},{1,5},{2,6},{3,7},{4,0},{5,1},{6,2},{7,3},{8,12},{9,13},{10,... | collective-permute-start | bytes 1671176 | tf_op jit(solution)/shard_map/ppermute | solution.py:213
  24.2 14.0 %collective-permute-start.12 = (bf16[128,2176]{1,0:T(8,128)(2,1)S(1)}, bf16[128,2176]{1,0:T(8,128)(2,1)S(1)}, u32[]{:S(2)}, u32[]{:S(2)}) collective-permute-start(bf16[128,2176]{1,0:T(8,128)(2,1)S(1)} %get-tuple-element.29.refs_4_), channel_id=1, source_target_pairs={{0,16},{1,17},{2,18},{3,19},{4,20},{5,21},{6,22},{7,23},{8,24},{9,... | collective-permute-start | bytes 1671176 | tf_op jit(solution)/shard_map/ppermute | solution.py:213
  25.1 13.1 %collective-permute-start.11 = (bf16[128,2176]{1,0:T(8,128)(2,1)S(1)}, bf16[128,2176]{1,0:T(8,128)(2,1)S(1)}, u32[]{:S(2)}, u32[]{:S(2)}) collective-permute-start(bf16[128,2176]{1,0:T(8,128)(2,1)S(1)} %get-tuple-element.29.refs_4_), channel_id=1, source_target_pairs={{0,2},{1,3},{2,0},{3,1},{4,6},{5,7},{6,4},{7,5},{8,10},{9,11},{10,... | collective-permute-start | bytes 1671176 | tf_op jit(solution)/shard_map/ppermute | solution.py:213
  26.6 1.0 %copy-start.2 = (bf16[64,2176]{1,0:T(8,128)(2,1)S(1)}, bf16[64,2176]{1,0:T(8,128)(2,1)}, u32[]{:S(2)}) copy-start(bf16[64,2176]{1,0:T(8,128)(2,1)} %shard_map.73.refs_0_) | copy-start | bytes 835588
  38.3 6.3 %copy-start = (bf16[1,2,256,2048]{3,2,1,0:T(8,128)(2,1)S(1)}, bf16[1,2,256,2048]{3,2,1,0:T(8,128)(2,1)}, u32[]{:S(2)}) copy-start(bf16[1,2,256,2048]{3,2,1,0:T(8,128)(2,1)} %param.11) | copy-start | bytes 6291460
  38.3 6.3 %copy-start.1 = (bf16[1,2,256,2048]{3,2,1,0:T(8,128)(2,1)S(1)}, bf16[1,2,256,2048]{3,2,1,0:T(8,128)(2,1)}, u32[]{:S(2)}) copy-start(bf16[1,2,256,2048]{3,2,1,0:T(8,128)(2,1)} %param.13) | copy-start | bytes 6291460
  38.3 6.3 %copy-start.3 = (bf16[1,256,2048]{2,1,0:T(8,128)(2,1)S(1)}, bf16[1,256,2048]{2,1,0:T(8,128)(2,1)}, u32[]{:S(2)}) copy-start(bf16[1,256,2048]{2,1,0:T(8,128)(2,1)} %param.12) | copy-start | bytes 3145732
  38.5 6.0 %collective-permute-start.13 = (bf16[768,2176]{1,0:T(8,128)(2,1)S(1)}, bf16[768,2176]{1,0:T(8,128)(2,1)S(1)}, u32[]{:S(2)}, u32[]{:S(2)}) collective-permute-start(bf16[768,2176]{1,0:T(8,128)(2,1)S(1)} %shard_map.77.mine), channel_id=1, source_target_pairs={{0,1},{1,0},{2,3},{3,2},{4,5},{5,4},{6,7},{7,6},{8,9},{9,8},{10,11... | collective-permute-start | bytes 10027016 | tf_op jit(solution)/shard_map/ppermute | solution.py:213
  38.6 16.1 %collective-permute-start.6 = (bf16[64,2176]{1,0:T(8,128)(2,1)S(1)}, bf16[64,2176]{1,0:T(8,128)(2,1)S(1)}, u32[]{:S(2)}, u32[]{:S(2)}) collective-permute-start(bf16[64,2176]{1,0:T(8,128)(2,1)S(1)} %get-tuple-element.26.refs_7_), channel_id=1, source_target_pairs={{0,2},{1,3},{2,0},{3,1},{4,6},{5,7},{6,4},{7,5},{8,10},{9,11},{10,... | collective-permute-start | bytes 835592 | tf_op jit(solution)/shard_map/ppermute | solution.py:213
  40.0 14.8 %collective-permute-start.7 = (bf16[64,2176]{1,0:T(8,128)(2,1)S(1)}, bf16[64,2176]{1,0:T(8,128)(2,1)S(1)}, u32[]{:S(2)}, u32[]{:S(2)}) collective-permute-start(bf16[64,2176]{1,0:T(8,128)(2,1)S(1)} %get-tuple-element.26.refs_7_), channel_id=1, source_target_pairs={{0,16},{1,17},{2,18},{3,19},{4,20},{5,21},{6,22},{7,23},{8,24},{9,... | collective-permute-start | bytes 835592 | tf_op jit(solution)/shard_map/ppermute | solution.py:213
  40.6 14.1 %collective-permute-start.5 = (bf16[64,2176]{1,0:T(8,128)(2,1)S(1)}, bf16[64,2176]{1,0:T(8,128)(2,1)S(1)}, u32[]{:S(2)}, u32[]{:S(2)}) collective-permute-start(bf16[64,2176]{1,0:T(8,128)(2,1)S(1)} %get-tuple-element.25), channel_id=1, source_target_pairs={{0,18},{1,19},{2,16},{3,17},{4,22},{5,23},{6,20},{7,21},{8,26},{9,... | collective-permute-start | bytes 835592 | tf_op jit(solution)/shard_map/ppermute | solution.py:213
  42.1 12.6 %collective-permute-start.8 = (bf16[64,2176]{1,0:T(8,128)(2,1)S(1)}, bf16[64,2176]{1,0:T(8,128)(2,1)S(1)}, u32[]{:S(2)}, u32[]{:S(2)}) collective-permute-start(bf16[64,2176]{1,0:T(8,128)(2,1)S(1)} %get-tuple-element.27), channel_id=1, source_target_pairs={{4,0},{5,1},{6,2},{7,3},{8,12},{9,13},{10,14},{11,15},{20,16},{21,... | collective-permute-start | bytes 835592 | tf_op jit(solution)/shard_map/ppermute | solution.py:213
  54.8 2.8 %collective-permute-start.14 = (bf16[256,2176]{1,0:T(8,128)(2,1)S(1)}, bf16[256,2176]{1,0:T(8,128)(2,1)S(1)}, u32[]{:S(2)}, u32[]{:S(2)}) collective-permute-start(bf16[256,2176]{1,0:T(8,128)(2,1)S(1)} %shard_map.79.mine), channel_id=1, source_target_pairs={{0,1},{1,0},{2,3},{3,2},{4,5},{5,4},{6,7},{7,6},{8,9},{9,8},{10,11... | collective-permute-start | bytes 3342344 | tf_op jit(solution)/shard_map/ppermute | solution.py:213

commit v4 on v3

--- a/solution.py
+++ b/solution.py
@@ -156,52 +156,47 @@
 ROWS = 256
 
 
-def rows_to_dirs(stacks, pick_ref, shards, x_ref, c_ref, wt_ref, dir_ref, tok_dev):
-    w_ref, v_ref, wo_ref = shards
+def sum_kernel(*refs, stacks, adds, leaves, tok_dev):
+    pieces = []
+    for stack, skipped in zip(refs, stacks):
+        pieces += [(stack, n) for n in range(skipped, stack.shape[0], 2 * tok_dev)]
+    pick_ref, w_ref, v_ref, wo_ref, *refs = refs[len(stacks) :]
+    if adds:
+        add_ref, *refs = refs
+    if leaves:
+        out_ref, x_ref, dir_ref, c_ref, wt_ref, sum_ref, sems = refs
+    else:
+        sum_ref, x_ref, dir_ref, c_ref, wt_ref = refs
     half = wo_ref.shape[0]
-    pieces = [(s, first) for s in stacks for first in range(0, s.shape[0], 2 * tok_dev)]
-    for start in range(0, x_ref.shape[0], ROWS):
-        part = pieces[start // tok_dev : (start + ROWS) // tok_dev]
-        x_at = x_ref.at[pl.ds(start, ROWS)]
+    rows = x_ref.shape[0]
+    for start in range(0, rows, c_ref.shape[0]):
+        step = min(c_ref.shape[0], rows - start)
+        part = pieces[start // tok_dev : (start + step) // tok_dev]
+        x_at = x_ref.at[pl.ds(start, step)]
         unpack(part, x_at, c_ref, wt_ref, tok_dev)
         weight = lax.dot_general(
-            pick_ref[...], wt_ref[...], NT, preferred_element_type=jnp.float32
+            pick_ref[...], wt_ref[0:step], NT, preferred_element_type=jnp.float32
         )
         both = jnp.concatenate([w_ref[...], v_ref[...]], axis=0)
         seen = lax.dot_general(both, x_at[...], NT, preferred_element_type=jnp.float32)
-        back = lax.dot_general(wo_ref[...], c_ref[...], NT, preferred_element_type=jnp.float32)
+        back = lax.dot_general(
+            wo_ref[...], c_ref[0:step], NT, preferred_element_type=jnp.float32
+        )
         parts = [seen[n * half : (n + 1) * half] for n in range(4)]
         gate_dir, up_dir = directions(*parts, back * weight[0:1])
-        dir_ref[0:half, start : start + ROWS] = gate_dir
-        dir_ref[half:, start : start + ROWS] = up_dir
-
-
-def early_kernel(
-    mine, theirs, pick_ref, w, v, wo, sum_ref, x_ref, dir_ref, c_ref, wt_ref, *, tok_dev
-):
-    rows_to_dirs((mine, theirs), pick_ref, (w, v, wo), x_ref, c_ref, wt_ref, dir_ref, tok_dev)
+        dir_ref[0:half, start : start + step] = gate_dir
+        dir_ref[half:, start : start + step] = up_dir
+    copies = []
     for n in range(sum_ref.shape[1] // COLUMNS):
         at = pl.ds(n * COLUMNS, COLUMNS)
-        sum_ref[:, at] = lax.dot_general(
+        term = lax.dot_general(
             dir_ref[...], x_ref[:, at], NN, preferred_element_type=jnp.float32
         )
-
-
-def last_kernel(
-    mine, theirs, pick_ref, w, v, wo, add_ref, out_ref, x_ref, dir_ref, c_ref, wt_ref, sum_ref, sems,
-    *, tok_dev
-):
-    rows_to_dirs((mine, theirs), pick_ref, (w, v, wo), x_ref, c_ref, wt_ref, dir_ref, tok_dev)
-    copies = []
-    for n in range(out_ref.shape[1] // COLUMNS):
-        at = pl.ds(n * COLUMNS, COLUMNS)
-        total = lax.dot_general(
-            dir_ref[...], x_ref[:, at], NN, preferred_element_type=jnp.float32
-        )
-        sum_ref[:, at] = total + add_ref[:, at]
-        copy = pltpu.make_async_copy(sum_ref.at[:, at], out_ref.at[:, at], sems.at[n])
-        copy.start()
-        copies.append(copy)
+        sum_ref[:, at] = term + add_ref[:, at] if adds else term
+        if leaves:
+            copy = pltpu.make_async_copy(sum_ref.at[:, at], out_ref.at[:, at], sems.at[n])
+            copy.start()
+            copies.append(copy)
     for copy in copies:
         copy.wait()
 
@@ -255,21 +250,31 @@
         w_out.reshape(half, model_dim),
     )
 
-    def call(kernel, stack, theirs, more, out_spec, scratch, limit):
-        rows = stack.shape[0]
-        operands = (stack, theirs, pick, *shards, *more)
+    def add_terms(stacks, total, limit, leaves=False, skipped=0):
+        skips = [skipped] + [0] * (len(stacks) - 1)
+        rows = (sum(stack.shape[0] for stack in stacks) - skipped) // 2
+        step = min(rows, ROWS)
+        adds = [] if total is None else [total]
+        operands = (*stacks, pick, *shards, *adds)
+        scratch = [
+            pltpu.VMEM((rows, model_dim), jnp.bfloat16),
+            pltpu.VMEM((2 * half, rows), jnp.bfloat16),
+            pltpu.VMEM((step, model_dim), jnp.bfloat16),
+            pltpu.VMEM((step, LANES), jnp.bfloat16),
+        ]
+        if leaves:
+            scratch += [
+                pltpu.VMEM((2 * half, model_dim), jnp.float32),
+                pltpu.SemaphoreType.DMA((model_dim // COLUMNS,)),
+            ]
         return pl.pallas_call(
-            functools.partial(kernel, tok_dev=tok_dev),
+            functools.partial(
+                sum_kernel, stacks=skips, adds=len(adds), leaves=leaves, tok_dev=tok_dev
+            ),
             in_specs=[inside] * len(operands),
-            out_specs=out_spec,
+            out_specs=pl.BlockSpec(memory_space=pl.ANY) if leaves else inside,
             out_shape=jax.ShapeDtypeStruct((2 * half, model_dim), jnp.float32),
-            scratch_shapes=[
-                pltpu.VMEM((rows, model_dim), jnp.bfloat16),
-                pltpu.VMEM((2 * half, rows), jnp.bfloat16),
-                pltpu.VMEM((ROWS, model_dim), jnp.bfloat16),
-                pltpu.VMEM((ROWS, LANES), jnp.bfloat16),
-            ]
-            + scratch,
+            scratch_shapes=scratch,
             compiler_params=pltpu.CompilerParams(vmem_limit_bytes=limit * 2**20),
             cost_estimate=pl.CostEstimate(
                 flops=2 * rows * model_dim * 7 * half,
@@ -302,6 +307,8 @@
     order = (Z_NEAR ^ Z_FAR, X ^ Y, X, Y, Z_NEAR)
     middle, across, beside_x, beside_y, near = (swap(own, m) for m in order)
 
+    (held,) = stack([own], [rows_of(0)])
+    middle, held = tied([middle, held])
     through, outward, pair = stack(
         [near, middle, across],
         [rows_of(0), rows_of(2)],
@@ -312,35 +319,32 @@
     outward = swap(outward, Z_NEAR)
     pair_x, pair_y = swap(pair, X), swap(after(pair, beside_x, beside_y), Y)
 
-    (held,) = stack([after(own, pair)], [rows_of(0)])
-    through, held = tied([through, held])
-
-    beyond, far, relayed = stack(
+    total = add_terms([held, beside_x, beside_y, across], None, 8)
+    through, total = tied([through, total])
+
+    beyond, far_x, far_y, far, relayed = stack(
         [through, outward, middle],
         [(rows_of(0), rows_of(2))],
-        [(rows_of(0), rows_of(1))],
+        *[[(rows_of(0), rows_of(1))]] * 3,
         [rows_of(0, 1)],
     )
-    third = [swap(beyond, X ^ Y), swap(far, X), swap(far, Y), swap(relayed, Z_NEAR, inner)]
-    (stack_a,) = stack(
+    third = [swap(beyond, X ^ Y), swap(far_x, X), swap(far_y, Y), swap(relayed, Z_NEAR, inner)]
+    (stack_b,) = stack(
         [held, beside_x, beside_y, across, pair, pair_x, pair_y, far, outward],
         [rows_of(n) for n in range(4)]
         + [rows_of(n, 0, 2) for n in range(4, 7)]
         + [rows_of(7), rows_of(8, 1)],
     )
-    total = call(early_kernel, stack_a, swap(stack_a, CORE), (), inside, [], 14)
+    total = add_terms([stack_b, swap(stack_b, CORE)], total, 14, skipped=4 * block)
     *third, total = tied([*third, total])
 
-    (stack_b,) = stack(
+    (stack_c,) = stack(
         [*third, through],
         [rows_of(0), rows_of(1), rows_of(2), (rows_of(4, 1), rows_of(3))],
     )
-    scratch = [
-        pltpu.VMEM((2 * half, model_dim), jnp.float32),
-        pltpu.SemaphoreType.DMA((model_dim // COLUMNS,)),
-    ]
-    outside = pl.BlockSpec(memory_space=pl.ANY)
-    out = call(last_kernel, stack_b, swap(stack_b, CORE), (total,), outside, scratch, 11)
+    theirs = swap(stack_c, CORE)
+    total = add_terms([stack_c], total, 8)
+    out = add_terms([theirs], total, 11, leaves=True)
     return out.reshape(1, 2, half, model_dim)
 
 

time: 62.4 us -> 63.3 us (1.014)
  waiting for transfers between devices: 26.6 us -> 16.1 us
  Pallas kernels: 14.2 us -> 20.9 us
  local copies, waits for them, and re-layouts: 0.97 us -> 5.41 us
    ppermute x15, waiting for transfers between devices: 26.6 us -> 16.1 us  [swap(): return lax.ppermute(value, axes, pairs)]
    pallas_call x2 -> x4, Pallas kernels: 12 us -> 18.4 us  [add_terms(): pl.pallas_call(functools.partial(sum_kernel, stacks=skips, adds=len(adds)...]
    unnamed x8 -> x14, local copies, waits for them, and re-layouts: 0.97 us -> 5.4 us
  transfers between devices with their start and end apart: 15 -> 15, of which waited for: 9 -> 8; matrix products, arithmetic and copies ran while one was open for 0% -> 0% of each run, Pallas kernels for 12% -> 23%
where the time goes in v4:
time: 63.3 us; the launch traced here: 63 us
  Pallas kernels  20.9 us (33%)
  starting transfers between devices  20.3 us (32%)
  waiting for transfers between devices  16.1 us (25%)
  local copies, waits for them, and re-layouts  5.41 us (9%)
    ppermute x15, starting transfers between devices, swap(): return lax.ppermute(value, axes, pairs)  20.3 us
    pallas_call x4, Pallas kernels, add_terms(): pl.pallas_call(functools.partial(sum_kernel, stacks=skips, adds=len(adds)...  18.4 us
    ppermute x15, waiting for transfers between devices, swap(): return lax.ppermute(value, axes, pairs)  16.1 us
    unnamed x14, local copies, waits for them, and re-layouts  5.4 us
    pallas_call x1, Pallas kernels, dense(): pl.pallas_call(functools.partial(pack_kernel, experts=experts), in_specs=...  1.74 us
  transfers between devices with their start and end apart: 15, of which 8 were waited for; matrix products, arithmetic and copies ran while one was open for 0% of the time, Pallas kernels for 23%

profile of v4, /device:TPU:0, one launch (start us, length us, event | category | flops | bytes accessed | tf_op | source)
XLA Modules:
  0.0 63.0 jit_solution(11607020249758584158)
XLA Ops:
  0.0 1.7 %shard_map.73.refs_0_ = bf16[64,2176]{1,0:T(8,128)(2,1)} custom-call(bf16[32,2048]{1,0:T(8,128)(2,1)} %tok_hbm.1, bf16[32,2048]{1,0:T(8,128)(2,1)} %cot_hbm.1, s32[8,32]{1,0:T(8,128)} %bitcast.19, f32[8,32]{1,0:T(8,128)} %bitcast.20), custom_call_target="tpu_custom_call" | custom-call | tf_op jit(solution)/shard_map/pallas_call | solution.py:229
  1.7 5.1 %collective-permute-start.1 = (bf16[64,2176]{1,0:T(8,128)(2,1)}, bf16[64,2176]{1,0:T(8,128)(2,1)S(1)}, u32[]{:S(2)}, u32[]{:S(2)}) collective-permute-start(bf16[64,2176]{1,0:T(8,128)(2,1)} %shard_map.73.refs_0_), channel_id=1, source_target_pairs={{0,12},{1,13},{2,14},{3,15},{4,8},{5,9},{6,10},{7,11},{8,4},{9,5},... | collective-permute-start | bytes 835592 | tf_op jit(solution)/shard_map/ppermute | solution.py:208
  6.9 2.4 %collective-permute-start.2 = (bf16[64,2176]{1,0:T(8,128)(2,1)}, bf16[64,2176]{1,0:T(8,128)(2,1)S(1)}, u32[]{:S(2)}, u32[]{:S(2)}) collective-permute-start(bf16[64,2176]{1,0:T(8,128)(2,1)} %shard_map.73.refs_0_), channel_id=1, source_target_pairs={{0,18},{1,19},{2,16},{3,17},{4,22},{5,23},{6,20},{7,21},{8,26},{9,... | collective-permute-start | bytes 835592 | tf_op jit(solution)/shard_map/ppermute | solution.py:208
  9.3 0.0 collective-permute-start
  9.3 0.5 collective-permute-start.5
  9.8 0.5 collective-permute-start.4
  10.4 0.0 copy-start.6
  10.4 1.0 %copy-done.6 = bf16[64,2176]{1,0:T(8,128)(2,1)S(1)} copy-done((bf16[64,2176]{1,0:T(8,128)(2,1)S(1)}, bf16[64,2176]{1,0:T(8,128)(2,1)}, u32[]{:S(2)}) %copy-start.6) | copy-done | bytes 278552
  11.4 3.2 %collective-permute-done.1.refs_1_.refs_2_ = bf16[64,2176]{1,0:T(8,128)(2,1)S(1)} collective-permute-done((bf16[64,2176]{1,0:T(8,128)(2,1)}, bf16[64,2176]{1,0:T(8,128)(2,1)S(1)}, u32[]{:S(2)}, u32[]{:S(2)}) %collective-permute-start.1) | collective-permute-done | bytes 278560 | tf_op jit(solution)/shard_map/ppermute | solution.py:208
  14.6 3.0 %collective-permute-done.2.refs_2_.refs_3_ = bf16[64,2176]{1,0:T(8,128)(2,1)S(1)} collective-permute-done((bf16[64,2176]{1,0:T(8,128)(2,1)}, bf16[64,2176]{1,0:T(8,128)(2,1)S(1)}, u32[]{:S(2)}, u32[]{:S(2)}) %collective-permute-start.2) | collective-permute-done | bytes 278560 | tf_op jit(solution)/shard_map/ppermute | solution.py:208
  17.6 2.2 %collective-permute-done.refs_0_ = bf16[64,2176]{1,0:T(8,128)(2,1)S(1)} collective-permute-done((bf16[64,2176]{1,0:T(8,128)(2,1)}, bf16[64,2176]{1,0:T(8,128)(2,1)S(1)}, u32[]{:S(2)}, u32[]{:S(2)}) %collective-permute-start) | collective-permute-done | bytes 278560 | tf_op jit(solution)/shard_map/ppermute | solution.py:208
  19.8 0.1 shard_map.75
  19.9 0.7 %collective-permute-start.3 = (bf16[128,2176]{1,0:T(8,128)(2,1)S(1)}, bf16[128,2176]{1,0:T(8,128)(2,1)S(1)}, u32[]{:S(2)}, u32[]{:S(2)}) collective-permute-start(bf16[128,2176]{1,0:T(8,128)(2,1)S(1)} %get-tuple-element.24), channel_id=1, source_target_pairs={{4,8},{5,9},{6,10},{7,11},{8,4},{9,5},{10,6},{11,7},{20,24},{21,25... | collective-permute-start | bytes 1671176 | tf_op jit(solution)/shard_map/ppermute | solution.py:208
  20.6 3.6 %collective-permute-start.6 = (bf16[128,2176]{1,0:T(8,128)(2,1)S(1)}, bf16[128,2176]{1,0:T(8,128)(2,1)S(1)}, u32[]{:S(2)}, u32[]{:S(2)}) collective-permute-start(bf16[128,2176]{1,0:T(8,128)(2,1)S(1)} %get-tuple-element.27), channel_id=1, source_target_pairs={{0,4},{1,5},{2,6},{3,7},{4,0},{5,1},{6,2},{7,3},{8,12},{9,13},{10,... | collective-permute-start | bytes 1671176 | tf_op jit(solution)/shard_map/ppermute | solution.py:208
  24.2 0.0 collective-permute-done.5.refs_2_
  24.2 0.0 collective-permute-done.4.refs_1_
  24.2 0.9 %collective-permute-start.12 = (bf16[128,2176]{1,0:T(8,128)(2,1)S(1)}, bf16[128,2176]{1,0:T(8,128)(2,1)S(1)}, u32[]{:S(2)}, u32[]{:S(2)}) collective-permute-start(bf16[128,2176]{1,0:T(8,128)(2,1)S(1)} %get-tuple-element.33.refs_4_), channel_id=1, source_target_pairs={{0,16},{1,17},{2,18},{3,19},{4,20},{5,21},{6,22},{7,23},{8,24},{9,... | collective-permute-start | bytes 1671176 | tf_op jit(solution)/shard_map/ppermute | solution.py:208
  25.1 1.5 %collective-permute-start.11 = (bf16[128,2176]{1,0:T(8,128)(2,1)S(1)}, bf16[128,2176]{1,0:T(8,128)(2,1)S(1)}, u32[]{:S(2)}, u32[]{:S(2)}) collective-permute-start(bf16[128,2176]{1,0:T(8,128)(2,1)S(1)} %get-tuple-element.33.refs_4_), channel_id=1, source_target_pairs={{0,2},{1,3},{2,0},{3,1},{4,6},{5,7},{6,4},{7,5},{8,10},{9,11},{10,... | collective-permute-start | bytes 1671176 | tf_op jit(solution)/shard_map/ppermute | solution.py:208
  26.6 0.0 copy-start
  26.6 1.6 %copy-done = bf16[1,2,256,2048]{3,2,1,0:T(8,128)(2,1)S(1)} copy-done((bf16[1,2,256,2048]{3,2,1,0:T(8,128)(2,1)S(1)}, bf16[1,2,256,2048]{3,2,1,0:T(8,128)(2,1)}, u32[]{:S(2)}) %copy-start) | copy-done | bytes 2097176
  28.2 0.0 copy-start.2
  28.2 1.6 %copy-done.2 = bf16[1,2,256,2048]{3,2,1,0:T(8,128)(2,1)S(1)} copy-done((bf16[1,2,256,2048]{3,2,1,0:T(8,128)(2,1)S(1)}, bf16[1,2,256,2048]{3,2,1,0:T(8,128)(2,1)}, u32[]{:S(2)}) %copy-start.2) | copy-done | bytes 2097176
  29.8 0.0 copy-start.4
  29.8 1.2 %copy-done.4 = bf16[1,256,2048]{2,1,0:T(8,128)(2,1)S(1)} copy-done((bf16[1,256,2048]{2,1,0:T(8,128)(2,1)S(1)}, bf16[1,256,2048]{2,1,0:T(8,128)(2,1)}, u32[]{:S(2)}) %copy-start.4) | copy-done | bytes 1048600
  31.0 3.2 %shard_map.76.refs_6_ = f32[512,2048]{1,0:T(8,128)S(1)} custom-call(bf16[64,2176]{1,0:T(8,128)(2,1)S(1)} %shard_map.74.refs_0_, bf16[64,2176]{1,0:T(8,128)(2,1)S(1)} %collective-permute-done.4.refs_1_, bf16[64,2176]{1,0:T(8,128)(2,1)S(1)} %collective-permute-done.5.refs_2_, bf16[64,2176]{1,0:T(8,128)(2,1)S(1)} %collective-permute-done.2.refs_2_.refs_3_, ...), custom_call_target="tpu_custom_call" | custom-call | flops 939524096 | bytes 12582912 | tf_op jit(solution)/shard_map/pallas_call | solution.py:270
  34.3 0.0 collective-permute-done.3.refs_0_.refs_4_
  34.3 2.4 %collective-permute-done.6.refs_1_.refs_8_ = bf16[128,2176]{1,0:T(8,128)(2,1)S(1)} collective-permute-done((bf16[128,2176]{1,0:T(8,128)(2,1)S(1)}, bf16[128,2176]{1,0:T(8,128)(2,1)S(1)}, u32[]{:S(2)}, u32[]{:S(2)}) %collective-permute-start.6) | collective-permute-done | bytes 557088 | tf_op jit(solution)/shard_map/ppermute | solution.py:208
  36.7 0.1 shard_map.77
  36.9 1.3 %collective-permute-done.12.refs_6_ = bf16[128,2176]{1,0:T(8,128)(2,1)S(1)} collective-permute-done((bf16[128,2176]{1,0:T(8,128)(2,1)S(1)}, bf16[128,2176]{1,0:T(8,128)(2,1)S(1)}, u32[]{:S(2)}, u32[]{:S(2)}) %collective-permute-start.12) | collective-permute-done | bytes 557088 | tf_op jit(solution)/shard_map/ppermute | solution.py:208
  38.2 0.1 collective-permute-done.11.refs_5_
  38.3 0.0 copy-start.1
  38.3 0.0 copy-start.3
  38.3 0.0 copy-start.5
  38.3 0.2 shard_map.78.refs_0_
  38.5 0.1 collective-permute-start.13
  38.6 1.5 %collective-permute-start.7 = (bf16[64,2176]{1,0:T(8,128)(2,1)S(1)}, bf16[64,2176]{1,0:T(8,128)(2,1)S(1)}, u32[]{:S(2)}, u32[]{:S(2)}) collective-permute-start(bf16[64,2176]{1,0:T(8,128)(2,1)S(1)} %get-tuple-element.28), channel_id=1, source_target_pairs={{0,18},{1,19},{2,16},{3,17},{4,22},{5,23},{6,20},{7,21},{8,26},{9,... | collective-permute-start | bytes 835592 | tf_op jit(solution)/shard_map/ppermute | solution.py:208
  40.0 1.7 %collective-permute-start.8 = (bf16[64,2176]{1,0:T(8,128)(2,1)S(1)}, bf16[64,2176]{1,0:T(8,128)(2,1)S(1)}, u32[]{:S(2)}, u32[]{:S(2)}) collective-permute-start(bf16[64,2176]{1,0:T(8,128)(2,1)S(1)} %get-tuple-element.29), channel_id=1, source_target_pairs={{0,2},{1,3},{2,0},{3,1},{4,6},{5,7},{6,4},{7,5},{8,10},{9,11},{10,... | collective-permute-start | bytes 835592 | tf_op jit(solution)/shard_map/ppermute | solution.py:208
  41.8 0.4 collective-permute-start.9
  42.1 1.3 %collective-permute-start.10 = (bf16[64,2176]{1,0:T(8,128)(2,1)S(1)}, bf16[64,2176]{1,0:T(8,128)(2,1)S(1)}, u32[]{:S(2)}, u32[]{:S(2)}) collective-permute-start(bf16[64,2176]{1,0:T(8,128)(2,1)S(1)} %get-tuple-element.31), channel_id=1, source_target_pairs={{4,0},{5,1},{6,2},{7,3},{8,12},{9,13},{10,14},{11,15},{20,16},{21,... | collective-permute-start | bytes 835592 | tf_op jit(solution)/shard_map/ppermute | solution.py:208
  43.4 1.1 %collective-permute-done.13.refs_1_ = bf16[768,2176]{1,0:T(8,128)(2,1)S(1)} collective-permute-done((bf16[768,2176]{1,0:T(8,128)(2,1)S(1)}, bf16[768,2176]{1,0:T(8,128)(2,1)S(1)}, u32[]{:S(2)}, u32[]{:S(2)}) %collective-permute-start.13) | collective-permute-done | bytes 3342368 | tf_op jit(solution)/shard_map/ppermute | solution.py:208
  44.5 0.0 copy-done.1
  44.5 0.0 copy-done.3
  44.5 0.0 copy-done.5
  44.5 7.5 %shard_map.79.refs_5_ = f32[512,2048]{1,0:T(8,128)S(1)} custom-call(bf16[768,2176]{1,0:T(8,128)(2,1)S(1)} %shard_map.78.refs_0_, bf16[768,2176]{1,0:T(8,128)(2,1)S(1)} %collective-permute-done.13.refs_1_, bf16[16,128]{1,0:T(8,128)(2,1)S(1)} %broadcast_in_dim.13.refs_4_.refs_2_.refs_1_, bf16[512,2048]{1,0:T(8,128)(2,1)S(1)} %bitcast.8, ...), custom_call_target="tpu_custom_call" | custom-call | flops 4697620480 | bytes 12582912 | tf_op jit(solution)/shard_map/pallas_call | solution.py:270
  52.0 0.0 collective-permute-done.7.refs_0_
  52.0 2.7 %collective-permute-done.8.refs_1_ = bf16[64,2176]{1,0:T(8,128)(2,1)S(1)} collective-permute-done((bf16[64,2176]{1,0:T(8,128)(2,1)S(1)}, bf16[64,2176]{1,0:T(8,128)(2,1)S(1)}, u32[]{:S(2)}, u32[]{:S(2)}) %collective-permute-start.8) | collective-permute-done | bytes 278560 | tf_op jit(solution)/shard_map/ppermute | solution.py:208
  54.8 0.0 collective-permute-done.9.refs_2_
  54.8 0.0 collective-permute-done.10.refs_3_
  54.8 0.3 shard_map.80.refs_0_
  55.0 0.1 collective-permute-start.14
  55.1 3.2 %shard_map.81.refs_5_ = f32[512,2048]{1,0:T(8,128)S(1)} custom-call(bf16[256,2176]{1,0:T(8,128)(2,1)S(1)} %shard_map.80.refs_0_, bf16[16,128]{1,0:T(8,128)(2,1)S(1)} %broadcast_in_dim.13.refs_4_.refs_2_.refs_1_, bf16[512,2048]{1,0:T(8,128)(2,1)S(1)} %bitcast.9, bf16[512,2048]{1,0:T(8,128)(2,1)S(1)} %bitcast.13, bf16[256,2048]{1,0:T(8,128)(2,1)S(1)} %bitcast.17, ...), custom_call_target="tpu_custom_call" | custom-call | flops 939524096 | bytes 12582912 | tf_op jit(solution)/shard_map/pallas_call | solution.py:270
  58.4 0.0 collective-permute-done.14.refs_0_
  58.4 4.5 %shard_map.82 = f32[512,2048]{1,0:T(8,128)} custom-call(bf16[256,2176]{1,0:T(8,128)(2,1)S(1)} %collective-permute-done.14.refs_0_, bf16[16,128]{1,0:T(8,128)(2,1)S(1)} %broadcast_in_dim.13.refs_4_.refs_2_.refs_1_, bf16[512,2048]{1,0:T(8,128)(2,1)S(1)} %bitcast.10, bf16[512,2048]{1,0:T(8,128)(2,1)S(1)} %bitcast.14, bf16[256,2048]{1,0:T(8,128)(2,1)S(1)} %bitcast.18, ...), custom_call_target="tpu_custom_call" | custom-call | flops 939524096 | bytes 12582912 | tf_op jit(solution)/shard_map/pallas_call | solution.py:270
  (3 shorter events, 0.0 us)
Async XLA Ops:
  1.7 12.9 %collective-permute-start.1 = (bf16[64,2176]{1,0:T(8,128)(2,1)}, bf16[64,2176]{1,0:T(8,128)(2,1)S(1)}, u32[]{:S(2)}, u32[]{:S(2)}) collective-permute-start(bf16[64,2176]{1,0:T(8,128)(2,1)} %shard_map.73.refs_0_), channel_id=1, source_target_pairs={{0,12},{1,13},{2,14},{3,15},{4,8},{5,9},{6,10},{7,11},{8,4},{9,5},... | collective-permute-start | bytes 835592 | tf_op jit(solution)/shard_map/ppermute | solution.py:208
  6.9 10.7 %collective-permute-start.2 = (bf16[64,2176]{1,0:T(8,128)(2,1)}, bf16[64,2176]{1,0:T(8,128)(2,1)S(1)}, u32[]{:S(2)}, u32[]{:S(2)}) collective-permute-start(bf16[64,2176]{1,0:T(8,128)(2,1)} %shard_map.73.refs_0_), channel_id=1, source_target_pairs={{0,18},{1,19},{2,16},{3,17},{4,22},{5,23},{6,20},{7,21},{8,26},{9,... | collective-permute-start | bytes 835592 | tf_op jit(solution)/shard_map/ppermute | solution.py:208
  9.3 10.5 %collective-permute-start = (bf16[64,2176]{1,0:T(8,128)(2,1)}, bf16[64,2176]{1,0:T(8,128)(2,1)S(1)}, u32[]{:S(2)}, u32[]{:S(2)}) collective-permute-start(bf16[64,2176]{1,0:T(8,128)(2,1)} %shard_map.73.refs_0_), channel_id=1, source_target_pairs={{0,4},{1,5},{2,6},{3,7},{4,0},{5,1},{6,2},{7,3},{8,12},{9,13},{10,... | collective-permute-start | bytes 835592 | tf_op jit(solution)/shard_map/ppermute | solution.py:208
  9.3 14.9 %collective-permute-start.5 = (bf16[64,2176]{1,0:T(8,128)(2,1)}, bf16[64,2176]{1,0:T(8,128)(2,1)S(1)}, u32[]{:S(2)}, u32[]{:S(2)}) collective-permute-start(bf16[64,2176]{1,0:T(8,128)(2,1)} %shard_map.73.refs_0_), channel_id=1, source_target_pairs={{0,16},{1,17},{2,18},{3,19},{4,20},{5,21},{6,22},{7,23},{8,24},{9,... | collective-permute-start | bytes 835592 | tf_op jit(solution)/shard_map/ppermute | solution.py:208
  9.8 14.4 %collective-permute-start.4 = (bf16[64,2176]{1,0:T(8,128)(2,1)}, bf16[64,2176]{1,0:T(8,128)(2,1)S(1)}, u32[]{:S(2)}, u32[]{:S(2)}) collective-permute-start(bf16[64,2176]{1,0:T(8,128)(2,1)} %shard_map.73.refs_0_), channel_id=1, source_target_pairs={{0,2},{1,3},{2,0},{3,1},{4,6},{5,7},{6,4},{7,5},{8,10},{9,11},{10,... | collective-permute-start | bytes 835592 | tf_op jit(solution)/shard_map/ppermute | solution.py:208
  10.4 1.0 %copy-start.6 = (bf16[64,2176]{1,0:T(8,128)(2,1)S(1)}, bf16[64,2176]{1,0:T(8,128)(2,1)}, u32[]{:S(2)}) copy-start(bf16[64,2176]{1,0:T(8,128)(2,1)} %shard_map.73.refs_0_) | copy-start | bytes 835588
  19.9 14.4 %collective-permute-start.3 = (bf16[128,2176]{1,0:T(8,128)(2,1)S(1)}, bf16[128,2176]{1,0:T(8,128)(2,1)S(1)}, u32[]{:S(2)}, u32[]{:S(2)}) collective-permute-start(bf16[128,2176]{1,0:T(8,128)(2,1)S(1)} %get-tuple-element.24), channel_id=1, source_target_pairs={{4,8},{5,9},{6,10},{7,11},{8,4},{9,5},{10,6},{11,7},{20,24},{21,25... | collective-permute-start | bytes 1671176 | tf_op jit(solution)/shard_map/ppermute | solution.py:208
  20.6 16.1 %collective-permute-start.6 = (bf16[128,2176]{1,0:T(8,128)(2,1)S(1)}, bf16[128,2176]{1,0:T(8,128)(2,1)S(1)}, u32[]{:S(2)}, u32[]{:S(2)}) collective-permute-start(bf16[128,2176]{1,0:T(8,128)(2,1)S(1)} %get-tuple-element.27), channel_id=1, source_target_pairs={{0,4},{1,5},{2,6},{3,7},{4,0},{5,1},{6,2},{7,3},{8,12},{9,13},{10,... | collective-permute-start | bytes 1671176 | tf_op jit(solution)/shard_map/ppermute | solution.py:208
  24.2 14.0 %collective-permute-start.12 = (bf16[128,2176]{1,0:T(8,128)(2,1)S(1)}, bf16[128,2176]{1,0:T(8,128)(2,1)S(1)}, u32[]{:S(2)}, u32[]{:S(2)}) collective-permute-start(bf16[128,2176]{1,0:T(8,128)(2,1)S(1)} %get-tuple-element.33.refs_4_), channel_id=1, source_target_pairs={{0,16},{1,17},{2,18},{3,19},{4,20},{5,21},{6,22},{7,23},{8,24},{9,... | collective-permute-start | bytes 1671176 | tf_op jit(solution)/shard_map/ppermute | solution.py:208
  25.1 13.1 %collective-permute-start.11 = (bf16[128,2176]{1,0:T(8,128)(2,1)S(1)}, bf16[128,2176]{1,0:T(8,128)(2,1)S(1)}, u32[]{:S(2)}, u32[]{:S(2)}) collective-permute-start(bf16[128,2176]{1,0:T(8,128)(2,1)S(1)} %get-tuple-element.33.refs_4_), channel_id=1, source_target_pairs={{0,2},{1,3},{2,0},{3,1},{4,6},{5,7},{6,4},{7,5},{8,10},{9,11},{10,... | collective-permute-start | bytes 1671176 | tf_op jit(solution)/shard_map/ppermute | solution.py:208
  26.6 1.6 %copy-start = (bf16[1,2,256,2048]{3,2,1,0:T(8,128)(2,1)S(1)}, bf16[1,2,256,2048]{3,2,1,0:T(8,128)(2,1)}, u32[]{:S(2)}) copy-start(bf16[1,2,256,2048]{3,2,1,0:T(8,128)(2,1)} %param.11) | copy-start | bytes 6291460
  28.2 1.6 %copy-start.2 = (bf16[1,2,256,2048]{3,2,1,0:T(8,128)(2,1)S(1)}, bf16[1,2,256,2048]{3,2,1,0:T(8,128)(2,1)}, u32[]{:S(2)}) copy-start(bf16[1,2,256,2048]{3,2,1,0:T(8,128)(2,1)} %param.13) | copy-start | bytes 6291460
  29.8 1.2 %copy-start.4 = (bf16[1,256,2048]{2,1,0:T(8,128)(2,1)S(1)}, bf16[1,256,2048]{2,1,0:T(8,128)(2,1)}, u32[]{:S(2)}) copy-start(bf16[1,256,2048]{2,1,0:T(8,128)(2,1)} %param.12) | copy-start | bytes 3145732
  38.3 6.2 %copy-start.1 = (bf16[1,2,256,2048]{3,2,1,0:T(8,128)(2,1)S(1)}, bf16[1,2,256,2048]{3,2,1,0:T(8,128)(2,1)}, u32[]{:S(2)}) copy-start(bf16[1,2,256,2048]{3,2,1,0:T(8,128)(2,1)} %param.11) | copy-start | bytes 6291460
  38.3 6.2 %copy-start.3 = (bf16[1,2,256,2048]{3,2,1,0:T(8,128)(2,1)S(1)}, bf16[1,2,256,2048]{3,2,1,0:T(8,128)(2,1)}, u32[]{:S(2)}) copy-start(bf16[1,2,256,2048]{3,2,1,0:T(8,128)(2,1)} %param.13) | copy-start | bytes 6291460
  38.3 6.2 %copy-start.5 = (bf16[1,256,2048]{2,1,0:T(8,128)(2,1)S(1)}, bf16[1,256,2048]{2,1,0:T(8,128)(2,1)}, u32[]{:S(2)}) copy-start(bf16[1,256,2048]{2,1,0:T(8,128)(2,1)} %param.12) | copy-start | bytes 3145732
  38.5 6.0 %collective-permute-start.13 = (bf16[768,2176]{1,0:T(8,128)(2,1)S(1)}, bf16[768,2176]{1,0:T(8,128)(2,1)S(1)}, u32[]{:S(2)}, u32[]{:S(2)}) collective-permute-start(bf16[768,2176]{1,0:T(8,128)(2,1)S(1)} %shard_map.78.refs_0_), channel_id=1, source_target_pairs={{0,1},{1,0},{2,3},{3,2},{4,5},{5,4},{6,7},{7,6},{8,9},{9,8},{10,11... | collective-permute-start | bytes 10027016 | tf_op jit(solution)/shard_map/ppermute | solution.py:208
  38.6 13.4 %collective-permute-start.7 = (bf16[64,2176]{1,0:T(8,128)(2,1)S(1)}, bf16[64,2176]{1,0:T(8,128)(2,1)S(1)}, u32[]{:S(2)}, u32[]{:S(2)}) collective-permute-start(bf16[64,2176]{1,0:T(8,128)(2,1)S(1)} %get-tuple-element.28), channel_id=1, source_target_pairs={{0,18},{1,19},{2,16},{3,17},{4,22},{5,23},{6,20},{7,21},{8,26},{9,... | collective-permute-start | bytes 835592 | tf_op jit(solution)/shard_map/ppermute | solution.py:208
  40.0 14.7 %collective-permute-start.8 = (bf16[64,2176]{1,0:T(8,128)(2,1)S(1)}, bf16[64,2176]{1,0:T(8,128)(2,1)S(1)}, u32[]{:S(2)}, u32[]{:S(2)}) collective-permute-start(bf16[64,2176]{1,0:T(8,128)(2,1)S(1)} %get-tuple-element.29), channel_id=1, source_target_pairs={{0,2},{1,3},{2,0},{3,1},{4,6},{5,7},{6,4},{7,5},{8,10},{9,11},{10,... | collective-permute-start | bytes 835592 | tf_op jit(solution)/shard_map/ppermute | solution.py:208
  41.8 13.0 %collective-permute-start.9 = (bf16[64,2176]{1,0:T(8,128)(2,1)S(1)}, bf16[64,2176]{1,0:T(8,128)(2,1)S(1)}, u32[]{:S(2)}, u32[]{:S(2)}) collective-permute-start(bf16[64,2176]{1,0:T(8,128)(2,1)S(1)} %get-tuple-element.30), channel_id=1, source_target_pairs={{0,16},{1,17},{2,18},{3,19},{4,20},{5,21},{6,22},{7,23},{8,24},{9,... | collective-permute-start | bytes 835592 | tf_op jit(solution)/shard_map/ppermute | solution.py:208
  42.1 12.6 %collective-permute-start.10 = (bf16[64,2176]{1,0:T(8,128)(2,1)S(1)}, bf16[64,2176]{1,0:T(8,128)(2,1)S(1)}, u32[]{:S(2)}, u32[]{:S(2)}) collective-permute-start(bf16[64,2176]{1,0:T(8,128)(2,1)S(1)} %get-tuple-element.31), channel_id=1, source_target_pairs={{4,0},{5,1},{6,2},{7,3},{8,12},{9,13},{10,14},{11,15},{20,16},{21,... | collective-permute-start | bytes 835592 | tf_op jit(solution)/shard_map/ppermute | solution.py:208
  55.0 3.3 %collective-permute-start.14 = (bf16[256,2176]{1,0:T(8,128)(2,1)S(1)}, bf16[256,2176]{1,0:T(8,128)(2,1)S(1)}, u32[]{:S(2)}, u32[]{:S(2)}) collective-permute-start(bf16[256,2176]{1,0:T(8,128)(2,1)S(1)} %shard_map.80.refs_0_), channel_id=1, source_target_pairs={{0,1},{1,0},{2,3},{3,2},{4,5},{5,4},{6,7},{7,6},{8,9},{9,8},{10,11... | collective-permute-start | bytes 3342344 | tf_op jit(solution)/shard_map/ppermute | solution.py:208

commit v5 on v3

--- a/solution.py
+++ b/solution.py
@@ -300,28 +300,29 @@
         return (n, first * block, count * block)
 
     order = (Z_NEAR ^ Z_FAR, X ^ Y, X, Y, Z_NEAR)
-    middle, across, beside_x, beside_y, near = (swap(own, m) for m in order)
-
-    through, outward, pair = stack(
+    middle, across, beside_x, beside_y, near = tied([swap(own, m) for m in order])
+
+    ready = stack(
         [near, middle, across],
+        *[[rows_of(0), rows_of(1)]] * 3,
         [rows_of(0), rows_of(2)],
         [rows_of(1), rows_of(2)],
-        [rows_of(0), rows_of(1)],
-    )
+    )
+    pair, pair_x, pair_y, through, outward = ready
+    pair_x, pair_y = swap(pair_x, X), swap(pair_y, Y)
     through = swap(through, Z_NEAR ^ Z_FAR, inner)
     outward = swap(outward, Z_NEAR)
-    pair_x, pair_y = swap(pair, X), swap(after(pair, beside_x, beside_y), Y)
-
-    (held,) = stack([after(own, pair)], [rows_of(0)])
-    through, held = tied([through, held])
-
-    beyond, far, relayed = stack(
+
+    (held,) = stack([after(own, near)], [rows_of(0)])
+    pair_x, pair_y, through, outward, held = tied([pair_x, pair_y, through, outward, held])
+
+    beyond, far_x, far_y, far, relayed = stack(
         [through, outward, middle],
         [(rows_of(0), rows_of(2))],
-        [(rows_of(0), rows_of(1))],
+        *[[(rows_of(0), rows_of(1))]] * 3,
         [rows_of(0, 1)],
     )
-    third = [swap(beyond, X ^ Y), swap(far, X), swap(far, Y), swap(relayed, Z_NEAR, inner)]
+    third = [swap(beyond, X ^ Y), swap(far_x, X), swap(far_y, Y), swap(relayed, Z_NEAR, inner)]
     (stack_a,) = stack(
         [held, beside_x, beside_y, across, pair, pair_x, pair_y, far, outward],
         [rows_of(n) for n in range(4)]

time: 62.4 us -> 64.7 us (1.037)
  starting transfers between devices: 20.3 us -> 23.7 us
  waiting for transfers between devices: 26.6 us -> 25.3 us
    ppermute x15, starting transfers between devices: 20.3 us -> 23.7 us  [swap(): return lax.ppermute(value, axes, pairs)]
    ppermute x15, waiting for transfers between devices: 26.6 us -> 25.3 us  [swap(): return lax.ppermute(value, axes, pairs)]
  transfers between devices with their start and end apart: 15 -> 15, of which waited for: 9 -> 11; matrix products, arithmetic and copies ran while one was open for 0% -> 0% of each run, Pallas kernels for 12% -> 12%
where the time goes in v5:
time: 64.7 us; the launch traced here: 64.5 us
  waiting for transfers between devices  25.3 us (39%)
  starting transfers between devices  23.7 us (37%)
  Pallas kernels  14.4 us (22%)
  local copies, waits for them, and re-layouts  0.98 us (2%)
    ppermute x15, waiting for transfers between devices, swap(): return lax.ppermute(value, axes, pairs)  25.3 us
    ppermute x15, starting transfers between devices, swap(): return lax.ppermute(value, axes, pairs)  23.7 us
    pallas_call x2, Pallas kernels, call(): pl.pallas_call(functools.partial(kernel, tok_dev=tok_dev), in_specs=[insi...  12 us
    pallas_call x1, Pallas kernels, dense(): pl.pallas_call(functools.partial(pack_kernel, experts=experts), in_specs=...  1.74 us
  transfers between devices with their start and end apart: 15, of which 11 were waited for; matrix products, arithmetic and copies ran while one was open for 0% of the time, Pallas kernels for 12%

profile of v5, /device:TPU:0, one launch (start us, length us, event | category | flops | bytes accessed | tf_op | source)
XLA Modules:
  0.0 64.5 jit_solution(5289348736229188223)
XLA Ops:
  0.0 1.7 %shard_map.73.refs_0_ = bf16[64,2176]{1,0:T(8,128)(2,1)} custom-call(bf16[32,2048]{1,0:T(8,128)(2,1)} %tok_hbm.1, bf16[32,2048]{1,0:T(8,128)(2,1)} %cot_hbm.1, s32[8,32]{1,0:T(8,128)} %bitcast.13, f32[8,32]{1,0:T(8,128)} %bitcast.14), custom_call_target="tpu_custom_call" | custom-call | tf_op jit(solution)/shard_map/pallas_call | solution.py:234
  1.7 3.1 %collective-permute-start.4 = (bf16[64,2176]{1,0:T(8,128)(2,1)}, bf16[64,2176]{1,0:T(8,128)(2,1)S(1)}, u32[]{:S(2)}, u32[]{:S(2)}) collective-permute-start(bf16[64,2176]{1,0:T(8,128)(2,1)} %shard_map.73.refs_0_), channel_id=1, source_target_pairs={{0,4},{1,5},{2,6},{3,7},{4,0},{5,1},{6,2},{7,3},{8,12},{9,13},{10,... | collective-permute-start | bytes 835592 | tf_op jit(solution)/shard_map/ppermute | solution.py:213
  4.8 1.5 %collective-permute-start.3 = (bf16[64,2176]{1,0:T(8,128)(2,1)}, bf16[64,2176]{1,0:T(8,128)(2,1)S(1)}, u32[]{:S(2)}, u32[]{:S(2)}) collective-permute-start(bf16[64,2176]{1,0:T(8,128)(2,1)} %shard_map.73.refs_0_), channel_id=1, source_target_pairs={{0,16},{1,17},{2,18},{3,19},{4,20},{5,21},{6,22},{7,23},{8,24},{9,... | collective-permute-start | bytes 835592 | tf_op jit(solution)/shard_map/ppermute | solution.py:213
  6.4 1.5 %collective-permute-start.2 = (bf16[64,2176]{1,0:T(8,128)(2,1)}, bf16[64,2176]{1,0:T(8,128)(2,1)S(1)}, u32[]{:S(2)}, u32[]{:S(2)}) collective-permute-start(bf16[64,2176]{1,0:T(8,128)(2,1)} %shard_map.73.refs_0_), channel_id=1, source_target_pairs={{0,2},{1,3},{2,0},{3,1},{4,6},{5,7},{6,4},{7,5},{8,10},{9,11},{10,... | collective-permute-start | bytes 835592 | tf_op jit(solution)/shard_map/ppermute | solution.py:213
  7.8 0.5 collective-permute-start.1
  8.3 2.5 %collective-permute-start = (bf16[64,2176]{1,0:T(8,128)(2,1)}, bf16[64,2176]{1,0:T(8,128)(2,1)S(1)}, u32[]{:S(2)}, u32[]{:S(2)}) collective-permute-start(bf16[64,2176]{1,0:T(8,128)(2,1)} %shard_map.73.refs_0_), channel_id=1, source_target_pairs={{0,12},{1,13},{2,14},{3,15},{4,8},{5,9},{6,10},{7,11},{8,4},{9,5},... | collective-permute-start | bytes 835592 | tf_op jit(solution)/shard_map/ppermute | solution.py:213
  10.8 1.3 %collective-permute-done.4.refs_0_ = bf16[64,2176]{1,0:T(8,128)(2,1)S(1)} collective-permute-done((bf16[64,2176]{1,0:T(8,128)(2,1)}, bf16[64,2176]{1,0:T(8,128)(2,1)S(1)}, u32[]{:S(2)}, u32[]{:S(2)}) %collective-permute-start.4) | collective-permute-done | bytes 278560 | tf_op jit(solution)/shard_map/ppermute | solution.py:213
  12.1 1.6 %collective-permute-done.3.refs_2_ = bf16[64,2176]{1,0:T(8,128)(2,1)S(1)} collective-permute-done((bf16[64,2176]{1,0:T(8,128)(2,1)}, bf16[64,2176]{1,0:T(8,128)(2,1)S(1)}, u32[]{:S(2)}, u32[]{:S(2)}) %collective-permute-start.3) | collective-permute-done | bytes 278560 | tf_op jit(solution)/shard_map/ppermute | solution.py:213
  13.7 2.4 %collective-permute-done.2.refs_1_ = bf16[64,2176]{1,0:T(8,128)(2,1)S(1)} collective-permute-done((bf16[64,2176]{1,0:T(8,128)(2,1)}, bf16[64,2176]{1,0:T(8,128)(2,1)S(1)}, u32[]{:S(2)}, u32[]{:S(2)}) %collective-permute-start.2) | collective-permute-done | bytes 278560 | tf_op jit(solution)/shard_map/ppermute | solution.py:213
  16.2 4.2 %collective-permute-done.1.refs_2_.refs_3_ = bf16[64,2176]{1,0:T(8,128)(2,1)S(1)} collective-permute-done((bf16[64,2176]{1,0:T(8,128)(2,1)}, bf16[64,2176]{1,0:T(8,128)(2,1)S(1)}, u32[]{:S(2)}, u32[]{:S(2)}) %collective-permute-start.1) | collective-permute-done | bytes 278560 | tf_op jit(solution)/shard_map/ppermute | solution.py:213
  20.3 0.0 collective-permute-done.refs_1_.refs_2_
  20.3 0.2 shard_map.74
  20.5 1.6 %collective-permute-start.5 = (bf16[128,2176]{1,0:T(8,128)(2,1)S(1)}, bf16[128,2176]{1,0:T(8,128)(2,1)S(1)}, u32[]{:S(2)}, u32[]{:S(2)}) collective-permute-start(bf16[128,2176]{1,0:T(8,128)(2,1)S(1)} %get-tuple-element.34), channel_id=1, source_target_pairs={{0,2},{1,3},{2,0},{3,1},{4,6},{5,7},{6,4},{7,5},{8,10},{9,11},{10,... | collective-permute-start | bytes 1671176 | tf_op jit(solution)/shard_map/ppermute | solution.py:213
  22.1 1.5 %collective-permute-start.6 = (bf16[128,2176]{1,0:T(8,128)(2,1)S(1)}, bf16[128,2176]{1,0:T(8,128)(2,1)S(1)}, u32[]{:S(2)}, u32[]{:S(2)}) collective-permute-start(bf16[128,2176]{1,0:T(8,128)(2,1)S(1)} %get-tuple-element.35), channel_id=1, source_target_pairs={{0,16},{1,17},{2,18},{3,19},{4,20},{5,21},{6,22},{7,23},{8,24},{9,... | collective-permute-start | bytes 1671176 | tf_op jit(solution)/shard_map/ppermute | solution.py:213
  23.6 0.7 %collective-permute-start.7 = (bf16[128,2176]{1,0:T(8,128)(2,1)S(1)}, bf16[128,2176]{1,0:T(8,128)(2,1)S(1)}, u32[]{:S(2)}, u32[]{:S(2)}) collective-permute-start(bf16[128,2176]{1,0:T(8,128)(2,1)S(1)} %get-tuple-element.36), channel_id=1, source_target_pairs={{4,8},{5,9},{6,10},{7,11},{8,4},{9,5},{10,6},{11,7},{20,24},{21,25... | collective-permute-start | bytes 1671176 | tf_op jit(solution)/shard_map/ppermute | solution.py:213
  24.3 5.9 %collective-permute-start.8 = (bf16[128,2176]{1,0:T(8,128)(2,1)S(1)}, bf16[128,2176]{1,0:T(8,128)(2,1)S(1)}, u32[]{:S(2)}, u32[]{:S(2)}) collective-permute-start(bf16[128,2176]{1,0:T(8,128)(2,1)S(1)} %get-tuple-element.37), channel_id=1, source_target_pairs={{0,4},{1,5},{2,6},{3,7},{4,0},{5,1},{6,2},{7,3},{8,12},{9,13},{10,... | collective-permute-start | bytes 1671176 | tf_op jit(solution)/shard_map/ppermute | solution.py:213
  30.2 0.0 copy-start.2
  30.2 1.0 %copy-done.2 = bf16[64,2176]{1,0:T(8,128)(2,1)S(1)} copy-done((bf16[64,2176]{1,0:T(8,128)(2,1)S(1)}, bf16[64,2176]{1,0:T(8,128)(2,1)}, u32[]{:S(2)}) %copy-start.2) | copy-done | bytes 278552
  31.2 2.5 %collective-permute-done.5.refs_5_ = bf16[128,2176]{1,0:T(8,128)(2,1)S(1)} collective-permute-done((bf16[128,2176]{1,0:T(8,128)(2,1)S(1)}, bf16[128,2176]{1,0:T(8,128)(2,1)S(1)}, u32[]{:S(2)}, u32[]{:S(2)}) %collective-permute-start.5) | collective-permute-done | bytes 557088 | tf_op jit(solution)/shard_map/ppermute | solution.py:213
  33.7 1.2 %collective-permute-done.6.refs_6_ = bf16[128,2176]{1,0:T(8,128)(2,1)S(1)} collective-permute-done((bf16[128,2176]{1,0:T(8,128)(2,1)S(1)}, bf16[128,2176]{1,0:T(8,128)(2,1)S(1)}, u32[]{:S(2)}, u32[]{:S(2)}) %collective-permute-start.6) | collective-permute-done | bytes 557088 | tf_op jit(solution)/shard_map/ppermute | solution.py:213
  34.9 0.0 collective-permute-done.7.refs_0_.refs_4_
  34.9 5.7 %collective-permute-done.8.refs_1_.refs_8_ = bf16[128,2176]{1,0:T(8,128)(2,1)S(1)} collective-permute-done((bf16[128,2176]{1,0:T(8,128)(2,1)S(1)}, bf16[128,2176]{1,0:T(8,128)(2,1)S(1)}, u32[]{:S(2)}, u32[]{:S(2)}) %collective-permute-start.8) | collective-permute-done | bytes 557088 | tf_op jit(solution)/shard_map/ppermute | solution.py:213
  40.6 0.1 shard_map.76
  40.8 0.0 copy-start
  40.8 0.0 copy-start.1
  40.8 0.0 copy-start.3
  40.8 0.2 shard_map.77.mine
  41.0 0.1 collective-permute-start.13
  41.1 0.5 collective-permute-start.9
  41.7 1.5 %collective-permute-start.10 = (bf16[64,2176]{1,0:T(8,128)(2,1)S(1)}, bf16[64,2176]{1,0:T(8,128)(2,1)S(1)}, u32[]{:S(2)}, u32[]{:S(2)}) collective-permute-start(bf16[64,2176]{1,0:T(8,128)(2,1)S(1)} %get-tuple-element.42), channel_id=1, source_target_pairs={{0,2},{1,3},{2,0},{3,1},{4,6},{5,7},{6,4},{7,5},{8,10},{9,11},{10,... | collective-permute-start | bytes 835592 | tf_op jit(solution)/shard_map/ppermute | solution.py:213
  43.2 1.5 %collective-permute-start.11 = (bf16[64,2176]{1,0:T(8,128)(2,1)S(1)}, bf16[64,2176]{1,0:T(8,128)(2,1)S(1)}, u32[]{:S(2)}, u32[]{:S(2)}) collective-permute-start(bf16[64,2176]{1,0:T(8,128)(2,1)S(1)} %get-tuple-element.43), channel_id=1, source_target_pairs={{0,16},{1,17},{2,18},{3,19},{4,20},{5,21},{6,22},{7,23},{8,24},{9,... | collective-permute-start | bytes 835592 | tf_op jit(solution)/shard_map/ppermute | solution.py:213
  44.7 1.3 %collective-permute-start.12 = (bf16[64,2176]{1,0:T(8,128)(2,1)S(1)}, bf16[64,2176]{1,0:T(8,128)(2,1)S(1)}, u32[]{:S(2)}, u32[]{:S(2)}) collective-permute-start(bf16[64,2176]{1,0:T(8,128)(2,1)S(1)} %get-tuple-element.44), channel_id=1, source_target_pairs={{4,0},{5,1},{6,2},{7,3},{8,12},{9,13},{10,14},{11,15},{20,16},{21,... | collective-permute-start | bytes 835592 | tf_op jit(solution)/shard_map/ppermute | solution.py:213
  46.0 1.1 %collective-permute-done.13.theirs = bf16[768,2176]{1,0:T(8,128)(2,1)S(1)} collective-permute-done((bf16[768,2176]{1,0:T(8,128)(2,1)S(1)}, bf16[768,2176]{1,0:T(8,128)(2,1)S(1)}, u32[]{:S(2)}, u32[]{:S(2)}) %collective-permute-start.13) | collective-permute-done | bytes 3342368 | tf_op jit(solution)/shard_map/ppermute | solution.py:213
  47.0 0.0 copy-done
  47.0 0.0 copy-done.1
  47.1 0.0 copy-done.3
  47.1 7.5 %shard_map.78.add_ref = f32[512,2048]{1,0:T(8,128)S(1)} custom-call(bf16[768,2176]{1,0:T(8,128)(2,1)S(1)} %shard_map.77.mine, bf16[768,2176]{1,0:T(8,128)(2,1)S(1)} %collective-permute-done.13.theirs, bf16[16,128]{1,0:T(8,128)(2,1)S(1)} %broadcast_in_dim.13.pick_ref, bf16[512,2048]{1,0:T(8,128)(2,1)S(1)} %bitcast.7, bf16[512,2048]{1,0:T(8,128)(2,1)S(1)} %bitcast.9, ...), custom_call_target="tpu_custom_call" | custom-call | flops 5637144576 | bytes 12582912 | tf_op jit(solution)/shard_map/pallas_call | solution.py:261
  54.5 0.0 collective-permute-done.9.refs_0_
  54.5 1.6 %collective-permute-done.10.refs_1_ = bf16[64,2176]{1,0:T(8,128)(2,1)S(1)} collective-permute-done((bf16[64,2176]{1,0:T(8,128)(2,1)S(1)}, bf16[64,2176]{1,0:T(8,128)(2,1)S(1)}, u32[]{:S(2)}, u32[]{:S(2)}) %collective-permute-start.10) | collective-permute-done | bytes 278560 | tf_op jit(solution)/shard_map/ppermute | solution.py:213
  56.1 0.9 %collective-permute-done.11.refs_2_ = bf16[64,2176]{1,0:T(8,128)(2,1)S(1)} collective-permute-done((bf16[64,2176]{1,0:T(8,128)(2,1)S(1)}, bf16[64,2176]{1,0:T(8,128)(2,1)S(1)}, u32[]{:S(2)}, u32[]{:S(2)}) %collective-permute-start.11) | collective-permute-done | bytes 278560 | tf_op jit(solution)/shard_map/ppermute | solution.py:213
  57.1 0.0 collective-permute-done.12.refs_3_
  57.1 0.1 shard_map.79.mine
  57.1 0.1 collective-permute-start.14
  57.2 2.7 %collective-permute-done.14.theirs = bf16[256,2176]{1,0:T(8,128)(2,1)S(1)} collective-permute-done((bf16[256,2176]{1,0:T(8,128)(2,1)S(1)}, bf16[256,2176]{1,0:T(8,128)(2,1)S(1)}, u32[]{:S(2)}, u32[]{:S(2)}) %collective-permute-start.14) | collective-permute-done | bytes 1114144 | tf_op jit(solution)/shard_map/ppermute | solution.py:213
  60.0 4.5 %shard_map.80 = f32[512,2048]{1,0:T(8,128)} custom-call(bf16[256,2176]{1,0:T(8,128)(2,1)S(1)} %shard_map.79.mine, bf16[256,2176]{1,0:T(8,128)(2,1)S(1)} %collective-permute-done.14.theirs, bf16[16,128]{1,0:T(8,128)(2,1)S(1)} %broadcast_in_dim.13.pick_ref, bf16[512,2048]{1,0:T(8,128)(2,1)S(1)} %bitcast.8, bf16[512,2048]{1,0:T(8,128)(2,1)S(1)} %bitcast.10, ...), custom_call_target="tpu_custom_call" | custom-call | flops 1879048192 | bytes 12582912 | tf_op jit(solution)/shard_map/pallas_call | solution.py:261
  (3 shorter events, 0.0 us)
Async XLA Ops:
  1.7 10.4 %collective-permute-start.4 = (bf16[64,2176]{1,0:T(8,128)(2,1)}, bf16[64,2176]{1,0:T(8,128)(2,1)S(1)}, u32[]{:S(2)}, u32[]{:S(2)}) collective-permute-start(bf16[64,2176]{1,0:T(8,128)(2,1)} %shard_map.73.refs_0_), channel_id=1, source_target_pairs={{0,4},{1,5},{2,6},{3,7},{4,0},{5,1},{6,2},{7,3},{8,12},{9,13},{10,... | collective-permute-start | bytes 835592 | tf_op jit(solution)/shard_map/ppermute | solution.py:213
  4.8 8.9 %collective-permute-start.3 = (bf16[64,2176]{1,0:T(8,128)(2,1)}, bf16[64,2176]{1,0:T(8,128)(2,1)S(1)}, u32[]{:S(2)}, u32[]{:S(2)}) collective-permute-start(bf16[64,2176]{1,0:T(8,128)(2,1)} %shard_map.73.refs_0_), channel_id=1, source_target_pairs={{0,16},{1,17},{2,18},{3,19},{4,20},{5,21},{6,22},{7,23},{8,24},{9,... | collective-permute-start | bytes 835592 | tf_op jit(solution)/shard_map/ppermute | solution.py:213
  6.4 9.8 %collective-permute-start.2 = (bf16[64,2176]{1,0:T(8,128)(2,1)}, bf16[64,2176]{1,0:T(8,128)(2,1)S(1)}, u32[]{:S(2)}, u32[]{:S(2)}) collective-permute-start(bf16[64,2176]{1,0:T(8,128)(2,1)} %shard_map.73.refs_0_), channel_id=1, source_target_pairs={{0,2},{1,3},{2,0},{3,1},{4,6},{5,7},{6,4},{7,5},{8,10},{9,11},{10,... | collective-permute-start | bytes 835592 | tf_op jit(solution)/shard_map/ppermute | solution.py:213
  7.8 12.5 %collective-permute-start.1 = (bf16[64,2176]{1,0:T(8,128)(2,1)}, bf16[64,2176]{1,0:T(8,128)(2,1)S(1)}, u32[]{:S(2)}, u32[]{:S(2)}) collective-permute-start(bf16[64,2176]{1,0:T(8,128)(2,1)} %shard_map.73.refs_0_), channel_id=1, source_target_pairs={{0,18},{1,19},{2,16},{3,17},{4,22},{5,23},{6,20},{7,21},{8,26},{9,... | collective-permute-start | bytes 835592 | tf_op jit(solution)/shard_map/ppermute | solution.py:213
  8.3 12.0 %collective-permute-start = (bf16[64,2176]{1,0:T(8,128)(2,1)}, bf16[64,2176]{1,0:T(8,128)(2,1)S(1)}, u32[]{:S(2)}, u32[]{:S(2)}) collective-permute-start(bf16[64,2176]{1,0:T(8,128)(2,1)} %shard_map.73.refs_0_), channel_id=1, source_target_pairs={{0,12},{1,13},{2,14},{3,15},{4,8},{5,9},{6,10},{7,11},{8,4},{9,5},... | collective-permute-start | bytes 835592 | tf_op jit(solution)/shard_map/ppermute | solution.py:213
  20.5 13.1 %collective-permute-start.5 = (bf16[128,2176]{1,0:T(8,128)(2,1)S(1)}, bf16[128,2176]{1,0:T(8,128)(2,1)S(1)}, u32[]{:S(2)}, u32[]{:S(2)}) collective-permute-start(bf16[128,2176]{1,0:T(8,128)(2,1)S(1)} %get-tuple-element.34), channel_id=1, source_target_pairs={{0,2},{1,3},{2,0},{3,1},{4,6},{5,7},{6,4},{7,5},{8,10},{9,11},{10,... | collective-permute-start | bytes 1671176 | tf_op jit(solution)/shard_map/ppermute | solution.py:213
  22.1 12.8 %collective-permute-start.6 = (bf16[128,2176]{1,0:T(8,128)(2,1)S(1)}, bf16[128,2176]{1,0:T(8,128)(2,1)S(1)}, u32[]{:S(2)}, u32[]{:S(2)}) collective-permute-start(bf16[128,2176]{1,0:T(8,128)(2,1)S(1)} %get-tuple-element.35), channel_id=1, source_target_pairs={{0,16},{1,17},{2,18},{3,19},{4,20},{5,21},{6,22},{7,23},{8,24},{9,... | collective-permute-start | bytes 1671176 | tf_op jit(solution)/shard_map/ppermute | solution.py:213
  23.6 11.3 %collective-permute-start.7 = (bf16[128,2176]{1,0:T(8,128)(2,1)S(1)}, bf16[128,2176]{1,0:T(8,128)(2,1)S(1)}, u32[]{:S(2)}, u32[]{:S(2)}) collective-permute-start(bf16[128,2176]{1,0:T(8,128)(2,1)S(1)} %get-tuple-element.36), channel_id=1, source_target_pairs={{4,8},{5,9},{6,10},{7,11},{8,4},{9,5},{10,6},{11,7},{20,24},{21,25... | collective-permute-start | bytes 1671176 | tf_op jit(solution)/shard_map/ppermute | solution.py:213
  24.3 16.3 %collective-permute-start.8 = (bf16[128,2176]{1,0:T(8,128)(2,1)S(1)}, bf16[128,2176]{1,0:T(8,128)(2,1)S(1)}, u32[]{:S(2)}, u32[]{:S(2)}) collective-permute-start(bf16[128,2176]{1,0:T(8,128)(2,1)S(1)} %get-tuple-element.37), channel_id=1, source_target_pairs={{0,4},{1,5},{2,6},{3,7},{4,0},{5,1},{6,2},{7,3},{8,12},{9,13},{10,... | collective-permute-start | bytes 1671176 | tf_op jit(solution)/shard_map/ppermute | solution.py:213
  30.2 1.0 %copy-start.2 = (bf16[64,2176]{1,0:T(8,128)(2,1)S(1)}, bf16[64,2176]{1,0:T(8,128)(2,1)}, u32[]{:S(2)}) copy-start(bf16[64,2176]{1,0:T(8,128)(2,1)} %shard_map.73.refs_0_) | copy-start | bytes 835588
  40.8 6.3 %copy-start = (bf16[1,2,256,2048]{3,2,1,0:T(8,128)(2,1)S(1)}, bf16[1,2,256,2048]{3,2,1,0:T(8,128)(2,1)}, u32[]{:S(2)}) copy-start(bf16[1,2,256,2048]{3,2,1,0:T(8,128)(2,1)} %param.11) | copy-start | bytes 6291460
  40.8 6.3 %copy-start.1 = (bf16[1,2,256,2048]{3,2,1,0:T(8,128)(2,1)S(1)}, bf16[1,2,256,2048]{3,2,1,0:T(8,128)(2,1)}, u32[]{:S(2)}) copy-start(bf16[1,2,256,2048]{3,2,1,0:T(8,128)(2,1)} %param.13) | copy-start | bytes 6291460
  40.8 6.3 %copy-start.3 = (bf16[1,256,2048]{2,1,0:T(8,128)(2,1)S(1)}, bf16[1,256,2048]{2,1,0:T(8,128)(2,1)}, u32[]{:S(2)}) copy-start(bf16[1,256,2048]{2,1,0:T(8,128)(2,1)} %param.12) | copy-start | bytes 3145732
  41.0 6.0 %collective-permute-start.13 = (bf16[768,2176]{1,0:T(8,128)(2,1)S(1)}, bf16[768,2176]{1,0:T(8,128)(2,1)S(1)}, u32[]{:S(2)}, u32[]{:S(2)}) collective-permute-start(bf16[768,2176]{1,0:T(8,128)(2,1)S(1)} %shard_map.77.mine), channel_id=1, source_target_pairs={{0,1},{1,0},{2,3},{3,2},{4,5},{5,4},{6,7},{7,6},{8,9},{9,8},{10,11... | collective-permute-start | bytes 10027016 | tf_op jit(solution)/shard_map/ppermute | solution.py:213
  41.1 13.4 %collective-permute-start.9 = (bf16[64,2176]{1,0:T(8,128)(2,1)S(1)}, bf16[64,2176]{1,0:T(8,128)(2,1)S(1)}, u32[]{:S(2)}, u32[]{:S(2)}) collective-permute-start(bf16[64,2176]{1,0:T(8,128)(2,1)S(1)} %get-tuple-element.41), channel_id=1, source_target_pairs={{0,18},{1,19},{2,16},{3,17},{4,22},{5,23},{6,20},{7,21},{8,26},{9,... | collective-permute-start | bytes 835592 | tf_op jit(solution)/shard_map/ppermute | solution.py:213
  41.7 14.5 %collective-permute-start.10 = (bf16[64,2176]{1,0:T(8,128)(2,1)S(1)}, bf16[64,2176]{1,0:T(8,128)(2,1)S(1)}, u32[]{:S(2)}, u32[]{:S(2)}) collective-permute-start(bf16[64,2176]{1,0:T(8,128)(2,1)S(1)} %get-tuple-element.42), channel_id=1, source_target_pairs={{0,2},{1,3},{2,0},{3,1},{4,6},{5,7},{6,4},{7,5},{8,10},{9,11},{10,... | collective-permute-start | bytes 835592 | tf_op jit(solution)/shard_map/ppermute | solution.py:213
  43.2 13.9 %collective-permute-start.11 = (bf16[64,2176]{1,0:T(8,128)(2,1)S(1)}, bf16[64,2176]{1,0:T(8,128)(2,1)S(1)}, u32[]{:S(2)}, u32[]{:S(2)}) collective-permute-start(bf16[64,2176]{1,0:T(8,128)(2,1)S(1)} %get-tuple-element.43), channel_id=1, source_target_pairs={{0,16},{1,17},{2,18},{3,19},{4,20},{5,21},{6,22},{7,23},{8,24},{9,... | collective-permute-start | bytes 835592 | tf_op jit(solution)/shard_map/ppermute | solution.py:213
  44.7 12.4 %collective-permute-start.12 = (bf16[64,2176]{1,0:T(8,128)(2,1)S(1)}, bf16[64,2176]{1,0:T(8,128)(2,1)S(1)}, u32[]{:S(2)}, u32[]{:S(2)}) collective-permute-start(bf16[64,2176]{1,0:T(8,128)(2,1)S(1)} %get-tuple-element.44), channel_id=1, source_target_pairs={{4,0},{5,1},{6,2},{7,3},{8,12},{9,13},{10,14},{11,15},{20,16},{21,... | collective-permute-start | bytes 835592 | tf_op jit(solution)/shard_map/ppermute | solution.py:213
  57.1 2.8 %collective-permute-start.14 = (bf16[256,2176]{1,0:T(8,128)(2,1)S(1)}, bf16[256,2176]{1,0:T(8,128)(2,1)S(1)}, u32[]{:S(2)}, u32[]{:S(2)}) collective-permute-start(bf16[256,2176]{1,0:T(8,128)(2,1)S(1)} %shard_map.79.mine), channel_id=1, source_target_pairs={{0,1},{1,0},{2,3},{3,2},{4,5},{5,4},{6,7},{7,6},{8,9},{9,8},{10,11... | collective-permute-start | bytes 3342344 | tf_op jit(solution)/shard_map/ppermute | solution.py:213

commit v6 on v3

--- a/solution.py
+++ b/solution.py
@@ -315,13 +315,13 @@
     (held,) = stack([after(own, pair)], [rows_of(0)])
     through, held = tied([through, held])
 
-    beyond, far, relayed = stack(
+    beyond, far_x, far_y, far, relayed = stack(
         [through, outward, middle],
         [(rows_of(0), rows_of(2))],
-        [(rows_of(0), rows_of(1))],
+        *[[(rows_of(0), rows_of(1))]] * 3,
         [rows_of(0, 1)],
     )
-    third = [swap(beyond, X ^ Y), swap(far, X), swap(far, Y), swap(relayed, Z_NEAR, inner)]
+    third = [swap(beyond, X ^ Y), swap(far_x, X), swap(far_y, Y), swap(relayed, Z_NEAR, inner)]
     (stack_a,) = stack(
         [held, beside_x, beside_y, across, pair, pair_x, pair_y, far, outward],
         [rows_of(n) for n in range(4)]

time: 62.4 us -> 62.9 us (level)
  waiting for transfers between devices: 26.6 us -> 29.1 us
  starting transfers between devices: 20.3 us -> 18.3 us
    ppermute x15, waiting for transfers between devices: 26.6 us -> 29.1 us  [swap(): return lax.ppermute(value, axes, pairs)]
    ppermute x15, starting transfers between devices: 20.3 us -> 18.3 us  [swap(): return lax.ppermute(value, axes, pairs)]
where the time goes in v6:
time: 62.9 us; the launch traced here: 62.7 us
  waiting for transfers between devices  29.1 us (46%)
  starting transfers between devices  18.3 us (29%)
  Pallas kernels  14.3 us (23%)
  local copies, waits for them, and re-layouts  0.97 us (2%)
    ppermute x15, waiting for transfers between devices, swap(): return lax.ppermute(value, axes, pairs)  29.1 us
    ppermute x15, starting transfers between devices, swap(): return lax.ppermute(value, axes, pairs)  18.3 us
    pallas_call x2, Pallas kernels, call(): pl.pallas_call(functools.partial(kernel, tok_dev=tok_dev), in_specs=[insi...  12 us
    pallas_call x1, Pallas kernels, dense(): pl.pallas_call(functools.partial(pack_kernel, experts=experts), in_specs=...  1.74 us
  transfers between devices with their start and end apart: 15, of which 9 were waited for; matrix products, arithmetic and copies ran while one was open for 0% of the time, Pallas kernels for 12%

profile of v6, /device:TPU:0, one launch (start us, length us, event | category | flops | bytes accessed | tf_op | source)
XLA Modules:
  0.0 62.7 jit_solution(631008556144259768)
XLA Ops:
  0.0 1.7 %shard_map.73.refs_0_ = bf16[64,2176]{1,0:T(8,128)(2,1)} custom-call(bf16[32,2048]{1,0:T(8,128)(2,1)} %tok_hbm.1, bf16[32,2048]{1,0:T(8,128)(2,1)} %cot_hbm.1, s32[8,32]{1,0:T(8,128)} %bitcast.13, f32[8,32]{1,0:T(8,128)} %bitcast.14), custom_call_target="tpu_custom_call" | custom-call | tf_op jit(solution)/shard_map/pallas_call | solution.py:234
  1.7 4.0 %collective-permute-start.2 = (bf16[64,2176]{1,0:T(8,128)(2,1)}, bf16[64,2176]{1,0:T(8,128)(2,1)S(1)}, u32[]{:S(2)}, u32[]{:S(2)}) collective-permute-start(bf16[64,2176]{1,0:T(8,128)(2,1)} %shard_map.73.refs_0_), channel_id=1, source_target_pairs={{0,18},{1,19},{2,16},{3,17},{4,22},{5,23},{6,20},{7,21},{8,26},{9,... | collective-permute-start | bytes 835592 | tf_op jit(solution)/shard_map/ppermute | solution.py:213
  5.7 3.6 %collective-permute-start.1 = (bf16[64,2176]{1,0:T(8,128)(2,1)}, bf16[64,2176]{1,0:T(8,128)(2,1)S(1)}, u32[]{:S(2)}, u32[]{:S(2)}) collective-permute-start(bf16[64,2176]{1,0:T(8,128)(2,1)} %shard_map.73.refs_0_), channel_id=1, source_target_pairs={{0,12},{1,13},{2,14},{3,15},{4,8},{5,9},{6,10},{7,11},{8,4},{9,5},... | collective-permute-start | bytes 835592 | tf_op jit(solution)/shard_map/ppermute | solution.py:213
  9.3 0.0 collective-permute-start
  9.3 0.5 collective-permute-start.10
  9.8 0.5 collective-permute-start.9
  10.4 2.8 %collective-permute-done.2.refs_2_.refs_3_ = bf16[64,2176]{1,0:T(8,128)(2,1)S(1)} collective-permute-done((bf16[64,2176]{1,0:T(8,128)(2,1)}, bf16[64,2176]{1,0:T(8,128)(2,1)S(1)}, u32[]{:S(2)}, u32[]{:S(2)}) %collective-permute-start.2) | collective-permute-done | bytes 278560 | tf_op jit(solution)/shard_map/ppermute | solution.py:213
  13.1 4.2 %collective-permute-done.1.refs_1_.refs_2_ = bf16[64,2176]{1,0:T(8,128)(2,1)S(1)} collective-permute-done((bf16[64,2176]{1,0:T(8,128)(2,1)}, bf16[64,2176]{1,0:T(8,128)(2,1)S(1)}, u32[]{:S(2)}, u32[]{:S(2)}) %collective-permute-start.1) | collective-permute-done | bytes 278560 | tf_op jit(solution)/shard_map/ppermute | solution.py:213
  17.3 4.7 %collective-permute-done.refs_0_ = bf16[64,2176]{1,0:T(8,128)(2,1)S(1)} collective-permute-done((bf16[64,2176]{1,0:T(8,128)(2,1)}, bf16[64,2176]{1,0:T(8,128)(2,1)S(1)}, u32[]{:S(2)}, u32[]{:S(2)}) %collective-permute-start) | collective-permute-done | bytes 278560 | tf_op jit(solution)/shard_map/ppermute | solution.py:213
  22.0 0.1 shard_map.74
  22.1 0.7 %collective-permute-start.3 = (bf16[128,2176]{1,0:T(8,128)(2,1)S(1)}, bf16[128,2176]{1,0:T(8,128)(2,1)S(1)}, u32[]{:S(2)}, u32[]{:S(2)}) collective-permute-start(bf16[128,2176]{1,0:T(8,128)(2,1)S(1)} %get-tuple-element.22), channel_id=1, source_target_pairs={{4,8},{5,9},{6,10},{7,11},{8,4},{9,5},{10,6},{11,7},{20,24},{21,25... | collective-permute-start | bytes 1671176 | tf_op jit(solution)/shard_map/ppermute | solution.py:213
  22.8 2.9 %collective-permute-start.4 = (bf16[128,2176]{1,0:T(8,128)(2,1)S(1)}, bf16[128,2176]{1,0:T(8,128)(2,1)S(1)}, u32[]{:S(2)}, u32[]{:S(2)}) collective-permute-start(bf16[128,2176]{1,0:T(8,128)(2,1)S(1)} %get-tuple-element.26), channel_id=1, source_target_pairs={{0,4},{1,5},{2,6},{3,7},{4,0},{5,1},{6,2},{7,3},{8,12},{9,13},{10,... | collective-permute-start | bytes 1671176 | tf_op jit(solution)/shard_map/ppermute | solution.py:213
  25.8 0.0 collective-permute-done.10.refs_2_
  25.8 0.0 collective-permute-done.9.refs_1_
  25.8 0.5 collective-permute-start.12
  26.3 0.5 collective-permute-start.11
  26.8 0.0 copy-start.2
  26.8 1.0 %copy-done.2 = bf16[64,2176]{1,0:T(8,128)(2,1)S(1)} copy-done((bf16[64,2176]{1,0:T(8,128)(2,1)S(1)}, bf16[64,2176]{1,0:T(8,128)(2,1)}, u32[]{:S(2)}) %copy-start.2) | copy-done | bytes 278552
  27.8 0.0 collective-permute-done.3.refs_0_.refs_4_
  27.8 9.6 %collective-permute-done.4.refs_1_.refs_8_ = bf16[128,2176]{1,0:T(8,128)(2,1)S(1)} collective-permute-done((bf16[128,2176]{1,0:T(8,128)(2,1)S(1)}, bf16[128,2176]{1,0:T(8,128)(2,1)S(1)}, u32[]{:S(2)}, u32[]{:S(2)}) %collective-permute-start.4) | collective-permute-done | bytes 557088 | tf_op jit(solution)/shard_map/ppermute | solution.py:213
  37.4 0.1 shard_map.76
  37.6 1.1 %collective-permute-done.12.refs_6_ = bf16[128,2176]{1,0:T(8,128)(2,1)S(1)} collective-permute-done((bf16[128,2176]{1,0:T(8,128)(2,1)S(1)}, bf16[128,2176]{1,0:T(8,128)(2,1)S(1)}, u32[]{:S(2)}, u32[]{:S(2)}) %collective-permute-start.12) | collective-permute-done | bytes 557088 | tf_op jit(solution)/shard_map/ppermute | solution.py:213
  38.7 0.2 collective-permute-done.11.refs_5_
  38.9 0.0 copy-start
  38.9 0.0 copy-start.1
  38.9 0.0 copy-start.3
  38.9 0.2 shard_map.77.mine
  39.2 0.1 collective-permute-start.13
  39.3 1.6 %collective-permute-start.5 = (bf16[64,2176]{1,0:T(8,128)(2,1)S(1)}, bf16[64,2176]{1,0:T(8,128)(2,1)S(1)}, u32[]{:S(2)}, u32[]{:S(2)}) collective-permute-start(bf16[64,2176]{1,0:T(8,128)(2,1)S(1)} %get-tuple-element.27), channel_id=1, source_target_pairs={{0,18},{1,19},{2,16},{3,17},{4,22},{5,23},{6,20},{7,21},{8,26},{9,... | collective-permute-start | bytes 835592 | tf_op jit(solution)/shard_map/ppermute | solution.py:213
  40.8 1.5 %collective-permute-start.6 = (bf16[64,2176]{1,0:T(8,128)(2,1)S(1)}, bf16[64,2176]{1,0:T(8,128)(2,1)S(1)}, u32[]{:S(2)}, u32[]{:S(2)}) collective-permute-start(bf16[64,2176]{1,0:T(8,128)(2,1)S(1)} %get-tuple-element.28), channel_id=1, source_target_pairs={{0,2},{1,3},{2,0},{3,1},{4,6},{5,7},{6,4},{7,5},{8,10},{9,11},{10,... | collective-permute-start | bytes 835592 | tf_op jit(solution)/shard_map/ppermute | solution.py:213
  42.3 0.5 collective-permute-start.7
  42.8 1.3 %collective-permute-start.8 = (bf16[64,2176]{1,0:T(8,128)(2,1)S(1)}, bf16[64,2176]{1,0:T(8,128)(2,1)S(1)}, u32[]{:S(2)}, u32[]{:S(2)}) collective-permute-start(bf16[64,2176]{1,0:T(8,128)(2,1)S(1)} %get-tuple-element.30), channel_id=1, source_target_pairs={{4,0},{5,1},{6,2},{7,3},{8,12},{9,13},{10,14},{11,15},{20,16},{21,... | collective-permute-start | bytes 835592 | tf_op jit(solution)/shard_map/ppermute | solution.py:213
  44.1 1.1 %collective-permute-done.13.theirs = bf16[768,2176]{1,0:T(8,128)(2,1)S(1)} collective-permute-done((bf16[768,2176]{1,0:T(8,128)(2,1)S(1)}, bf16[768,2176]{1,0:T(8,128)(2,1)S(1)}, u32[]{:S(2)}, u32[]{:S(2)}) %collective-permute-start.13) | collective-permute-done | bytes 3342368 | tf_op jit(solution)/shard_map/ppermute | solution.py:213
  45.2 0.0 copy-done
  45.2 0.0 copy-done.1
  45.2 0.0 copy-done.3
  45.2 7.5 %shard_map.78.add_ref = f32[512,2048]{1,0:T(8,128)S(1)} custom-call(bf16[768,2176]{1,0:T(8,128)(2,1)S(1)} %shard_map.77.mine, bf16[768,2176]{1,0:T(8,128)(2,1)S(1)} %collective-permute-done.13.theirs, bf16[16,128]{1,0:T(8,128)(2,1)S(1)} %broadcast_in_dim.13.pick_ref, bf16[512,2048]{1,0:T(8,128)(2,1)S(1)} %bitcast.7, bf16[512,2048]{1,0:T(8,128)(2,1)S(1)} %bitcast.9, ...), custom_call_target="tpu_custom_call" | custom-call | flops 5637144576 | bytes 12582912 | tf_op jit(solution)/shard_map/pallas_call | solution.py:261
  52.7 0.0 collective-permute-done.5.refs_0_
  52.7 2.6 %collective-permute-done.6.refs_1_ = bf16[64,2176]{1,0:T(8,128)(2,1)S(1)} collective-permute-done((bf16[64,2176]{1,0:T(8,128)(2,1)S(1)}, bf16[64,2176]{1,0:T(8,128)(2,1)S(1)}, u32[]{:S(2)}, u32[]{:S(2)}) %collective-permute-start.6) | collective-permute-done | bytes 278560 | tf_op jit(solution)/shard_map/ppermute | solution.py:213
  55.3 0.0 collective-permute-done.7.refs_2_
  55.3 0.0 collective-permute-done.8.refs_3_
  55.3 0.1 shard_map.79.mine
  55.4 0.1 collective-permute-start.14
  55.5 2.7 %collective-permute-done.14.theirs = bf16[256,2176]{1,0:T(8,128)(2,1)S(1)} collective-permute-done((bf16[256,2176]{1,0:T(8,128)(2,1)S(1)}, bf16[256,2176]{1,0:T(8,128)(2,1)S(1)}, u32[]{:S(2)}, u32[]{:S(2)}) %collective-permute-start.14) | collective-permute-done | bytes 1114144 | tf_op jit(solution)/shard_map/ppermute | solution.py:213
  58.2 4.5 %shard_map.80 = f32[512,2048]{1,0:T(8,128)} custom-call(bf16[256,2176]{1,0:T(8,128)(2,1)S(1)} %shard_map.79.mine, bf16[256,2176]{1,0:T(8,128)(2,1)S(1)} %collective-permute-done.14.theirs, bf16[16,128]{1,0:T(8,128)(2,1)S(1)} %broadcast_in_dim.13.pick_ref, bf16[512,2048]{1,0:T(8,128)(2,1)S(1)} %bitcast.8, bf16[512,2048]{1,0:T(8,128)(2,1)S(1)} %bitcast.10, ...), custom_call_target="tpu_custom_call" | custom-call | flops 1879048192 | bytes 12582912 | tf_op jit(solution)/shard_map/pallas_call | solution.py:261
  (3 shorter events, 0.0 us)
Async XLA Ops:
  1.7 11.4 %collective-permute-start.2 = (bf16[64,2176]{1,0:T(8,128)(2,1)}, bf16[64,2176]{1,0:T(8,128)(2,1)S(1)}, u32[]{:S(2)}, u32[]{:S(2)}) collective-permute-start(bf16[64,2176]{1,0:T(8,128)(2,1)} %shard_map.73.refs_0_), channel_id=1, source_target_pairs={{0,18},{1,19},{2,16},{3,17},{4,22},{5,23},{6,20},{7,21},{8,26},{9,... | collective-permute-start | bytes 835592 | tf_op jit(solution)/shard_map/ppermute | solution.py:213
  5.7 11.6 %collective-permute-start.1 = (bf16[64,2176]{1,0:T(8,128)(2,1)}, bf16[64,2176]{1,0:T(8,128)(2,1)S(1)}, u32[]{:S(2)}, u32[]{:S(2)}) collective-permute-start(bf16[64,2176]{1,0:T(8,128)(2,1)} %shard_map.73.refs_0_), channel_id=1, source_target_pairs={{0,12},{1,13},{2,14},{3,15},{4,8},{5,9},{6,10},{7,11},{8,4},{9,5},... | collective-permute-start | bytes 835592 | tf_op jit(solution)/shard_map/ppermute | solution.py:213
  9.3 12.7 %collective-permute-start = (bf16[64,2176]{1,0:T(8,128)(2,1)}, bf16[64,2176]{1,0:T(8,128)(2,1)S(1)}, u32[]{:S(2)}, u32[]{:S(2)}) collective-permute-start(bf16[64,2176]{1,0:T(8,128)(2,1)} %shard_map.73.refs_0_), channel_id=1, source_target_pairs={{0,4},{1,5},{2,6},{3,7},{4,0},{5,1},{6,2},{7,3},{8,12},{9,13},{10,... | collective-permute-start | bytes 835592 | tf_op jit(solution)/shard_map/ppermute | solution.py:213
  9.3 16.5 %collective-permute-start.10 = (bf16[64,2176]{1,0:T(8,128)(2,1)}, bf16[64,2176]{1,0:T(8,128)(2,1)S(1)}, u32[]{:S(2)}, u32[]{:S(2)}) collective-permute-start(bf16[64,2176]{1,0:T(8,128)(2,1)} %shard_map.73.refs_0_), channel_id=1, source_target_pairs={{0,16},{1,17},{2,18},{3,19},{4,20},{5,21},{6,22},{7,23},{8,24},{9,... | collective-permute-start | bytes 835592 | tf_op jit(solution)/shard_map/ppermute | solution.py:213
  9.8 16.0 %collective-permute-start.9 = (bf16[64,2176]{1,0:T(8,128)(2,1)}, bf16[64,2176]{1,0:T(8,128)(2,1)S(1)}, u32[]{:S(2)}, u32[]{:S(2)}) collective-permute-start(bf16[64,2176]{1,0:T(8,128)(2,1)} %shard_map.73.refs_0_), channel_id=1, source_target_pairs={{0,2},{1,3},{2,0},{3,1},{4,6},{5,7},{6,4},{7,5},{8,10},{9,11},{10,... | collective-permute-start | bytes 835592 | tf_op jit(solution)/shard_map/ppermute | solution.py:213
  22.1 5.7 %collective-permute-start.3 = (bf16[128,2176]{1,0:T(8,128)(2,1)S(1)}, bf16[128,2176]{1,0:T(8,128)(2,1)S(1)}, u32[]{:S(2)}, u32[]{:S(2)}) collective-permute-start(bf16[128,2176]{1,0:T(8,128)(2,1)S(1)} %get-tuple-element.22), channel_id=1, source_target_pairs={{4,8},{5,9},{6,10},{7,11},{8,4},{9,5},{10,6},{11,7},{20,24},{21,25... | collective-permute-start | bytes 1671176 | tf_op jit(solution)/shard_map/ppermute | solution.py:213
  22.8 14.6 %collective-permute-start.4 = (bf16[128,2176]{1,0:T(8,128)(2,1)S(1)}, bf16[128,2176]{1,0:T(8,128)(2,1)S(1)}, u32[]{:S(2)}, u32[]{:S(2)}) collective-permute-start(bf16[128,2176]{1,0:T(8,128)(2,1)S(1)} %get-tuple-element.26), channel_id=1, source_target_pairs={{0,4},{1,5},{2,6},{3,7},{4,0},{5,1},{6,2},{7,3},{8,12},{9,13},{10,... | collective-permute-start | bytes 1671176 | tf_op jit(solution)/shard_map/ppermute | solution.py:213
  25.8 12.9 %collective-permute-start.12 = (bf16[128,2176]{1,0:T(8,128)(2,1)S(1)}, bf16[128,2176]{1,0:T(8,128)(2,1)S(1)}, u32[]{:S(2)}, u32[]{:S(2)}) collective-permute-start(bf16[128,2176]{1,0:T(8,128)(2,1)S(1)} %get-tuple-element.32.refs_4_), channel_id=1, source_target_pairs={{0,16},{1,17},{2,18},{3,19},{4,20},{5,21},{6,22},{7,23},{8,24},{9,... | collective-permute-start | bytes 1671176 | tf_op jit(solution)/shard_map/ppermute | solution.py:213
  26.3 12.7 %collective-permute-start.11 = (bf16[128,2176]{1,0:T(8,128)(2,1)S(1)}, bf16[128,2176]{1,0:T(8,128)(2,1)S(1)}, u32[]{:S(2)}, u32[]{:S(2)}) collective-permute-start(bf16[128,2176]{1,0:T(8,128)(2,1)S(1)} %get-tuple-element.32.refs_4_), channel_id=1, source_target_pairs={{0,2},{1,3},{2,0},{3,1},{4,6},{5,7},{6,4},{7,5},{8,10},{9,11},{10,... | collective-permute-start | bytes 1671176 | tf_op jit(solution)/shard_map/ppermute | solution.py:213
  26.8 1.0 %copy-start.2 = (bf16[64,2176]{1,0:T(8,128)(2,1)S(1)}, bf16[64,2176]{1,0:T(8,128)(2,1)}, u32[]{:S(2)}) copy-start(bf16[64,2176]{1,0:T(8,128)(2,1)} %shard_map.73.refs_0_) | copy-start | bytes 835588
  38.9 6.3 %copy-start = (bf16[1,2,256,2048]{3,2,1,0:T(8,128)(2,1)S(1)}, bf16[1,2,256,2048]{3,2,1,0:T(8,128)(2,1)}, u32[]{:S(2)}) copy-start(bf16[1,2,256,2048]{3,2,1,0:T(8,128)(2,1)} %param.11) | copy-start | bytes 6291460
  38.9 6.3 %copy-start.1 = (bf16[1,2,256,2048]{3,2,1,0:T(8,128)(2,1)S(1)}, bf16[1,2,256,2048]{3,2,1,0:T(8,128)(2,1)}, u32[]{:S(2)}) copy-start(bf16[1,2,256,2048]{3,2,1,0:T(8,128)(2,1)} %param.13) | copy-start | bytes 6291460
  38.9 6.3 %copy-start.3 = (bf16[1,256,2048]{2,1,0:T(8,128)(2,1)S(1)}, bf16[1,256,2048]{2,1,0:T(8,128)(2,1)}, u32[]{:S(2)}) copy-start(bf16[1,256,2048]{2,1,0:T(8,128)(2,1)} %param.12) | copy-start | bytes 3145732
  39.2 6.0 %collective-permute-start.13 = (bf16[768,2176]{1,0:T(8,128)(2,1)S(1)}, bf16[768,2176]{1,0:T(8,128)(2,1)S(1)}, u32[]{:S(2)}, u32[]{:S(2)}) collective-permute-start(bf16[768,2176]{1,0:T(8,128)(2,1)S(1)} %shard_map.77.mine), channel_id=1, source_target_pairs={{0,1},{1,0},{2,3},{3,2},{4,5},{5,4},{6,7},{7,6},{8,9},{9,8},{10,11... | collective-permute-start | bytes 10027016 | tf_op jit(solution)/shard_map/ppermute | solution.py:213
  39.3 13.4 %collective-permute-start.5 = (bf16[64,2176]{1,0:T(8,128)(2,1)S(1)}, bf16[64,2176]{1,0:T(8,128)(2,1)S(1)}, u32[]{:S(2)}, u32[]{:S(2)}) collective-permute-start(bf16[64,2176]{1,0:T(8,128)(2,1)S(1)} %get-tuple-element.27), channel_id=1, source_target_pairs={{0,18},{1,19},{2,16},{3,17},{4,22},{5,23},{6,20},{7,21},{8,26},{9,... | collective-permute-start | bytes 835592 | tf_op jit(solution)/shard_map/ppermute | solution.py:213
  40.8 14.5 %collective-permute-start.6 = (bf16[64,2176]{1,0:T(8,128)(2,1)S(1)}, bf16[64,2176]{1,0:T(8,128)(2,1)S(1)}, u32[]{:S(2)}, u32[]{:S(2)}) collective-permute-start(bf16[64,2176]{1,0:T(8,128)(2,1)S(1)} %get-tuple-element.28), channel_id=1, source_target_pairs={{0,2},{1,3},{2,0},{3,1},{4,6},{5,7},{6,4},{7,5},{8,10},{9,11},{10,... | collective-permute-start | bytes 835592 | tf_op jit(solution)/shard_map/ppermute | solution.py:213
  42.3 13.0 %collective-permute-start.7 = (bf16[64,2176]{1,0:T(8,128)(2,1)S(1)}, bf16[64,2176]{1,0:T(8,128)(2,1)S(1)}, u32[]{:S(2)}, u32[]{:S(2)}) collective-permute-start(bf16[64,2176]{1,0:T(8,128)(2,1)S(1)} %get-tuple-element.29), channel_id=1, source_target_pairs={{0,16},{1,17},{2,18},{3,19},{4,20},{5,21},{6,22},{7,23},{8,24},{9,... | collective-permute-start | bytes 835592 | tf_op jit(solution)/shard_map/ppermute | solution.py:213
  42.8 12.5 %collective-permute-start.8 = (bf16[64,2176]{1,0:T(8,128)(2,1)S(1)}, bf16[64,2176]{1,0:T(8,128)(2,1)S(1)}, u32[]{:S(2)}, u32[]{:S(2)}) collective-permute-start(bf16[64,2176]{1,0:T(8,128)(2,1)S(1)} %get-tuple-element.30), channel_id=1, source_target_pairs={{4,0},{5,1},{6,2},{7,3},{8,12},{9,13},{10,14},{11,15},{20,16},{21,... | collective-permute-start | bytes 835592 | tf_op jit(solution)/shard_map/ppermute | solution.py:213
  55.4 2.8 %collective-permute-start.14 = (bf16[256,2176]{1,0:T(8,128)(2,1)S(1)}, bf16[256,2176]{1,0:T(8,128)(2,1)S(1)}, u32[]{:S(2)}, u32[]{:S(2)}) collective-permute-start(bf16[256,2176]{1,0:T(8,128)(2,1)S(1)} %shard_map.79.mine), channel_id=1, source_target_pairs={{0,1},{1,0},{2,3},{3,2},{4,5},{5,4},{6,7},{7,6},{8,9},{9,8},{10,11... | collective-permute-start | bytes 3342344 | tf_op jit(solution)/shard_map/ppermute | solution.py:213

commit v7 on v3

--- a/solution.py
+++ b/solution.py
@@ -152,7 +152,7 @@
         c_ref[at, :] = piece[first + tok_dev : first + 2 * tok_dev, 0:model_dim]
 
 
-COLUMNS = 512
+COLUMNS = 256
 ROWS = 256
 
 

time: 62.4 us -> 62.3 us (level)
  no operation moved by 1% of the time
where the time goes in v7:
time: 62.3 us; the launch traced here: 62.1 us
  waiting for transfers between devices  26.6 us (43%)
  starting transfers between devices  20.3 us (33%)
  Pallas kernels  14.1 us (23%)
  local copies, waits for them, and re-layouts  0.97 us (2%)
    ppermute x15, waiting for transfers between devices, swap(): return lax.ppermute(value, axes, pairs)  26.6 us
    ppermute x15, starting transfers between devices, swap(): return lax.ppermute(value, axes, pairs)  20.3 us
    pallas_call x2, Pallas kernels, call(): pl.pallas_call(functools.partial(kernel, tok_dev=tok_dev), in_specs=[insi...  11.9 us
    pallas_call x1, Pallas kernels, dense(): pl.pallas_call(functools.partial(pack_kernel, experts=experts), in_specs=...  1.74 us
  transfers between devices with their start and end apart: 15, of which 9 were waited for; matrix products, arithmetic and copies ran while one was open for 0% of the time, Pallas kernels for 12%

profile of v7, /device:TPU:0, one launch (start us, length us, event | category | flops | bytes accessed | tf_op | source)
XLA Modules:
  0.0 62.1 jit_solution(8453421149451679435)
XLA Ops:
  0.0 1.7 %shard_map.73.refs_0_ = bf16[64,2176]{1,0:T(8,128)(2,1)} custom-call(bf16[32,2048]{1,0:T(8,128)(2,1)} %tok_hbm.1, bf16[32,2048]{1,0:T(8,128)(2,1)} %cot_hbm.1, s32[8,32]{1,0:T(8,128)} %bitcast.13, f32[8,32]{1,0:T(8,128)} %bitcast.14), custom_call_target="tpu_custom_call" | custom-call | tf_op jit(solution)/shard_map/pallas_call | solution.py:234
  1.7 5.1 %collective-permute-start.1 = (bf16[64,2176]{1,0:T(8,128)(2,1)}, bf16[64,2176]{1,0:T(8,128)(2,1)S(1)}, u32[]{:S(2)}, u32[]{:S(2)}) collective-permute-start(bf16[64,2176]{1,0:T(8,128)(2,1)} %shard_map.73.refs_0_), channel_id=1, source_target_pairs={{0,12},{1,13},{2,14},{3,15},{4,8},{5,9},{6,10},{7,11},{8,4},{9,5},... | collective-permute-start | bytes 835592 | tf_op jit(solution)/shard_map/ppermute | solution.py:213
  6.9 2.4 %collective-permute-start.2 = (bf16[64,2176]{1,0:T(8,128)(2,1)}, bf16[64,2176]{1,0:T(8,128)(2,1)S(1)}, u32[]{:S(2)}, u32[]{:S(2)}) collective-permute-start(bf16[64,2176]{1,0:T(8,128)(2,1)} %shard_map.73.refs_0_), channel_id=1, source_target_pairs={{0,18},{1,19},{2,16},{3,17},{4,22},{5,23},{6,20},{7,21},{8,26},{9,... | collective-permute-start | bytes 835592 | tf_op jit(solution)/shard_map/ppermute | solution.py:213
  9.3 0.0 collective-permute-start
  9.3 0.5 collective-permute-start.10
  9.8 0.5 collective-permute-start.9
  10.4 4.2 %collective-permute-done.1.refs_1_.refs_2_ = bf16[64,2176]{1,0:T(8,128)(2,1)S(1)} collective-permute-done((bf16[64,2176]{1,0:T(8,128)(2,1)}, bf16[64,2176]{1,0:T(8,128)(2,1)S(1)}, u32[]{:S(2)}, u32[]{:S(2)}) %collective-permute-start.1) | collective-permute-done | bytes 278560 | tf_op jit(solution)/shard_map/ppermute | solution.py:213
  14.6 3.0 %collective-permute-done.2.refs_2_.refs_3_ = bf16[64,2176]{1,0:T(8,128)(2,1)S(1)} collective-permute-done((bf16[64,2176]{1,0:T(8,128)(2,1)}, bf16[64,2176]{1,0:T(8,128)(2,1)S(1)}, u32[]{:S(2)}, u32[]{:S(2)}) %collective-permute-start.2) | collective-permute-done | bytes 278560 | tf_op jit(solution)/shard_map/ppermute | solution.py:213
  17.6 2.2 %collective-permute-done.refs_0_ = bf16[64,2176]{1,0:T(8,128)(2,1)S(1)} collective-permute-done((bf16[64,2176]{1,0:T(8,128)(2,1)}, bf16[64,2176]{1,0:T(8,128)(2,1)S(1)}, u32[]{:S(2)}, u32[]{:S(2)}) %collective-permute-start) | collective-permute-done | bytes 278560 | tf_op jit(solution)/shard_map/ppermute | solution.py:213
  19.8 0.1 shard_map.74
  19.9 0.7 %collective-permute-start.3 = (bf16[128,2176]{1,0:T(8,128)(2,1)S(1)}, bf16[128,2176]{1,0:T(8,128)(2,1)S(1)}, u32[]{:S(2)}, u32[]{:S(2)}) collective-permute-start(bf16[128,2176]{1,0:T(8,128)(2,1)S(1)} %get-tuple-element.20), channel_id=1, source_target_pairs={{4,8},{5,9},{6,10},{7,11},{8,4},{9,5},{10,6},{11,7},{20,24},{21,25... | collective-permute-start | bytes 1671176 | tf_op jit(solution)/shard_map/ppermute | solution.py:213
  20.6 3.6 %collective-permute-start.4 = (bf16[128,2176]{1,0:T(8,128)(2,1)S(1)}, bf16[128,2176]{1,0:T(8,128)(2,1)S(1)}, u32[]{:S(2)}, u32[]{:S(2)}) collective-permute-start(bf16[128,2176]{1,0:T(8,128)(2,1)S(1)} %get-tuple-element.24), channel_id=1, source_target_pairs={{0,4},{1,5},{2,6},{3,7},{4,0},{5,1},{6,2},{7,3},{8,12},{9,13},{10,... | collective-permute-start | bytes 1671176 | tf_op jit(solution)/shard_map/ppermute | solution.py:213
  24.2 0.0 collective-permute-done.10.refs_2_
  24.2 0.0 collective-permute-done.9.refs_1_
  24.2 0.9 %collective-permute-start.12 = (bf16[128,2176]{1,0:T(8,128)(2,1)S(1)}, bf16[128,2176]{1,0:T(8,128)(2,1)S(1)}, u32[]{:S(2)}, u32[]{:S(2)}) collective-permute-start(bf16[128,2176]{1,0:T(8,128)(2,1)S(1)} %get-tuple-element.29.refs_4_), channel_id=1, source_target_pairs={{0,16},{1,17},{2,18},{3,19},{4,20},{5,21},{6,22},{7,23},{8,24},{9,... | collective-permute-start | bytes 1671176 | tf_op jit(solution)/shard_map/ppermute | solution.py:213
  25.1 1.5 %collective-permute-start.11 = (bf16[128,2176]{1,0:T(8,128)(2,1)S(1)}, bf16[128,2176]{1,0:T(8,128)(2,1)S(1)}, u32[]{:S(2)}, u32[]{:S(2)}) collective-permute-start(bf16[128,2176]{1,0:T(8,128)(2,1)S(1)} %get-tuple-element.29.refs_4_), channel_id=1, source_target_pairs={{0,2},{1,3},{2,0},{3,1},{4,6},{5,7},{6,4},{7,5},{8,10},{9,11},{10,... | collective-permute-start | bytes 1671176 | tf_op jit(solution)/shard_map/ppermute | solution.py:213
  26.6 0.0 copy-start.2
  26.6 1.0 %copy-done.2 = bf16[64,2176]{1,0:T(8,128)(2,1)S(1)} copy-done((bf16[64,2176]{1,0:T(8,128)(2,1)S(1)}, bf16[64,2176]{1,0:T(8,128)(2,1)}, u32[]{:S(2)}) %copy-start.2) | copy-done | bytes 278552
  27.6 0.0 collective-permute-done.3.refs_0_.refs_4_
  27.6 9.1 %collective-permute-done.4.refs_1_.refs_8_ = bf16[128,2176]{1,0:T(8,128)(2,1)S(1)} collective-permute-done((bf16[128,2176]{1,0:T(8,128)(2,1)S(1)}, bf16[128,2176]{1,0:T(8,128)(2,1)S(1)}, u32[]{:S(2)}, u32[]{:S(2)}) %collective-permute-start.4) | collective-permute-done | bytes 557088 | tf_op jit(solution)/shard_map/ppermute | solution.py:213
  36.7 0.1 shard_map.76
  36.8 1.4 %collective-permute-done.12.refs_6_ = bf16[128,2176]{1,0:T(8,128)(2,1)S(1)} collective-permute-done((bf16[128,2176]{1,0:T(8,128)(2,1)S(1)}, bf16[128,2176]{1,0:T(8,128)(2,1)S(1)}, u32[]{:S(2)}, u32[]{:S(2)}) %collective-permute-start.12) | collective-permute-done | bytes 557088 | tf_op jit(solution)/shard_map/ppermute | solution.py:213
  38.2 0.1 collective-permute-done.11.refs_5_
  38.3 0.0 copy-start
  38.3 0.0 copy-start.1
  38.3 0.0 copy-start.3
  38.3 0.2 shard_map.77.mine
  38.5 0.1 collective-permute-start.13
  38.6 1.4 %collective-permute-start.6 = (bf16[64,2176]{1,0:T(8,128)(2,1)S(1)}, bf16[64,2176]{1,0:T(8,128)(2,1)S(1)}, u32[]{:S(2)}, u32[]{:S(2)}) collective-permute-start(bf16[64,2176]{1,0:T(8,128)(2,1)S(1)} %get-tuple-element.26.refs_7_), channel_id=1, source_target_pairs={{0,2},{1,3},{2,0},{3,1},{4,6},{5,7},{6,4},{7,5},{8,10},{9,11},{10,... | collective-permute-start | bytes 835592 | tf_op jit(solution)/shard_map/ppermute | solution.py:213
  40.0 0.6 %collective-permute-start.7 = (bf16[64,2176]{1,0:T(8,128)(2,1)S(1)}, bf16[64,2176]{1,0:T(8,128)(2,1)S(1)}, u32[]{:S(2)}, u32[]{:S(2)}) collective-permute-start(bf16[64,2176]{1,0:T(8,128)(2,1)S(1)} %get-tuple-element.26.refs_7_), channel_id=1, source_target_pairs={{0,16},{1,17},{2,18},{3,19},{4,20},{5,21},{6,22},{7,23},{8,24},{9,... | collective-permute-start | bytes 835592 | tf_op jit(solution)/shard_map/ppermute | solution.py:213
  40.6 1.5 %collective-permute-start.5 = (bf16[64,2176]{1,0:T(8,128)(2,1)S(1)}, bf16[64,2176]{1,0:T(8,128)(2,1)S(1)}, u32[]{:S(2)}, u32[]{:S(2)}) collective-permute-start(bf16[64,2176]{1,0:T(8,128)(2,1)S(1)} %get-tuple-element.25), channel_id=1, source_target_pairs={{0,18},{1,19},{2,16},{3,17},{4,22},{5,23},{6,20},{7,21},{8,26},{9,... | collective-permute-start | bytes 835592 | tf_op jit(solution)/shard_map/ppermute | solution.py:213
  42.1 1.3 %collective-permute-start.8 = (bf16[64,2176]{1,0:T(8,128)(2,1)S(1)}, bf16[64,2176]{1,0:T(8,128)(2,1)S(1)}, u32[]{:S(2)}, u32[]{:S(2)}) collective-permute-start(bf16[64,2176]{1,0:T(8,128)(2,1)S(1)} %get-tuple-element.27), channel_id=1, source_target_pairs={{4,0},{5,1},{6,2},{7,3},{8,12},{9,13},{10,14},{11,15},{20,16},{21,... | collective-permute-start | bytes 835592 | tf_op jit(solution)/shard_map/ppermute | solution.py:213
  43.4 1.1 %collective-permute-done.13.theirs = bf16[768,2176]{1,0:T(8,128)(2,1)S(1)} collective-permute-done((bf16[768,2176]{1,0:T(8,128)(2,1)S(1)}, bf16[768,2176]{1,0:T(8,128)(2,1)S(1)}, u32[]{:S(2)}, u32[]{:S(2)}) %collective-permute-start.13) | collective-permute-done | bytes 3342368 | tf_op jit(solution)/shard_map/ppermute | solution.py:213
  44.5 0.0 copy-done
  44.5 0.0 copy-done.1
  44.5 0.0 copy-done.3
  44.5 7.5 %shard_map.78.add_ref = f32[512,2048]{1,0:T(8,128)S(1)} custom-call(bf16[768,2176]{1,0:T(8,128)(2,1)S(1)} %shard_map.77.mine, bf16[768,2176]{1,0:T(8,128)(2,1)S(1)} %collective-permute-done.13.theirs, bf16[16,128]{1,0:T(8,128)(2,1)S(1)} %broadcast_in_dim.13.pick_ref, bf16[512,2048]{1,0:T(8,128)(2,1)S(1)} %bitcast.7, bf16[512,2048]{1,0:T(8,128)(2,1)S(1)} %bitcast.9, ...), custom_call_target="tpu_custom_call" | custom-call | flops 5637144576 | bytes 12582912 | tf_op jit(solution)/shard_map/pallas_call | solution.py:261
  52.0 2.7 %collective-permute-done.5.refs_0_ = bf16[64,2176]{1,0:T(8,128)(2,1)S(1)} collective-permute-done((bf16[64,2176]{1,0:T(8,128)(2,1)S(1)}, bf16[64,2176]{1,0:T(8,128)(2,1)S(1)}, u32[]{:S(2)}, u32[]{:S(2)}) %collective-permute-start.5) | collective-permute-done | bytes 278560 | tf_op jit(solution)/shard_map/ppermute | solution.py:213
  54.7 0.0 collective-permute-done.6.refs_1_
  54.7 0.0 collective-permute-done.7.refs_2_
  54.7 0.0 collective-permute-done.8.refs_3_
  54.7 0.1 shard_map.79.mine
  54.8 0.1 collective-permute-start.14
  54.9 2.7 %collective-permute-done.14.theirs = bf16[256,2176]{1,0:T(8,128)(2,1)S(1)} collective-permute-done((bf16[256,2176]{1,0:T(8,128)(2,1)S(1)}, bf16[256,2176]{1,0:T(8,128)(2,1)S(1)}, u32[]{:S(2)}, u32[]{:S(2)}) %collective-permute-start.14) | collective-permute-done | bytes 1114144 | tf_op jit(solution)/shard_map/ppermute | solution.py:213
  57.7 4.4 %shard_map.80 = f32[512,2048]{1,0:T(8,128)} custom-call(bf16[256,2176]{1,0:T(8,128)(2,1)S(1)} %shard_map.79.mine, bf16[256,2176]{1,0:T(8,128)(2,1)S(1)} %collective-permute-done.14.theirs, bf16[16,128]{1,0:T(8,128)(2,1)S(1)} %broadcast_in_dim.13.pick_ref, bf16[512,2048]{1,0:T(8,128)(2,1)S(1)} %bitcast.8, bf16[512,2048]{1,0:T(8,128)(2,1)S(1)} %bitcast.10, ...), custom_call_target="tpu_custom_call" | custom-call | flops 1879048192 | bytes 12582912 | tf_op jit(solution)/shard_map/pallas_call | solution.py:261
  (3 shorter events, 0.0 us)
Async XLA Ops:
  1.7 12.9 %collective-permute-start.1 = (bf16[64,2176]{1,0:T(8,128)(2,1)}, bf16[64,2176]{1,0:T(8,128)(2,1)S(1)}, u32[]{:S(2)}, u32[]{:S(2)}) collective-permute-start(bf16[64,2176]{1,0:T(8,128)(2,1)} %shard_map.73.refs_0_), channel_id=1, source_target_pairs={{0,12},{1,13},{2,14},{3,15},{4,8},{5,9},{6,10},{7,11},{8,4},{9,5},... | collective-permute-start | bytes 835592 | tf_op jit(solution)/shard_map/ppermute | solution.py:213
  6.9 10.7 %collective-permute-start.2 = (bf16[64,2176]{1,0:T(8,128)(2,1)}, bf16[64,2176]{1,0:T(8,128)(2,1)S(1)}, u32[]{:S(2)}, u32[]{:S(2)}) collective-permute-start(bf16[64,2176]{1,0:T(8,128)(2,1)} %shard_map.73.refs_0_), channel_id=1, source_target_pairs={{0,18},{1,19},{2,16},{3,17},{4,22},{5,23},{6,20},{7,21},{8,26},{9,... | collective-permute-start | bytes 835592 | tf_op jit(solution)/shard_map/ppermute | solution.py:213
  9.3 10.5 %collective-permute-start = (bf16[64,2176]{1,0:T(8,128)(2,1)}, bf16[64,2176]{1,0:T(8,128)(2,1)S(1)}, u32[]{:S(2)}, u32[]{:S(2)}) collective-permute-start(bf16[64,2176]{1,0:T(8,128)(2,1)} %shard_map.73.refs_0_), channel_id=1, source_target_pairs={{0,4},{1,5},{2,6},{3,7},{4,0},{5,1},{6,2},{7,3},{8,12},{9,13},{10,... | collective-permute-start | bytes 835592 | tf_op jit(solution)/shard_map/ppermute | solution.py:213
  9.3 14.9 %collective-permute-start.10 = (bf16[64,2176]{1,0:T(8,128)(2,1)}, bf16[64,2176]{1,0:T(8,128)(2,1)S(1)}, u32[]{:S(2)}, u32[]{:S(2)}) collective-permute-start(bf16[64,2176]{1,0:T(8,128)(2,1)} %shard_map.73.refs_0_), channel_id=1, source_target_pairs={{0,16},{1,17},{2,18},{3,19},{4,20},{5,21},{6,22},{7,23},{8,24},{9,... | collective-permute-start | bytes 835592 | tf_op jit(solution)/shard_map/ppermute | solution.py:213
  9.8 14.4 %collective-permute-start.9 = (bf16[64,2176]{1,0:T(8,128)(2,1)}, bf16[64,2176]{1,0:T(8,128)(2,1)S(1)}, u32[]{:S(2)}, u32[]{:S(2)}) collective-permute-start(bf16[64,2176]{1,0:T(8,128)(2,1)} %shard_map.73.refs_0_), channel_id=1, source_target_pairs={{0,2},{1,3},{2,0},{3,1},{4,6},{5,7},{6,4},{7,5},{8,10},{9,11},{10,... | collective-permute-start | bytes 835592 | tf_op jit(solution)/shard_map/ppermute | solution.py:213
  19.9 7.7 %collective-permute-start.3 = (bf16[128,2176]{1,0:T(8,128)(2,1)S(1)}, bf16[128,2176]{1,0:T(8,128)(2,1)S(1)}, u32[]{:S(2)}, u32[]{:S(2)}) collective-permute-start(bf16[128,2176]{1,0:T(8,128)(2,1)S(1)} %get-tuple-element.20), channel_id=1, source_target_pairs={{4,8},{5,9},{6,10},{7,11},{8,4},{9,5},{10,6},{11,7},{20,24},{21,25... | collective-permute-start | bytes 1671176 | tf_op jit(solution)/shard_map/ppermute | solution.py:213
  20.6 16.1 %collective-permute-start.4 = (bf16[128,2176]{1,0:T(8,128)(2,1)S(1)}, bf16[128,2176]{1,0:T(8,128)(2,1)S(1)}, u32[]{:S(2)}, u32[]{:S(2)}) collective-permute-start(bf16[128,2176]{1,0:T(8,128)(2,1)S(1)} %get-tuple-element.24), channel_id=1, source_target_pairs={{0,4},{1,5},{2,6},{3,7},{4,0},{5,1},{6,2},{7,3},{8,12},{9,13},{10,... | collective-permute-start | bytes 1671176 | tf_op jit(solution)/shard_map/ppermute | solution.py:213
  24.2 14.0 %collective-permute-start.12 = (bf16[128,2176]{1,0:T(8,128)(2,1)S(1)}, bf16[128,2176]{1,0:T(8,128)(2,1)S(1)}, u32[]{:S(2)}, u32[]{:S(2)}) collective-permute-start(bf16[128,2176]{1,0:T(8,128)(2,1)S(1)} %get-tuple-element.29.refs_4_), channel_id=1, source_target_pairs={{0,16},{1,17},{2,18},{3,19},{4,20},{5,21},{6,22},{7,23},{8,24},{9,... | collective-permute-start | bytes 1671176 | tf_op jit(solution)/shard_map/ppermute | solution.py:213
  25.1 13.1 %collective-permute-start.11 = (bf16[128,2176]{1,0:T(8,128)(2,1)S(1)}, bf16[128,2176]{1,0:T(8,128)(2,1)S(1)}, u32[]{:S(2)}, u32[]{:S(2)}) collective-permute-start(bf16[128,2176]{1,0:T(8,128)(2,1)S(1)} %get-tuple-element.29.refs_4_), channel_id=1, source_target_pairs={{0,2},{1,3},{2,0},{3,1},{4,6},{5,7},{6,4},{7,5},{8,10},{9,11},{10,... | collective-permute-start | bytes 1671176 | tf_op jit(solution)/shard_map/ppermute | solution.py:213
  26.6 1.0 %copy-start.2 = (bf16[64,2176]{1,0:T(8,128)(2,1)S(1)}, bf16[64,2176]{1,0:T(8,128)(2,1)}, u32[]{:S(2)}) copy-start(bf16[64,2176]{1,0:T(8,128)(2,1)} %shard_map.73.refs_0_) | copy-start | bytes 835588
  38.3 6.3 %copy-start = (bf16[1,2,256,2048]{3,2,1,0:T(8,128)(2,1)S(1)}, bf16[1,2,256,2048]{3,2,1,0:T(8,128)(2,1)}, u32[]{:S(2)}) copy-start(bf16[1,2,256,2048]{3,2,1,0:T(8,128)(2,1)} %param.11) | copy-start | bytes 6291460
  38.3 6.3 %copy-start.1 = (bf16[1,2,256,2048]{3,2,1,0:T(8,128)(2,1)S(1)}, bf16[1,2,256,2048]{3,2,1,0:T(8,128)(2,1)}, u32[]{:S(2)}) copy-start(bf16[1,2,256,2048]{3,2,1,0:T(8,128)(2,1)} %param.13) | copy-start | bytes 6291460
  38.3 6.3 %copy-start.3 = (bf16[1,256,2048]{2,1,0:T(8,128)(2,1)S(1)}, bf16[1,256,2048]{2,1,0:T(8,128)(2,1)}, u32[]{:S(2)}) copy-start(bf16[1,256,2048]{2,1,0:T(8,128)(2,1)} %param.12) | copy-start | bytes 3145732
  38.5 6.0 %collective-permute-start.13 = (bf16[768,2176]{1,0:T(8,128)(2,1)S(1)}, bf16[768,2176]{1,0:T(8,128)(2,1)S(1)}, u32[]{:S(2)}, u32[]{:S(2)}) collective-permute-start(bf16[768,2176]{1,0:T(8,128)(2,1)S(1)} %shard_map.77.mine), channel_id=1, source_target_pairs={{0,1},{1,0},{2,3},{3,2},{4,5},{5,4},{6,7},{7,6},{8,9},{9,8},{10,11... | collective-permute-start | bytes 10027016 | tf_op jit(solution)/shard_map/ppermute | solution.py:213
  38.6 16.1 %collective-permute-start.6 = (bf16[64,2176]{1,0:T(8,128)(2,1)S(1)}, bf16[64,2176]{1,0:T(8,128)(2,1)S(1)}, u32[]{:S(2)}, u32[]{:S(2)}) collective-permute-start(bf16[64,2176]{1,0:T(8,128)(2,1)S(1)} %get-tuple-element.26.refs_7_), channel_id=1, source_target_pairs={{0,2},{1,3},{2,0},{3,1},{4,6},{5,7},{6,4},{7,5},{8,10},{9,11},{10,... | collective-permute-start | bytes 835592 | tf_op jit(solution)/shard_map/ppermute | solution.py:213
  40.0 14.8 %collective-permute-start.7 = (bf16[64,2176]{1,0:T(8,128)(2,1)S(1)}, bf16[64,2176]{1,0:T(8,128)(2,1)S(1)}, u32[]{:S(2)}, u32[]{:S(2)}) collective-permute-start(bf16[64,2176]{1,0:T(8,128)(2,1)S(1)} %get-tuple-element.26.refs_7_), channel_id=1, source_target_pairs={{0,16},{1,17},{2,18},{3,19},{4,20},{5,21},{6,22},{7,23},{8,24},{9,... | collective-permute-start | bytes 835592 | tf_op jit(solution)/shard_map/ppermute | solution.py:213
  40.6 14.1 %collective-permute-start.5 = (bf16[64,2176]{1,0:T(8,128)(2,1)S(1)}, bf16[64,2176]{1,0:T(8,128)(2,1)S(1)}, u32[]{:S(2)}, u32[]{:S(2)}) collective-permute-start(bf16[64,2176]{1,0:T(8,128)(2,1)S(1)} %get-tuple-element.25), channel_id=1, source_target_pairs={{0,18},{1,19},{2,16},{3,17},{4,22},{5,23},{6,20},{7,21},{8,26},{9,... | collective-permute-start | bytes 835592 | tf_op jit(solution)/shard_map/ppermute | solution.py:213
  42.1 12.6 %collective-permute-start.8 = (bf16[64,2176]{1,0:T(8,128)(2,1)S(1)}, bf16[64,2176]{1,0:T(8,128)(2,1)S(1)}, u32[]{:S(2)}, u32[]{:S(2)}) collective-permute-start(bf16[64,2176]{1,0:T(8,128)(2,1)S(1)} %get-tuple-element.27), channel_id=1, source_target_pairs={{4,0},{5,1},{6,2},{7,3},{8,12},{9,13},{10,14},{11,15},{20,16},{21,... | collective-permute-start | bytes 835592 | tf_op jit(solution)/shard_map/ppermute | solution.py:213
  54.8 2.8 %collective-permute-start.14 = (bf16[256,2176]{1,0:T(8,128)(2,1)S(1)}, bf16[256,2176]{1,0:T(8,128)(2,1)S(1)}, u32[]{:S(2)}, u32[]{:S(2)}) collective-permute-start(bf16[256,2176]{1,0:T(8,128)(2,1)S(1)} %shard_map.79.mine), channel_id=1, source_target_pairs={{0,1},{1,0},{2,3},{3,2},{4,5},{5,4},{6,7},{7,6},{8,9},{9,8},{10,11... | collective-permute-start | bytes 3342344 | tf_op jit(solution)/shard_map/ppermute | solution.py:213
